TPU v7x, 256 devices: a whole 4x4x8 slice. The times are simulated.
256 devices in a mesh: row: 64 (over z, x_hi, y), head: 4 (over x_lo, core).
Axes of the slice: x: 4 (x_hi: 2, x_lo: 2; x = x_hi * 2 + x_lo), y: 4, z: 8, core: 2. Of those that a mesh axis runs over, the one named last changes fastest.
Arguments:
- samples: bfloat16 [128, 512, 2048], P('row', None, 'head'), may hold values from -12 to 12
- norm_gain: float32 [2048], replicated, may hold values from 0.25 to 1.75
- row_qkv: bfloat16 [3, 2048, 1024], P(None, None, 'head'), may hold values from -0.09082975 to 0.09082975
- col_qkv: bfloat16 [3, 2048, 1024], P(None, None, 'head'), may hold values from -0.09082975 to 0.09082975
- row_out: bfloat16 [1024, 2048], P('head'), may hold values from -0.1875 to 0.1875
- col_out: bfloat16 [1024, 2048], P('head'), may hold values from -0.1875 to 0.1875
Outputs:
- layer_out: bfloat16 [128, 512, 2048], P('row', None, 'head')
All inputs are finite; a program needn't handle non-finite values.
Results may differ from a plain program's by a relative error of at most 0.012.
Values may be sent and summed in bfloat16 or wider, within the bound.
No kernel may reach another device: no remote copies, remote signals or barrier semaphores. Data moves between devices by JAX's collectives and lax.ppermute only.
A program may use at most 64 MiB of HBM per device.

v0:
```python
import jax
import jax.numpy as jnp
from jax import lax
from jax.sharding import PartitionSpec as P

HD = 128


def layer_norm(values, norm_gain):
    values = values.astype(jnp.float32)
    mean = jnp.mean(values, axis=-1, keepdims=True)
    centred = values - mean
    var = jnp.mean(centred * centred, axis=-1, keepdims=True)
    return (centred * lax.rsqrt(var + 1e-05) * norm_gain).astype(jnp.bfloat16)


def softmax_rounded(scores, allowed):
    scores = jnp.where(allowed, scores, -jnp.inf)
    top = jnp.max(scores, axis=-1, keepdims=True)
    expo = jnp.exp(scores - top)
    return (expo / jnp.sum(expo, axis=-1, keepdims=True)).astype(jnp.bfloat16)


def column_attend(parts):
    query, keys, vals = parts
    full_rows = query.shape[0]
    scores = jnp.einsum("qche,kche->chqk", query, keys, preferred_element_type=jnp.float32) * (
        1.0 / HD**0.5
    )
    allowed = jnp.arange(full_rows)[:, None] >= jnp.arange(full_rows)[None, :]
    weights = softmax_rounded(scores, allowed[None, None])
    return jnp.einsum("chqk,kche->qche", weights, vals, preferred_element_type=jnp.float32).astype(
        jnp.bfloat16
    )


def shards(samples, norm_gain, row_qkv, col_qkv, row_out, col_out):
    rows_local, cols, feat_local = samples.shape
    tokens_local = rows_local * cols
    whole = lax.all_gather(samples, "head", axis=2, tiled=True)
    normed = layer_norm(whole, norm_gain).reshape(tokens_local, -1)

    def project(weights):
        mixed = jnp.einsum("nd,tde->tne", normed, weights, preferred_element_type=jnp.float32)
        return mixed.astype(jnp.bfloat16).reshape(3, rows_local, cols, -1, HD)

    stacked = project(row_qkv)
    scores = jnp.einsum(
        "rqhe,rkhe->rhqk", stacked[0], stacked[1], preferred_element_type=jnp.float32
    ) * (1.0 / HD**0.5)
    allowed = jnp.arange(cols)[:, None] >= jnp.arange(cols)[None, :]
    weights = softmax_rounded(scores, allowed[None, None])
    attended = jnp.einsum(
        "rhqk,rkhe->rqhe", weights, stacked[2], preferred_element_type=jnp.float32
    )
    row_attn = attended.astype(jnp.bfloat16).reshape(tokens_local, -1)
    stacked = project(col_qkv)
    moved = column_attend(
        (
            lax.all_to_all(stacked[0], "row", split_axis=1, concat_axis=0, tiled=True),
            lax.all_to_all(stacked[1], "row", split_axis=1, concat_axis=0, tiled=True),
            lax.all_to_all(stacked[2], "row", split_axis=1, concat_axis=0, tiled=True),
        )
    )
    returned = lax.all_to_all(moved, "row", split_axis=0, concat_axis=1, tiled=True)
    col_attn = returned.reshape(tokens_local, -1)
    partial_term = jnp.dot(row_attn, row_out, preferred_element_type=jnp.float32)
    partial_term = partial_term + jnp.dot(col_attn, col_out, preferred_element_type=jnp.float32)
    summed = lax.psum_scatter(
        partial_term.astype(jnp.bfloat16), "head", scatter_dimension=1, tiled=True
    ).astype(jnp.float32)
    total = samples.astype(jnp.float32) + summed.reshape(rows_local, cols, feat_local)
    return total.astype(jnp.bfloat16)


def solution(mesh):
    placed = (
        P("row", None, "head"),
        P(),
        P(None, None, "head"),
        P(None, None, "head"),
        P("head", None),
        P("head", None),
    )
    return jax.shard_map(
        shards, mesh=mesh, in_specs=placed, out_specs=P("row", None, "head"), check_vma=False
    )
```

profile of v0, /device:TPU:1, one launch (start us, length us, event | category | flops | bytes accessed | tf_op | source)
XLA Modules:
  0.0 257.0 jit_solution(5796557568246533460)
XLA Ops:
  6.5 0.0 copy-start
  6.5 0.0 all-gather.2.cloned.1.call-start
  6.5 0.7 all-gather.2.cloned.1.call-update
  7.3 0.0 copy-start.4
  7.3 55.2 %all-gather.2.cloned.1.call-done = bf16[2,512,2048]{2,1,0:T(8,128)(2,1)} async-done(((bf16[2,512,512]{2,1,0:T(8,128)(2,1)}), bf16[2,512,2048]{2,1,0:T(8,128)(2,1)}) %all-gather.2.cloned.1.call-update) | async-done | bytes 4194320 | tf_op jit(solution)/shard_map/all_gather | solution.py:40
  62.5 0.0 copy-start.1
  62.5 3.0 %convert_reduce_fusion = f32[2,512]{1,0:T(2,128)S(1)} fusion(bf16[2,512,2048]{2,1,0:T(8,128)(2,1)} %all-gather.2.cloned.1.call-done), kind=kLoop, calls=%fused_computation.3 | loop fusion | flops 4193280 | bytes 4198400 | tf_op jit(solution)/shard_map/reduce_sum | solution.py:11
  65.5 0.5 copy-done.1
  66.0 1.2 fusion.4
  67.2 0.0 copy-done.4
  67.2 1.4 fusion.6
  68.6 0.0 copy-start.2
  68.7 0.0 copy-done
  68.7 3.4 %fusion.14 = bf16[3,1024,256]{2,1,0:T(8,128)(2,1)S(1)} fusion(bf16[1024,2048,1]{1,0,2:T(8,128)(2,1)S(1)} %bitcast.47, bf16[3,2048,256]{2,1,0:T(8,128)(2,1)S(1)} %copy-done), kind=kOutput, calls=%fused_computation.23 | convolution fusion | flops 3222011904 | bytes 8912896 | tf_op jit(solution)/shard_map/nd,tde->tne/dot_general | solution.py:44
  72.1 0.0 copy-done.2
  72.1 1.2 fusion.33
  73.3 2.0 squeeze.23
  75.3 2.2 copy.49
  77.5 12.6 %all-to-all-start.2 = ((bf16[2,512,2,128]{3,2,0,1:T(2,128)(2,1)}), bf16[2,512,2,128]{3,2,0,1:T(2,128)(2,1)}, u32[]{:S(2)}, u32[]{:S(2)}) async-start(bf16[2,512,2,128]{3,2,0,1:T(2,128)(2,1)} %copy.49), calls=%async_computation.2 | async-start | bytes 1048576 | tf_op jit(solution)/shard_map/all_to_all | solution.py:61
  90.1 0.1 iota_compare_fusion
  90.2 2.0 squeeze.22
  92.1 2.2 copy.47
  94.3 2.0 squeeze.21
  96.3 2.3 copy.44
  98.6 8.8 %all-to-all-done.2 = bf16[2,512,2,128]{3,2,0,1:T(2,128)(2,1)} async-done(((bf16[2,512,2,128]{3,2,0,1:T(2,128)(2,1)}), bf16[2,512,2,128]{3,2,0,1:T(2,128)(2,1)}, u32[]{:S(2)}, u32[]{:S(2)}) %all-to-all-start.2) | async-done | bytes 524320 | tf_op jit(solution)/shard_map/all_to_all | solution.py:61
  107.4 7.6 %all-to-all-start.1 = ((bf16[2,512,2,128]{3,2,0,1:T(2,128)(2,1)}), bf16[2,512,2,128]{3,2,0,1:T(2,128)(2,1)}, u32[]{:S(2)}, u32[]{:S(2)}) async-start(bf16[2,512,2,128]{3,2,0,1:T(2,128)(2,1)} %copy.47), calls=%async_computation.1 | async-start | bytes 1048576 | tf_op jit(solution)/shard_map/all_to_all | solution.py:60
  115.0 6.6 %fusion.13 = bf16[3,1024,256]{2,1,0:T(8,128)(2,1)S(1)} fusion(bf16[1024,2048,1]{1,0,2:T(8,128)(2,1)} %bitcast.48, bf16[3,2048,256]{2,1,0:T(8,128)(2,1)} %param.8), kind=kOutput, calls=%fused_computation.22 | convolution fusion | flops 3222011904 | bytes 8912896 | tf_op jit(solution)/shard_map/nd,tde->tne/dot_general | solution.py:44
  121.6 1.2 fusion.34
  122.7 2.0 squeeze.20
  124.7 2.0 squeeze.19
  126.7 3.0 %all-to-all-done.1 = bf16[2,512,2,128]{3,2,0,1:T(2,128)(2,1)} async-done(((bf16[2,512,2,128]{3,2,0,1:T(2,128)(2,1)}), bf16[2,512,2,128]{3,2,0,1:T(2,128)(2,1)}, u32[]{:S(2)}, u32[]{:S(2)}) %all-to-all-start.1) | async-done | bytes 524320 | tf_op jit(solution)/shard_map/all_to_all | solution.py:60
  129.7 9.2 %all-to-all-start = ((bf16[2,512,2,128]{3,2,0,1:T(2,128)(2,1)}), bf16[2,512,2,128]{3,2,0,1:T(2,128)(2,1)}, u32[]{:S(2)}, u32[]{:S(2)}) async-start(bf16[2,512,2,128]{3,2,0,1:T(2,128)(2,1)} %copy.44), calls=%async_computation | async-start | bytes 1048576 | tf_op jit(solution)/shard_map/all_to_all | solution.py:62
  138.8 3.9 %fusion.26 = f32[2,2,512,512]{2,3,1,0:T(8,128)} fusion(bf16[2,512,2,128]{3,2,1,0:T(2,128)(2,1)} %squeeze.20, bf16[2,512,2,128]{3,2,1,0:T(2,128)(2,1)} %squeeze.19), kind=kOutput, calls=%fused_computation.40 | convolution fusion | flops 268435456 | bytes 5242880 | tf_op jit(solution)/shard_map/rqhe,rkhe->rhqk/dot_general | solution.py:48
  142.7 2.0 squeeze.18
  144.7 7.2 %fusion.35 = (f32[2,2,512]{2,1,0:T(2,128)S(1)}, f32[2,2,512,512]{2,3,1,0:T(8,128)}) fusion(f32[2,2,512,512]{2,3,1,0:T(8,128)} %fusion.26, pred[512,512]{0,1:T(8,128)(4,1)S(1)} %iota_compare_fusion), kind=kOutput, calls=%fused_computation.52 | output fusion | flops 6291967 | bytes 8658944 | tf_op jit(solution)/shard_map/sub | solution.py:20
  151.9 1.4 copy.50
  153.3 1.4 copy.48
  154.8 0.5 fusion.17
  155.3 0.0 copy-start.3
  155.3 1.0 copy-done.3
  156.2 0.2 fusion.36
  156.5 0.0 all-to-all-done
  156.5 1.1 copy.72
  157.6 0.9 copy.46
  158.5 3.1 %fusion.20 = bf16[128,8,2,128]{0,3,2,1:T(8,128)(2,1)} fusion(bf16[128,8,2,128]{3,1,2,0:T(8,128)(2,1)} %bitcast.56, f32[8,2,128]{2,1,0:T(2,128)S(1)} %fusion.36, f32[8,2,128,128]{2,3,1,0:T(8,128)} %copy-done.3), kind=kOutput, calls=%fused_computation.31 | convolution fusion | flops 68159616 | bytes 2105344 | tf_op jit(solution)/shard_map/chqk,kche->qche/dot_general | solution.py:32
  161.6 2.1 copy.53
  163.6 12.3 %all-to-all-start.3 = ((bf16[128,8,2,128]{3,2,1,0:T(2,128)(2,1)}), bf16[128,8,2,128]{3,2,1,0:T(2,128)(2,1)}, u32[]{:S(2)}, u32[]{:S(2)}) async-start(bf16[128,8,2,128]{3,2,1,0:T(2,128)(2,1)} %copy.53), calls=%async_computation.3 | async-start | bytes 1048576 | tf_op jit(solution)/shard_map/all_to_all | solution.py:65
  176.0 0.3 reduce-scatter.2.cloned.1.call-start
  176.3 3.7 %fusion.19 = bf16[2,512,2,128]{1,3,2,0:T(8,128)(2,1)} fusion(f32[2,2,512,512]{2,3,1,0:T(8,128)} %get-tuple-element.12, f32[2,2,512]{2,1,0:T(2,128)S(1)} %get-tuple-element.11, bf16[2,512,2,128]{3,2,1,0:T(2,128)(2,1)} %squeeze.18), kind=kOutput, calls=%fused_computation.30 | convolution fusion | flops 270794752 | bytes 5251072 | tf_op jit(solution)/shard_map/rhqk,rkhe->rqhe/dot_general | solution.py:53
  179.9 2.0 copy.43
  182.0 5.9 %fusion.21 = f32[1024,2048]{1,0:T(8,128)} fusion(bf16[256,2048]{1,0:T(8,128)(2,1)} %param.10, bf16[128,8,2,128]{3,2,1,0:T(2,128)(2,1)} %bitcast.49), kind=kOutput, calls=%fused_computation.34 | convolution fusion | flops 1073741824 | bytes 9961472 | tf_op jit(solution)/shard_map/dot_general | solution.py:67
  187.8 2.0 all-to-all-done.3
  189.8 1.1 copy.54
  191.0 7.1 %add_convert_fusion = bf16[1024,2048]{1,0:T(8,128)(2,1)} fusion(f32[1024,2048]{1,0:T(8,128)} %fusion.21, bf16[1024,256]{1,0:T(8,128)(2,1)S(1)} %bitcast.50, bf16[256,2048]{1,0:T(8,128)(2,1)} %param.11), kind=kOutput, calls=%fused_computation.9 | convolution fusion | flops 1077936128 | bytes 14155776 | tf_op jit(solution)/shard_map/dot_general | solution.py:68
  198.1 0.0 reduce-scatter.2.cloned.1.call-update
  198.1 49.3 %reduce-scatter.2.cloned.1.call-done = bf16[1024,512]{1,0:T(8,128)(2,1)} async-done(((bf16[1024,2048]{1,0:T(8,128)(2,1)}), bf16[1024,512]{1,0:T(8,128)(2,1)}) %reduce-scatter.2.cloned.1.call-update) | async-done | bytes 1048592 | tf_op jit(solution)/shard_map/reduce_scatter | solution.py:69
  247.4 2.8 %fusion.8 = bf16[2,512,512]{2,1,0:T(8,128)(2,1)} fusion(bf16[2,512,512]{2,1,0:T(8,128)(2,1)} %bitcast.55, bf16[2,512,512]{2,1,0:T(8,128)(2,1)} %param.6), kind=kLoop, calls=%fused_computation.15 | loop fusion | flops 2097152 | bytes 3145728 | tf_op jit(solution)/shard_map/convert_element_type | solution.py:73
  (4 shorter events, 0.1 us)
Async XLA Ops:
  6.5 62.1 %copy-start = (bf16[3,2048,256]{2,1,0:T(8,128)(2,1)S(1)}, bf16[3,2048,256]{2,1,0:T(8,128)(2,1)}, u32[]{:S(2)}) copy-start(bf16[3,2048,256]{2,1,0:T(8,128)(2,1)} %param.9) | copy-start | bytes 9437188
  6.5 56.0 %all-gather.2.cloned.1.call-start = ((), (), s32[]{:S(2)}) async-start(), calls=%async_computation.5 | async-start | bytes 5242880 | tf_op jit(solution)/shard_map/all_gather | solution.py:40
  7.3 59.9 %copy-start.4 = (f32[2048]{0:T(1024)S(1)}, f32[2048]{0:T(1024)}, u32[]{:S(2)}) copy-start(f32[2048]{0:T(1024)} %param.7) | copy-start | bytes 24580
  62.5 3.4 %copy-start.1 = (bf16[2,512,2048]{2,1,0:T(8,128)(2,1)S(1)}, bf16[2,512,2048]{2,1,0:T(8,128)(2,1)}, u32[]{:S(2)}) copy-start(bf16[2,512,2048]{2,1,0:T(8,128)(2,1)} %all-gather.2.cloned.1.call-done) | copy-start | bytes 12582916
  68.6 3.4 %copy-start.2 = (bf16[2,512,2048]{2,1,0:T(8,128)(2,1)}, bf16[2,512,2048]{2,1,0:T(8,128)(2,1)S(1)}, u32[]{:S(2)}) copy-start(bf16[2,512,2048]{2,1,0:T(8,128)(2,1)S(1)} %fusion.6) | copy-start | bytes 12582916
  77.5 29.9 %all-to-all-start.2 = ((bf16[2,512,2,128]{3,2,0,1:T(2,128)(2,1)}), bf16[2,512,2,128]{3,2,0,1:T(2,128)(2,1)}, u32[]{:S(2)}, u32[]{:S(2)}) async-start(bf16[2,512,2,128]{3,2,0,1:T(2,128)(2,1)} %copy.49), calls=%async_computation.2 | async-start | bytes 1048576 | tf_op jit(solution)/shard_map/all_to_all | solution.py:61
  107.4 22.3 %all-to-all-start.1 = ((bf16[2,512,2,128]{3,2,0,1:T(2,128)(2,1)}), bf16[2,512,2,128]{3,2,0,1:T(2,128)(2,1)}, u32[]{:S(2)}, u32[]{:S(2)}) async-start(bf16[2,512,2,128]{3,2,0,1:T(2,128)(2,1)} %copy.47), calls=%async_computation.1 | async-start | bytes 1048576 | tf_op jit(solution)/shard_map/all_to_all | solution.py:60
  129.7 26.8 %all-to-all-start = ((bf16[2,512,2,128]{3,2,0,1:T(2,128)(2,1)}), bf16[2,512,2,128]{3,2,0,1:T(2,128)(2,1)}, u32[]{:S(2)}, u32[]{:S(2)}) async-start(bf16[2,512,2,128]{3,2,0,1:T(2,128)(2,1)} %copy.44), calls=%async_computation | async-start | bytes 1048576 | tf_op jit(solution)/shard_map/all_to_all | solution.py:62
  155.3 1.0 copy-start.3
  163.6 26.2 %all-to-all-start.3 = ((bf16[128,8,2,128]{3,2,1,0:T(2,128)(2,1)}), bf16[128,8,2,128]{3,2,1,0:T(2,128)(2,1)}, u32[]{:S(2)}, u32[]{:S(2)}) async-start(bf16[128,8,2,128]{3,2,1,0:T(2,128)(2,1)} %copy.53), calls=%async_computation.3 | async-start | bytes 1048576 | tf_op jit(solution)/shard_map/all_to_all | solution.py:65
  176.0 71.4 %reduce-scatter.2.cloned.1.call-start = ((), (), s32[]{:S(2)}) async-start(), calls=%async_computation.6 | async-start | bytes 5242880 | tf_op jit(solution)/shard_map/reduce_scatter | solution.py:69
Sparse Core Ops, SparseCore 0:
  9.2 53.2 all-gather.1
  198.2 49.1 reduce-scatter.1
where the time goes:
time: 258 us; the launch traced here: 257 us
  waiting for transfers between devices  119 us (46%)
  starting transfers between devices  41.9 us (16%)
  matrix products  34.1 us (13%)
  local copies, waits for them, and re-layouts  32.4 us (13%)
  other arithmetic  16 us (6%)
  between operations  13.6 us (5%)
    all_gather x1, waiting for transfers between devices, shards(): whole = lax.all_gather(samples, 'head', axis=2, tiled=True)  55.2 us
    reduce_scatter x1, waiting for transfers between devices, shards(): lax.psum_scatter(partial_term.astype(jnp.bfloat16), 'head', scatter_dimen...  49.3 us
    all_to_all x1, starting transfers between devices, shards(): lax.all_to_all(stacked[1], 'row', split_axis=1, concat_axis=0, tiled=True)  12.6 us
    all_to_all x1, starting transfers between devices, shards(): lax.all_to_all(moved, 'row', split_axis=0, concat_axis=1, tiled=True)  12.3 us
    dot_general x2, matrix products, project(): jnp.einsum('nd,tde->tne', normed, weights, preferred_element_type=jnp.flo...  9.99 us
    all_to_all x1, starting transfers between devices, shards(): lax.all_to_all(stacked[2], 'row', split_axis=1, concat_axis=0, tiled=True)  9.16 us
    all_to_all x1, waiting for transfers between devices, shards(): lax.all_to_all(stacked[1], 'row', split_axis=1, concat_axis=0, tiled=True)  8.81 us
    all_to_all x1, starting transfers between devices, shards(): lax.all_to_all(stacked[0], 'row', split_axis=1, concat_axis=0, tiled=True)  7.6 us
  transfers between devices with their start and end apart: 6, of which 5 were waited for; matrix products, arithmetic and copies ran while one was open for 19% of the time, Pallas kernels for 0%

commit v1 on v0

v1 whole, which is shorter than its diff:
```python
import math

import jax
import jax.numpy as jnp
from jax import lax
from jax.experimental import pallas as pl
from jax.experimental.pallas import tpu as pltpu
from jax.sharding import PartitionSpec as P

HD = 128
CHUNKS = 2
OWNED = 4
F32 = jnp.float32
BF16 = jnp.bfloat16
MIB = 2**20
VM = pl.BlockSpec(memory_space=pltpu.VMEM)
SM = pl.BlockSpec(memory_space=pltpu.SMEM)


def call(body, ins, outs, flops, scratch=(), scalars=1):
    moved = sum(math.prod(x.shape) * x.dtype.itemsize for x in list(ins) + list(outs))
    return pl.pallas_call(
        body,
        out_shape=tuple(outs),
        in_specs=[SM] * scalars + [VM] * (len(ins) - scalars),
        out_specs=tuple([VM] * len(outs)),
        scratch_shapes=list(scratch),
        compiler_params=pltpu.CompilerParams(vmem_limit_bytes=28 * MIB),
        cost_estimate=pl.CostEstimate(flops=flops, bytes_accessed=moved, transcendentals=0),
    )(*ins)


def sds(shape, dtype=BF16):
    return jax.ShapeDtypeStruct(shape, dtype)


def block(number, width):
    return pl.ds(pl.multiple_of(number * width, width), width)


def interleave(first, second):
    n, f = first.shape
    a, b = first.reshape(n // 8, 8, f), second.reshape(n // 8, 8, f)
    low = lax.broadcasted_iota(jnp.int32, a.shape, 1) < OWNED
    t0 = jnp.where(low, a, pltpu.roll(b, OWNED, 1))
    t1 = jnp.where(low, pltpu.roll(a, OWNED, 1), b)
    return jnp.stack([t0, t1], axis=1).reshape(2 * n, f)


def deinterleave(tokens):
    n, f = tokens.shape
    both = tokens.reshape(n // 16, 2, 8, f)
    t0, t1 = both[:, 0], both[:, 1]
    low = lax.broadcasted_iota(jnp.int32, t0.shape, 1) < OWNED
    a = jnp.where(low, t0, pltpu.roll(t1, OWNED, 1))
    b = jnp.where(low, pltpu.roll(t0, OWNED, 1), t1)
    return a.reshape(n // 2, f), b.reshape(n // 2, f)


def norm_project_kernel(h_ref, a_ref, b_ref, c_ref, d_ref, gain_ref, w_ref, normed_ref, qkv_ref):
    h = h_ref[0]
    parts = ((a_ref, 0), (b_ref, 2), (c_ref, 1), (d_ref, 3))
    _, cols, width = a_ref.shape
    features = 4 * width
    tile = min(32, cols)

    @pl.loop(0, cols // tile)
    def _(i):
        at = pl.ds(pl.multiple_of(i * tile, tile), tile)
        stats = []
        for r in range(2):
            total = sum(jnp.sum(ref[r, at, :].astype(F32), axis=-1, keepdims=True) for ref, _ in parts)
            mean = total * (1.0 / features)
            sq = 0.0
            for ref, _ in parts:
                centred = ref[r, at, :].astype(F32) - mean
                sq = sq + jnp.sum(centred * centred, axis=-1, keepdims=True)
            stats.append((mean, lax.rsqrt(sq * (1.0 / features) + 1e-05)))
        for ref, flip in parts:
            where = block(h ^ flip, width)
            gain = gain_ref[:, where]
            rows = [(ref[r, at, :].astype(F32) - stats[r][0]) * stats[r][1] * gain for r in range(2)]
            to = pl.ds(pl.multiple_of(i * 2 * tile, 2 * tile), 2 * tile)
            normed_ref[to, where] = interleave(*rows).astype(BF16)

    for t in range(3):
        wide = w_ref.shape[2]
        qkv_ref[:, t * wide : (t + 1) * wide] = jnp.dot(
            normed_ref[...], w_ref[t], preferred_element_type=F32
        ).astype(BF16)


def attend(q_ref, q_at, keys, vals, start, bits, out_ref, out_at):
    n = q_ref.shape[0]
    tile = min(256, n)
    factor = math.log2(math.e) / HD**0.5
    for i in range(n // tile):
        q = q_ref[i * tile : (i + 1) * tile, q_at]
        scores = []
        upto = start + (i + 1) * tile
        used = []
        base = 0
        for k_ref, k_at in keys:
            have = k_ref.shape[0]
            take = min(have, upto - base)
            used.append((base, take))
            s = lax.dot_general(q, k_ref[:take, k_at], (((1,), (1,)), ((), ())), preferred_element_type=F32)
            ta = lax.broadcasted_iota(jnp.int32, s.shape, 0) + (start + i * tile)
            tb = lax.broadcasted_iota(jnp.int32, s.shape, 1) + base
            ok = (((ta ^ tb) & bits) == 0) & (tb <= ta)
            scores.append(jnp.where(ok, s * factor, -jnp.inf))
            base += have
        top = scores[0].max(axis=-1, keepdims=True)
        for s in scores[1:]:
            top = jnp.maximum(top, s.max(axis=-1, keepdims=True))
        expo = [jnp.exp2(s - top) for s in scores]
        total = sum(e.sum(axis=-1, keepdims=True) for e in expo)
        out = 0.0
        for e, (v_ref, v_at), (_, take) in zip(expo, vals, used):
            out = out + jnp.dot(e.astype(BF16), v_ref[:take, v_at], preferred_element_type=F32)
        out_ref[i * tile : (i + 1) * tile, out_at] = (out / total).astype(BF16)


def lanes(t, head, wide):
    return slice(t * wide + head * HD, t * wide + (head + 1) * HD)


def row_kernel(*refs):
    normed_ref, w_ref = refs[:2]
    earlier = refs[2:-2]
    attn_ref, qkv_ref = refs[-2:]
    wide = w_ref.shape[2]
    for t in range(3):
        qkv_ref[:, t * wide : (t + 1) * wide] = jnp.dot(
            normed_ref[...], w_ref[t], preferred_element_type=F32
        ).astype(BF16)
    sources = list(earlier) + [qkv_ref]
    start = sum(e.shape[0] for e in earlier)
    for head in range(wide // HD):
        attend(
            qkv_ref,
            lanes(0, head, wide),
            [(s, lanes(1, head, wide)) for s in sources],
            [(s, lanes(2, head, wide)) for s in sources],
            start,
            OWNED,
            attn_ref,
            lanes(0, head, wide),
        )


def col_kernel(qkv_ref, attn_ref):
    wide = attn_ref.shape[1]
    for head in range(wide // HD):
        attend(
            qkv_ref,
            lanes(0, head, wide),
            [(qkv_ref, lanes(1, head, wide))],
            [(qkv_ref, lanes(2, head, wide))],
            0,
            OWNED - 1,
            attn_ref,
            lanes(0, head, wide),
        )


def out_dot(row_ref, col_ref, wr_ref, wc_ref, where):
    return jnp.dot(row_ref[...], wr_ref[:, where], preferred_element_type=F32) + jnp.dot(
        col_ref[...], wc_ref[:, where], preferred_element_type=F32
    )


def out_core_kernel(h_ref, row_ref, col_ref, wr_ref, wc_ref, y3_ref, y1_ref):
    h = h_ref[0]
    width = y3_ref.shape[1]
    y3_ref[...] = out_dot(row_ref, col_ref, wr_ref, wc_ref, block(h ^ 3, width)).astype(BF16)
    y1_ref[...] = out_dot(row_ref, col_ref, wr_ref, wc_ref, block(h ^ 1, width)).astype(BF16)


def out_chip_kernel(h_ref, row_ref, col_ref, wr_ref, wc_ref, r2_ref, s2_ref):
    width = s2_ref.shape[1]
    own = out_dot(row_ref, col_ref, wr_ref, wc_ref, block(h_ref[0] ^ 2, width))
    s2_ref[...] = (own + r2_ref[...].astype(F32)).astype(BF16)


def out_own_kernel(h_ref, row_ref, col_ref, wr_ref, wc_ref, r0_ref, own_ref):
    width = own_ref.shape[1]
    own = out_dot(row_ref, col_ref, wr_ref, wc_ref, block(h_ref[0], width))
    own_ref[...] = own + r0_ref[...].astype(F32)


def final_kernel(samples_ref, *refs):
    out_ref = refs[-1]
    cols = samples_ref.shape[1] // CHUNKS
    for k in range(CHUNKS):
        own_ref, rx_ref = refs[2 * k], refs[2 * k + 1]
        step = min(64, cols)

        @pl.loop(0, cols // step)
        def _(i):
            tok = pl.ds(pl.multiple_of(i * 2 * step, 2 * step), 2 * step)
            pair = deinterleave(own_ref[tok, :] + rx_ref[tok, :].astype(F32))
            at = pl.ds(pl.multiple_of(k * cols + i * step, step), step)
            for r in range(2):
                out_ref[r, at, :] = (samples_ref[r, at, :].astype(F32) + pair[r]).astype(BF16)


def shards(samples, norm_gain, row_qkv, col_qkv, row_out, col_out):
    rows, cols, width = samples.shape
    wide = col_qkv.shape[2]
    features = 4 * width
    part = cols // CHUNKS
    tokens = rows * part
    h = lax.axis_index("head").astype(jnp.int32).reshape(1)
    gain = norm_gain.reshape(1, features)

    def over_chip(x):
        return lax.ppermute(x, "head", [(i, i ^ 2) for i in range(4)])

    def over_core(x):
        return lax.ppermute(x, "head", [(i, i ^ 1) for i in range(4)])

    def exchange(x):
        return lax.all_to_all(x, "row", 0, 0, tiled=True)

    qkv_flops = 2 * tokens * features * 3 * wide
    moved, normed = [], []
    for k in range(CHUNKS):
        a = samples[:, k * part : (k + 1) * part, :]
        b = over_chip(a)
        c = over_core(a)
        d = over_core(b)
        n, col = call(
            norm_project_kernel,
            (h, a, b, c, d, gain, col_qkv),
            (sds((tokens, features)), sds((tokens, 3 * wide))),
            qkv_flops,
        )
        normed.append(n)
        moved.append(exchange(col))
    row_attn, row_state = [], []
    for k in range(CHUNKS):
        attn, state = call(
            row_kernel,
            (normed[k], row_qkv, *row_state),
            (sds((tokens, wide)), sds((tokens, 3 * wide))),
            qkv_flops + 4 * (k + 1) * tokens * tokens * wide,
            scalars=0,
        )
        row_attn.append(attn)
        row_state.append(state)
    pairs = []
    for k in range(CHUNKS):
        (attn,) = call(
            col_kernel, (moved[k],), (sds((tokens, wide)),), 4 * tokens * tokens * wide, scalars=0
        )
        ops = (h, row_attn[k], exchange(attn), row_out, col_out)
        piece = 4 * tokens * wide * width
        y3, y1 = call(out_core_kernel, ops, (sds((tokens, width)),) * 2, 2 * piece)
        (s2,) = call(out_chip_kernel, ops + (over_core(y3),), (sds((tokens, width)),), piece)
        (own,) = call(out_own_kernel, ops + (over_core(y1),), (sds((tokens, width), F32),), piece)
        pairs += [own, over_chip(s2)]
    (out,) = call(final_kernel, (samples, *pairs), (sds(samples.shape),), samples.size, scalars=0)
    return out


def solution(mesh):
    placed = (
        P("row", None, "head"),
        P(),
        P(None, None, "head"),
        P(None, None, "head"),
        P("head", None),
        P("head", None),
    )
    return jax.shard_map(
        shards, mesh=mesh, in_specs=placed, out_specs=P("row", None, "head"), check_vma=False
    )
```

time: 258 us -> 181 us (0.70)
  waiting for transfers between devices: 119 us -> 82 us
  matrix products: 34.1 us -> 0 us
  Pallas kernels: 0 us -> 29.6 us
  local copies, waits for them, and re-layouts: 32.4 us -> 12.7 us
  other arithmetic: 16 us -> 0 us
  between operations: 13.6 us -> 0.18 us
  starting transfers between devices: 41.9 us -> 55.3 us
    all_gather x1 -> x0, waiting for transfers between devices: 55.2 us -> none  [shards(): whole = lax.all_gather(samples, 'head', axis=2, tiled=True)]
    ppermute x0 -> x12, waiting for transfers between devices: none -> 53.2 us  [the longest x4 49.7 us: over_chip(): return lax.ppermute(x, 'head', [(i, i ^ 2) for i in range(4)])]
    reduce_scatter x1 -> x0, waiting for transfers between devices: 49.3 us -> none  [shards(): lax.psum_scatter(partial_term.astype(jnp.bfloat16), 'head', scatter_dimen...]
    dot_general x8 -> x0, matrix products: 34.1 us -> none  [the longest x2 9.99 us: project(): jnp.einsum('nd,tde->tne', normed, weights, preferred_element_type=jnp.flo...]
    pallas_call x0 -> x13, Pallas kernels: none -> 29.6 us  [call(): pl.pallas_call(body, out_shape=tuple(outs), in_specs=[SM] * scalars + [VM...]
    squeeze x9 -> x0, local copies, waits for them, and re-layouts: 18.4 us -> none  [the longest x3 6.18 us: shards(): stacked[2]]
    all_to_all x4, waiting for transfers between devices: 13.8 us -> 28.8 us  [exchange(): return lax.all_to_all(x, 'row', 0, 0, tiled=True)]
    ppermute x0 -> x12, starting transfers between devices: none -> 13 us  [the longest x8 8.85 us: over_core(): return lax.ppermute(x, 'head', [(i, i ^ 1) for i in range(4)])]
  transfers between devices with their start and end apart: 6 -> 16, of which waited for: 5 -> 9; matrix products, arithmetic and copies ran while one was open for 19% -> 0% of each run, Pallas kernels for 0% -> 13%
where the time goes in v1:
time: 181 us; the launch traced here: 180 us
  waiting for transfers between devices  82 us (45%)
  starting transfers between devices  55.3 us (31%)
  Pallas kernels  29.6 us (16%)
  local copies, waits for them, and re-layouts  12.7 us (7%)
    ppermute x4, waiting for transfers between devices, over_chip(): return lax.ppermute(x, 'head', [(i, i ^ 2) for i in range(4)])  49.7 us
    all_to_all x4, starting transfers between devices, exchange(): return lax.all_to_all(x, 'row', 0, 0, tiled=True)  42.3 us
    pallas_call x13, Pallas kernels, call(): pl.pallas_call(body, out_shape=tuple(outs), in_specs=[SM] * scalars + [VM...  29.6 us
    all_to_all x4, waiting for transfers between devices, exchange(): return lax.all_to_all(x, 'row', 0, 0, tiled=True)  28.8 us
    unnamed x28, local copies, waits for them, and re-layouts  11.5 us
    ppermute x8, starting transfers between devices, over_core(): return lax.ppermute(x, 'head', [(i, i ^ 1) for i in range(4)])  8.85 us
    ppermute x4, starting transfers between devices, over_chip(): return lax.ppermute(x, 'head', [(i, i ^ 2) for i in range(4)])  4.17 us
  transfers between devices with their start and end apart: 16, of which 9 were waited for; matrix products, arithmetic and copies ran while one was open for 0% of the time, Pallas kernels for 13%

profile of v1, /device:TPU:1, one launch (start us, length us, event | category | flops | bytes accessed | tf_op | source)
XLA Modules:
  0.0 179.9 jit_solution(9922493654575632624)
XLA Ops:
  0.0 1.3 fusion
  1.3 2.1 %collective-permute-start.6 = (bf16[2,256,512]{2,1,0:T(8,128)(2,1)S(1)}, bf16[2,256,512]{2,1,0:T(8,128)(2,1)S(1)}, u32[]{:S(2)}, u32[]{:S(2)}) collective-permute-start(bf16[2,256,512]{2,1,0:T(8,128)(2,1)S(1)} %get-tuple-element.27.a_ref), channel_id=1, source_target_pairs={{0,2},{1,3},{2,0},{3,1},{4,6},{5,7},{6,4},{7,5},{8,10},{9,11},{10,... | collective-permute-start | bytes 1572872 | tf_op jit(solution)/shard_map/ppermute | solution.py:218
  3.4 1.3 collective-permute-start.7
  4.7 9.0 %collective-permute-done.6.b_ref = bf16[2,256,512]{2,1,0:T(8,128)(2,1)S(1)} collective-permute-done((bf16[2,256,512]{2,1,0:T(8,128)(2,1)S(1)}, bf16[2,256,512]{2,1,0:T(8,128)(2,1)S(1)}, u32[]{:S(2)}, u32[]{:S(2)}) %collective-permute-start.6) | collective-permute-done | bytes 524320 | tf_op jit(solution)/shard_map/ppermute | solution.py:218
  13.7 2.6 %collective-permute-start.8 = (bf16[2,256,512]{2,1,0:T(8,128)(2,1)S(1)}, bf16[2,256,512]{2,1,0:T(8,128)(2,1)S(1)}, u32[]{:S(2)}, u32[]{:S(2)}) collective-permute-start(bf16[2,256,512]{2,1,0:T(8,128)(2,1)S(1)} %collective-permute-done.6.b_ref), channel_id=1, source_target_pairs={{0,1},{1,0},{2,3},{3,2},{4,5},{5,4},{6,7},{7,6},{8,9},{9,8},{10,11... | collective-permute-start | bytes 1572872 | tf_op jit(solution)/shard_map/ppermute | solution.py:221
  16.3 0.0 collective-permute-done.7.c_ref
  16.3 1.5 collective-permute-done.8.d_ref
  17.8 1.9 %copy-done.3 = bf16[3,2048,256]{2,1,0:T(8,128)(2,1)S(1)} copy-done((bf16[3,2048,256]{2,1,0:T(8,128)(2,1)S(1)}, bf16[3,2048,256]{2,1,0:T(8,128)(2,1)}, u32[]{:S(2)}) %copy-start.3) | copy-done | bytes 3145752
  19.7 0.7 copy-done.8
  20.4 5.6 %shard_map.70 = (bf16[512,2048]{1,0:T(8,128)(2,1)S(1)}, bf16[512,768]{1,0:T(8,128)(2,1)}) custom-call(s32[1]{0:T(128)} %bitcast.h_ref, bf16[2,256,512]{2,1,0:T(8,128)(2,1)S(1)} %get-tuple-element.27.a_ref, bf16[2,256,512]{2,1,0:T(8,128)(2,1)S(1)} %collective-permute-done.6.b_ref, bf16[2,256,512]{2,1,0:T(8,128)(2,1)S(1)} %collective-permute-done.7.c_ref, ...), custom_call_target="tpu_custom_call" | custom-call | flops 1610612736 | bytes 8134660 | tf_op jit(solution)/shard_map/pallas_call | solution.py:22
  26.0 1.4 copy-done.10
  27.3 14.5 %all-to-all-start.2 = ((bf16[64,8,768]{2,1,0:T(8,128)(2,1)}), bf16[64,8,768]{2,1,0:T(8,128)(2,1)S(1)}, u32[]{:S(2)}, u32[]{:S(2)}) async-start(bf16[64,8,768]{2,1,0:T(8,128)(2,1)} %bitcast.6), calls=%async_computation.2 | async-start | bytes 1572864 | tf_op jit(solution)/shard_map/all_to_all | solution.py:224
  41.9 0.4 collective-permute-start
  42.3 0.9 collective-permute-start.1
  43.2 19.2 %collective-permute-done.b_ref = bf16[2,256,512]{2,1,0:T(8,128)(2,1)S(1)} collective-permute-done((bf16[2,256,512]{2,1,0:T(8,128)(2,1)S(1)}, bf16[2,256,512]{2,1,0:T(8,128)(2,1)S(1)}, u32[]{:S(2)}, u32[]{:S(2)}) %collective-permute-start) | collective-permute-done | bytes 524320 | tf_op jit(solution)/shard_map/ppermute | solution.py:218
  62.5 1.3 collective-permute-start.2
  63.8 0.0 collective-permute-done.1.c_ref
  63.8 1.5 collective-permute-done.2.d_ref
  65.3 0.0 copy-done.9
  65.3 1.9 %copy-done.4 = bf16[3,2048,256]{2,1,0:T(8,128)(2,1)S(1)} copy-done((bf16[3,2048,256]{2,1,0:T(8,128)(2,1)S(1)}, bf16[3,2048,256]{2,1,0:T(8,128)(2,1)}, u32[]{:S(2)}) %copy-start.4) | copy-done | bytes 3145752
  67.2 5.5 %shard_map.64 = (bf16[512,2048]{1,0:T(8,128)(2,1)S(1)}, bf16[512,768]{1,0:T(8,128)(2,1)}) custom-call(s32[1]{0:T(128)} %bitcast.h_ref, bf16[2,256,512]{2,1,0:T(8,128)(2,1)S(1)} %get-tuple-element.28.a_ref, bf16[2,256,512]{2,1,0:T(8,128)(2,1)S(1)} %collective-permute-done.b_ref, bf16[2,256,512]{2,1,0:T(8,128)(2,1)S(1)} %collective-permute-done.1.c_ref, ...), custom_call_target="tpu_custom_call" | custom-call | flops 1610612736 | bytes 8134660 | tf_op jit(solution)/shard_map/pallas_call | solution.py:22
  72.8 1.3 copy-done.12
  74.1 0.0 all-to-all-done.2
  74.1 12.3 %all-to-all-start = ((bf16[64,8,768]{2,1,0:T(8,128)(2,1)}), bf16[64,8,768]{2,1,0:T(8,128)(2,1)S(1)}, u32[]{:S(2)}, u32[]{:S(2)}) async-start(bf16[64,8,768]{2,1,0:T(8,128)(2,1)} %bitcast.2), calls=%async_computation | async-start | bytes 1572864 | tf_op jit(solution)/shard_map/all_to_all | solution.py:224
  86.4 2.1 %shard_map.72 = bf16[512,256]{1,0:T(8,128)(2,1)} custom-call(bf16[512,768]{1,0:T(8,128)(2,1)S(1)} %bitcast.16), custom_call_target="tpu_custom_call" | custom-call | flops 268435456 | bytes 1048576 | tf_op jit(solution)/shard_map/pallas_call | solution.py:22
  88.5 19.0 %all-to-all-done = bf16[64,8,768]{2,1,0:T(8,128)(2,1)S(1)} async-done(((bf16[64,8,768]{2,1,0:T(8,128)(2,1)}), bf16[64,8,768]{2,1,0:T(8,128)(2,1)S(1)}, u32[]{:S(2)}, u32[]{:S(2)}) %all-to-all-start) | async-done | bytes 786464 | tf_op jit(solution)/shard_map/all_to_all | solution.py:224
  107.5 8.8 %all-to-all-start.3 = ((bf16[64,8,256]{2,1,0:T(8,128)(2,1)}), bf16[64,8,256]{2,1,0:T(8,128)(2,1)S(1)}, u32[]{:S(2)}, u32[]{:S(2)}) async-start(bf16[64,8,256]{2,1,0:T(8,128)(2,1)} %bitcast.8), calls=%async_computation.3 | async-start | bytes 524288 | tf_op jit(solution)/shard_map/all_to_all | solution.py:224
  116.3 2.1 %shard_map.66 = bf16[512,256]{1,0:T(8,128)(2,1)} custom-call(bf16[512,768]{1,0:T(8,128)(2,1)S(1)} %bitcast.17), custom_call_target="tpu_custom_call" | custom-call | flops 268435456 | bytes 1048576 | tf_op jit(solution)/shard_map/pallas_call | solution.py:22
  118.4 9.8 %all-to-all-done.3 = bf16[64,8,256]{2,1,0:T(8,128)(2,1)S(1)} async-done(((bf16[64,8,256]{2,1,0:T(8,128)(2,1)}), bf16[64,8,256]{2,1,0:T(8,128)(2,1)S(1)}, u32[]{:S(2)}, u32[]{:S(2)}) %all-to-all-start.3) | async-done | bytes 262176 | tf_op jit(solution)/shard_map/all_to_all | solution.py:224
  128.2 6.7 %all-to-all-start.1 = ((bf16[64,8,256]{2,1,0:T(8,128)(2,1)}), bf16[64,8,256]{2,1,0:T(8,128)(2,1)S(1)}, u32[]{:S(2)}, u32[]{:S(2)}) async-start(bf16[64,8,256]{2,1,0:T(8,128)(2,1)} %bitcast.4), calls=%async_computation.1 | async-start | bytes 524288 | tf_op jit(solution)/shard_map/all_to_all | solution.py:224
  134.9 0.0 copy-start.5
  134.9 1.9 %copy-done.5 = bf16[3,2048,256]{2,1,0:T(8,128)(2,1)S(1)} copy-done((bf16[3,2048,256]{2,1,0:T(8,128)(2,1)S(1)}, bf16[3,2048,256]{2,1,0:T(8,128)(2,1)}, u32[]{:S(2)}) %copy-start.5) | copy-done | bytes 3145752
  136.8 1.6 copy-done.13
  138.4 3.5 %shard_map.65 = (bf16[512,256]{1,0:T(8,128)(2,1)S(1)}, bf16[512,768]{1,0:T(8,128)(2,1)S(1)}) custom-call(bf16[512,2048]{1,0:T(8,128)(2,1)S(1)} %copy-done.13, bf16[3,2048,256]{2,1,0:T(8,128)(2,1)S(1)} %copy-done.5), custom_call_target="tpu_custom_call" | custom-call | flops 1879048192 | bytes 6291456 | tf_op jit(solution)/shard_map/pallas_call | solution.py:22
  141.9 0.0 copy-done.6
  141.9 0.0 copy-done.11
  141.9 0.0 copy-start
  141.9 0.0 copy-start.1
  141.9 4.5 %shard_map.71 = (bf16[512,256]{1,0:T(8,128)(2,1)S(1)}, bf16[512,768]{1,0:T(8,128)(2,1)}) custom-call(bf16[512,2048]{1,0:T(8,128)(2,1)S(1)} %copy-done.11, bf16[3,2048,256]{2,1,0:T(8,128)(2,1)S(1)} %copy-done.6, bf16[512,768]{1,0:T(8,128)(2,1)S(1)} %get-tuple-element.22.refs_2_), custom_call_target="tpu_custom_call" | custom-call | flops 2147483648 | bytes 7077888 | tf_op jit(solution)/shard_map/pallas_call | solution.py:22
  146.4 0.0 copy-done
  146.4 0.0 copy-done.1
  146.4 1.4 shard_map.73
  147.8 0.8 copy-done.7
  148.6 2.0 %collective-permute-start.10 = (bf16[512,512]{1,0:T(8,128)(2,1)}, bf16[512,512]{1,0:T(8,128)(2,1)}, u32[]{:S(2)}, u32[]{:S(2)}) collective-permute-start(bf16[512,512]{1,0:T(8,128)(2,1)} %get-tuple-element.26), channel_id=1, source_target_pairs={{0,1},{1,0},{2,3},{3,2},{4,5},{5,4},{6,7},{7,6},{8,9},{9,8},{10,11... | collective-permute-start | bytes 1572872 | tf_op jit(solution)/shard_map/ppermute | solution.py:221
  150.7 0.0 all-to-all-done.1
  150.7 0.7 shard_map.67
  151.4 0.1 collective-permute-start.4
  151.5 0.5 collective-permute-start.9
  152.0 0.1 collective-permute-start.3
  152.1 0.5 collective-permute-done.10.r2_ref
  152.5 1.5 shard_map.75
  154.0 0.3 collective-permute-start.11
  154.3 0.0 collective-permute-done.4.r2_ref
  154.3 0.4 shard_map.69
  154.8 1.3 collective-permute-start.5
  156.1 0.0 collective-permute-done.9.r0_ref
  156.1 0.4 shard_map.74.refs_2_
  156.6 0.0 copy-start.2
  156.6 0.0 collective-permute-done.3.r0_ref
  156.6 0.4 shard_map.68.refs_0_
  157.0 10.2 %collective-permute-done.11.refs_3_ = bf16[512,512]{1,0:T(8,128)(2,1)S(1)} collective-permute-done((bf16[512,512]{1,0:T(8,128)(2,1)S(1)}, bf16[512,512]{1,0:T(8,128)(2,1)S(1)}, u32[]{:S(2)}, u32[]{:S(2)}) %collective-permute-start.11) | collective-permute-done | bytes 524320 | tf_op jit(solution)/shard_map/ppermute | solution.py:218
  167.2 11.2 %collective-permute-done.5.refs_1_ = bf16[512,512]{1,0:T(8,128)(2,1)S(1)} collective-permute-done((bf16[512,512]{1,0:T(8,128)(2,1)S(1)}, bf16[512,512]{1,0:T(8,128)(2,1)S(1)}, u32[]{:S(2)}, u32[]{:S(2)}) %collective-permute-start.5) | collective-permute-done | bytes 524320 | tf_op jit(solution)/shard_map/ppermute | solution.py:218
  178.5 0.0 copy-done.2
  178.5 1.5 shard_map.76
  (10 shorter events, 0.0 us)
Async XLA Ops:
  1.3 12.4 %collective-permute-start.6 = (bf16[2,256,512]{2,1,0:T(8,128)(2,1)S(1)}, bf16[2,256,512]{2,1,0:T(8,128)(2,1)S(1)}, u32[]{:S(2)}, u32[]{:S(2)}) collective-permute-start(bf16[2,256,512]{2,1,0:T(8,128)(2,1)S(1)} %get-tuple-element.27.a_ref), channel_id=1, source_target_pairs={{0,2},{1,3},{2,0},{3,1},{4,6},{5,7},{6,4},{7,5},{8,10},{9,11},{10,... | collective-permute-start | bytes 1572872 | tf_op jit(solution)/shard_map/ppermute | solution.py:218
  3.4 12.9 %collective-permute-start.7 = (bf16[2,256,512]{2,1,0:T(8,128)(2,1)S(1)}, bf16[2,256,512]{2,1,0:T(8,128)(2,1)S(1)}, u32[]{:S(2)}, u32[]{:S(2)}) collective-permute-start(bf16[2,256,512]{2,1,0:T(8,128)(2,1)S(1)} %get-tuple-element.27.a_ref), channel_id=1, source_target_pairs={{0,1},{1,0},{2,3},{3,2},{4,5},{5,4},{6,7},{7,6},{8,9},{9,8},{10,11... | collective-permute-start | bytes 1572872 | tf_op jit(solution)/shard_map/ppermute | solution.py:221
  13.7 4.1 %collective-permute-start.8 = (bf16[2,256,512]{2,1,0:T(8,128)(2,1)S(1)}, bf16[2,256,512]{2,1,0:T(8,128)(2,1)S(1)}, u32[]{:S(2)}, u32[]{:S(2)}) collective-permute-start(bf16[2,256,512]{2,1,0:T(8,128)(2,1)S(1)} %collective-permute-done.6.b_ref), channel_id=1, source_target_pairs={{0,1},{1,0},{2,3},{3,2},{4,5},{5,4},{6,7},{7,6},{8,9},{9,8},{10,11... | collective-permute-start | bytes 1572872 | tf_op jit(solution)/shard_map/ppermute | solution.py:221
  17.8 1.9 %copy-start.3 = (bf16[3,2048,256]{2,1,0:T(8,128)(2,1)S(1)}, bf16[3,2048,256]{2,1,0:T(8,128)(2,1)}, u32[]{:S(2)}) copy-start(bf16[3,2048,256]{2,1,0:T(8,128)(2,1)} %w_ref.3) | copy-start | bytes 9437188
  19.7 0.7 copy-start.8
  20.4 44.9 %copy-start.9 = (f32[2048]{0:T(1024)S(1)}, f32[2048]{0:T(1024)}, u32[]{:S(2)}) copy-start(f32[2048]{0:T(1024)} %param.7) | copy-start | bytes 24580
  26.0 1.4 copy-start.10
  27.3 46.7 %all-to-all-start.2 = ((bf16[64,8,768]{2,1,0:T(8,128)(2,1)}), bf16[64,8,768]{2,1,0:T(8,128)(2,1)S(1)}, u32[]{:S(2)}, u32[]{:S(2)}) async-start(bf16[64,8,768]{2,1,0:T(8,128)(2,1)} %bitcast.6), calls=%async_computation.2 | async-start | bytes 1572864 | tf_op jit(solution)/shard_map/all_to_all | solution.py:224
  41.9 20.6 %collective-permute-start = (bf16[2,256,512]{2,1,0:T(8,128)(2,1)S(1)}, bf16[2,256,512]{2,1,0:T(8,128)(2,1)S(1)}, u32[]{:S(2)}, u32[]{:S(2)}) collective-permute-start(bf16[2,256,512]{2,1,0:T(8,128)(2,1)S(1)} %get-tuple-element.28.a_ref), channel_id=1, source_target_pairs={{0,2},{1,3},{2,0},{3,1},{4,6},{5,7},{6,4},{7,5},{8,10},{9,11},{10,... | collective-permute-start | bytes 1572872 | tf_op jit(solution)/shard_map/ppermute | solution.py:218
  42.3 21.5 %collective-permute-start.1 = (bf16[2,256,512]{2,1,0:T(8,128)(2,1)S(1)}, bf16[2,256,512]{2,1,0:T(8,128)(2,1)S(1)}, u32[]{:S(2)}, u32[]{:S(2)}) collective-permute-start(bf16[2,256,512]{2,1,0:T(8,128)(2,1)S(1)} %get-tuple-element.28.a_ref), channel_id=1, source_target_pairs={{0,1},{1,0},{2,3},{3,2},{4,5},{5,4},{6,7},{7,6},{8,9},{9,8},{10,11... | collective-permute-start | bytes 1572872 | tf_op jit(solution)/shard_map/ppermute | solution.py:221
  62.5 2.8 %collective-permute-start.2 = (bf16[2,256,512]{2,1,0:T(8,128)(2,1)S(1)}, bf16[2,256,512]{2,1,0:T(8,128)(2,1)S(1)}, u32[]{:S(2)}, u32[]{:S(2)}) collective-permute-start(bf16[2,256,512]{2,1,0:T(8,128)(2,1)S(1)} %collective-permute-done.b_ref), channel_id=1, source_target_pairs={{0,1},{1,0},{2,3},{3,2},{4,5},{5,4},{6,7},{7,6},{8,9},{9,8},{10,11... | collective-permute-start | bytes 1572872 | tf_op jit(solution)/shard_map/ppermute | solution.py:221
  65.3 1.9 %copy-start.4 = (bf16[3,2048,256]{2,1,0:T(8,128)(2,1)S(1)}, bf16[3,2048,256]{2,1,0:T(8,128)(2,1)}, u32[]{:S(2)}) copy-start(bf16[3,2048,256]{2,1,0:T(8,128)(2,1)} %w_ref.3) | copy-start | bytes 9437188
  72.7 1.3 copy-start.12
  74.1 33.4 %all-to-all-start = ((bf16[64,8,768]{2,1,0:T(8,128)(2,1)}), bf16[64,8,768]{2,1,0:T(8,128)(2,1)S(1)}, u32[]{:S(2)}, u32[]{:S(2)}) async-start(bf16[64,8,768]{2,1,0:T(8,128)(2,1)} %bitcast.2), calls=%async_computation | async-start | bytes 1572864 | tf_op jit(solution)/shard_map/all_to_all | solution.py:224
  107.5 20.7 %all-to-all-start.3 = ((bf16[64,8,256]{2,1,0:T(8,128)(2,1)}), bf16[64,8,256]{2,1,0:T(8,128)(2,1)S(1)}, u32[]{:S(2)}, u32[]{:S(2)}) async-start(bf16[64,8,256]{2,1,0:T(8,128)(2,1)} %bitcast.8), calls=%async_computation.3 | async-start | bytes 524288 | tf_op jit(solution)/shard_map/all_to_all | solution.py:224
  128.2 22.4 %all-to-all-start.1 = ((bf16[64,8,256]{2,1,0:T(8,128)(2,1)}), bf16[64,8,256]{2,1,0:T(8,128)(2,1)S(1)}, u32[]{:S(2)}, u32[]{:S(2)}) async-start(bf16[64,8,256]{2,1,0:T(8,128)(2,1)} %bitcast.4), calls=%async_computation.1 | async-start | bytes 524288 | tf_op jit(solution)/shard_map/all_to_all | solution.py:224
  134.9 1.9 %copy-start.5 = (bf16[3,2048,256]{2,1,0:T(8,128)(2,1)S(1)}, bf16[3,2048,256]{2,1,0:T(8,128)(2,1)}, u32[]{:S(2)}) copy-start(bf16[3,2048,256]{2,1,0:T(8,128)(2,1)} %refs_1_.3) | copy-start | bytes 9437188
  136.8 1.6 copy-start.13
  138.4 3.5 %copy-start.6 = (bf16[3,2048,256]{2,1,0:T(8,128)(2,1)S(1)}, bf16[3,2048,256]{2,1,0:T(8,128)(2,1)}, u32[]{:S(2)}) copy-start(bf16[3,2048,256]{2,1,0:T(8,128)(2,1)} %refs_1_.3) | copy-start | bytes 9437188
  138.4 3.5 %copy-start.11 = (bf16[512,2048]{1,0:T(8,128)(2,1)S(1)}, bf16[512,2048]{1,0:T(8,128)(2,1)}, u32[]{:S(2)}) copy-start(bf16[512,2048]{1,0:T(8,128)(2,1)} %copy-done.10) | copy-start | bytes 6291460
  141.9 4.5 %copy-start = (bf16[256,2048]{1,0:T(8,128)(2,1)S(1)}, bf16[256,2048]{1,0:T(8,128)(2,1)}, u32[]{:S(2)}) copy-start(bf16[256,2048]{1,0:T(8,128)(2,1)} %wr_ref.11) | copy-start | bytes 3145732
  141.9 4.5 %copy-start.1 = (bf16[256,2048]{1,0:T(8,128)(2,1)S(1)}, bf16[256,2048]{1,0:T(8,128)(2,1)}, u32[]{:S(2)}) copy-start(bf16[256,2048]{1,0:T(8,128)(2,1)} %wc_ref.11) | copy-start | bytes 3145732
  147.8 0.8 copy-start.7
  148.6 3.9 %collective-permute-start.10 = (bf16[512,512]{1,0:T(8,128)(2,1)}, bf16[512,512]{1,0:T(8,128)(2,1)}, u32[]{:S(2)}, u32[]{:S(2)}) collective-permute-start(bf16[512,512]{1,0:T(8,128)(2,1)} %get-tuple-element.26), channel_id=1, source_target_pairs={{0,1},{1,0},{2,3},{3,2},{4,5},{5,4},{6,7},{7,6},{8,9},{9,8},{10,11... | collective-permute-start | bytes 1572872 | tf_op jit(solution)/shard_map/ppermute | solution.py:221
  151.4 3.0 %collective-permute-start.4 = (bf16[512,512]{1,0:T(8,128)(2,1)S(1)}, bf16[512,512]{1,0:T(8,128)(2,1)S(1)}, u32[]{:S(2)}, u32[]{:S(2)}) collective-permute-start(bf16[512,512]{1,0:T(8,128)(2,1)S(1)} %get-tuple-element.20), channel_id=1, source_target_pairs={{0,1},{1,0},{2,3},{3,2},{4,5},{5,4},{6,7},{7,6},{8,9},{9,8},{10,11... | collective-permute-start | bytes 1572872 | tf_op jit(solution)/shard_map/ppermute | solution.py:221
  151.5 4.6 %collective-permute-start.9 = (bf16[512,512]{1,0:T(8,128)(2,1)}, bf16[512,512]{1,0:T(8,128)(2,1)S(1)}, u32[]{:S(2)}, u32[]{:S(2)}) collective-permute-start(bf16[512,512]{1,0:T(8,128)(2,1)} %copy-done.7), channel_id=1, source_target_pairs={{0,1},{1,0},{2,3},{3,2},{4,5},{5,4},{6,7},{7,6},{8,9},{9,8},{10,11... | collective-permute-start | bytes 1572872 | tf_op jit(solution)/shard_map/ppermute | solution.py:221
  152.0 4.6 %collective-permute-start.3 = (bf16[512,512]{1,0:T(8,128)(2,1)S(1)}, bf16[512,512]{1,0:T(8,128)(2,1)S(1)}, u32[]{:S(2)}, u32[]{:S(2)}) collective-permute-start(bf16[512,512]{1,0:T(8,128)(2,1)S(1)} %get-tuple-element.19), channel_id=1, source_target_pairs={{0,1},{1,0},{2,3},{3,2},{4,5},{5,4},{6,7},{7,6},{8,9},{9,8},{10,11... | collective-permute-start | bytes 1572872 | tf_op jit(solution)/shard_map/ppermute | solution.py:221
  154.0 13.2 %collective-permute-start.11 = (bf16[512,512]{1,0:T(8,128)(2,1)S(1)}, bf16[512,512]{1,0:T(8,128)(2,1)S(1)}, u32[]{:S(2)}, u32[]{:S(2)}) collective-permute-start(bf16[512,512]{1,0:T(8,128)(2,1)S(1)} %shard_map.75), channel_id=1, source_target_pairs={{0,2},{1,3},{2,0},{3,1},{4,6},{5,7},{6,4},{7,5},{8,10},{9,11},{10,... | collective-permute-start | bytes 1572872 | tf_op jit(solution)/shard_map/ppermute | solution.py:218
  154.8 23.7 %collective-permute-start.5 = (bf16[512,512]{1,0:T(8,128)(2,1)S(1)}, bf16[512,512]{1,0:T(8,128)(2,1)S(1)}, u32[]{:S(2)}, u32[]{:S(2)}) collective-permute-start(bf16[512,512]{1,0:T(8,128)(2,1)S(1)} %shard_map.69), channel_id=1, source_target_pairs={{0,2},{1,3},{2,0},{3,1},{4,6},{5,7},{6,4},{7,5},{8,10},{9,11},{10,... | collective-permute-start | bytes 1572872 | tf_op jit(solution)/shard_map/ppermute | solution.py:218
  156.6 21.9 %copy-start.2 = (bf16[2,512,512]{2,1,0:T(8,128)(2,1)S(1)}, bf16[2,512,512]{2,1,0:T(8,128)(2,1)}, u32[]{:S(2)}) copy-start(bf16[2,512,512]{2,1,0:T(8,128)(2,1)} %samples_ref.1) | copy-start | bytes 3145732

commit v2 on v1

v2 whole, which is shorter than its diff:
```python
import functools
import math

import jax
import jax.numpy as jnp
from jax import lax
from jax.experimental import pallas as pl
from jax.experimental.pallas import tpu as pltpu
from jax.sharding import PartitionSpec as P

HD = 128
OWNED = 4
F32 = jnp.float32
BF16 = jnp.bfloat16
ROOMY, WHOLE = 24, 60
SM = pl.BlockSpec(memory_space=pltpu.SMEM)
ANY = pl.BlockSpec(memory_space=pl.ANY)


VM = pl.BlockSpec(memory_space=pltpu.VMEM)


def params(limit):
    return pltpu.CompilerParams(vmem_limit_bytes=limit * 2**20)


def cost(flops, arrays, weight=1):
    moved = sum(math.prod(x.shape) * x.dtype.itemsize for x in arrays)
    return pl.CostEstimate(flops=flops * weight, bytes_accessed=moved * weight, transcendentals=0)


def call(body, scalars, ins, raws, outs, flops, scratch=(), after=()):
    used = len(scalars) + len(ins) + len(raws)

    def kernel(*refs):
        body(*refs[:used], *refs[used + len(after) :])

    return pl.pallas_call(
        kernel,
        out_shape=tuple(outs),
        in_specs=[SM] * len(scalars) + [VM] * len(ins) + [ANY] * (len(raws) + len(after)),
        out_specs=tuple([VM] * len(outs)),
        scratch_shapes=list(scratch),
        compiler_params=params(ROOMY),
        cost_estimate=cost(flops, list(ins) + list(raws) + list(outs)),
    )(*scalars, *ins, *raws, *after)


def sds(shape, dtype=BF16):
    return jax.ShapeDtypeStruct(shape, dtype)


def block(number, width):
    return pl.ds(pl.multiple_of(number * width, width), width)


def interleave(first, second):
    n, f = first.shape
    a, b = first.reshape(n // 8, 8, f), second.reshape(n // 8, 8, f)
    low = lax.broadcasted_iota(jnp.int32, a.shape, 1) < OWNED
    t0 = jnp.where(low, a, pltpu.roll(b, OWNED, 1))
    t1 = jnp.where(low, pltpu.roll(a, OWNED, 1), b)
    return t0.reshape(n, f), t1.reshape(n, f)


def deinterleave(t0, t1):
    n, f = t0.shape
    t0, t1 = t0.reshape(n // 8, 8, f), t1.reshape(n // 8, 8, f)
    low = lax.broadcasted_iota(jnp.int32, t0.shape, 1) < OWNED
    a = jnp.where(low, t0, pltpu.roll(t1, OWNED, 1))
    b = jnp.where(low, pltpu.roll(t0, OWNED, 1), t1)
    return a.reshape(n, f), b.reshape(n, f)


def fetch(sources, targets, sems):
    copies = [pltpu.make_async_copy(s, t, sems.at[i]) for i, (s, t) in enumerate(zip(sources, targets))]
    for copy in copies:
        copy.start()
    return copies


def lanes(t, head, wide):
    return slice(t * wide + head * HD, t * wide + (head + 1) * HD)


def attend(q_ref, q_at, keys, vals, start, bits, out_ref, out_at):
    n = q_ref.shape[0]
    tile = min(256, n)
    factor = math.log2(math.e) / HD**0.5
    for i in range(n // tile):
        q = q_ref[i * tile : (i + 1) * tile, q_at]
        scores = []
        upto = start + (i + 1) * tile
        used = []
        base = 0
        for k_ref, k_at in keys:
            have = k_ref.shape[0]
            take = min(have, upto - base)
            used.append((base, take))
            s = lax.dot_general(q, k_ref[:take, k_at], (((1,), (1,)), ((), ())), preferred_element_type=F32)
            ta = lax.broadcasted_iota(jnp.int32, s.shape, 0) + (start + i * tile)
            tb = lax.broadcasted_iota(jnp.int32, s.shape, 1) + base
            ok = (((ta ^ tb) & bits) == 0) & (tb <= ta)
            scores.append(jnp.where(ok, s * factor, -jnp.inf))
            base += have
        top = scores[0].max(axis=-1, keepdims=True)
        for s in scores[1:]:
            top = jnp.maximum(top, s.max(axis=-1, keepdims=True))
        expo = [jnp.exp2(s - top) for s in scores]
        total = sum(e.sum(axis=-1, keepdims=True) for e in expo)
        out = 0.0
        for e, (v_ref, v_at), (_, take) in zip(expo, vals, used):
            out = out + jnp.dot(e.astype(BF16), v_ref[:take, v_at], preferred_element_type=F32)
        out_ref[i * tile : (i + 1) * tile, out_at] = (out / total).astype(BF16)


def permute_kernel(samples_hbm, out_hbm, in_ref, out_ref, sems):
    cols, width = samples_hbm.shape[1:]
    step = cols // 4
    spans = [pl.ds(i * step, step) for i in range(4)]
    arriving = fetch([samples_hbm.at[:, at] for at in spans], [in_ref.at[:, at] for at in spans], sems.at[0])
    leaving = []
    for i, at in enumerate(spans):
        arriving[i].wait()
        halves = interleave(in_ref[0, at, :].astype(F32), in_ref[1, at, :].astype(F32))
        tiles = jnp.stack([t.reshape(step // 8, 8, width) for t in halves], axis=1)
        to = pl.ds(i * 2 * step, 2 * step)
        out_ref[to, :] = tiles.reshape(2 * step, width).astype(BF16)
        leaving += fetch([out_ref.at[to]], [out_hbm.at[to]], sems.at[1, i : i + 1])
    for copy in leaving:
        copy.wait()


def permute(samples):
    rows, cols, width = samples.shape
    out = sds((rows * cols, width))
    return pl.pallas_call(
        permute_kernel,
        out_shape=out,
        in_specs=[ANY],
        out_specs=ANY,
        scratch_shapes=[
            pltpu.VMEM(samples.shape, BF16),
            pltpu.VMEM(out.shape, BF16),
            pltpu.SemaphoreType.DMA((2, 4)),
        ],
        compiler_params=params(WHOLE),
        cost_estimate=cost(samples.size, [samples, out]),
    )(samples)


def norm_into(h, refs, gain_ref, normed_ref):
    tokens, width = refs[0].shape
    features = 4 * width
    tile = min(32, tokens)

    @pl.loop(0, tokens // tile, unroll=2)
    def _(i):
        at = pl.ds(pl.multiple_of(i * tile, tile), tile)
        total = sum(ref[at, :].astype(F32) for ref in refs)
        mean = jnp.sum(total, axis=-1, keepdims=True) * (1.0 / features)
        squares = 0.0
        for ref in refs:
            centred = ref[at, :].astype(F32) - mean
            squares = squares + centred * centred
        var = jnp.sum(squares, axis=-1, keepdims=True) * (1.0 / features)
        scale = lax.rsqrt(var + 1e-05)
        for ref, flip in zip(refs, (0, 2, 1, 3)):
            where = block(h ^ flip, width)
            rows = (ref[at, :].astype(F32) - mean) * scale * gain_ref[:, where]
            normed_ref[at, where] = rows.astype(BF16)


def project(normed_ref, w_ref, copies, qkv_ref):
    wide = w_ref.shape[2]
    for t in range(3):
        copies[t].wait()
        qkv_ref[:, t * wide : (t + 1) * wide] = jnp.dot(
            normed_ref[...], w_ref[t], preferred_element_type=F32
        ).astype(BF16)


def heads(qkv_ref, bits, attn_ref):
    wide = attn_ref.shape[1]
    for head in range(wide // HD):
        keys, vals = lanes(1, head, wide), lanes(2, head, wide)
        attend(qkv_ref, lanes(0, head, wide), [(qkv_ref, keys)], [(qkv_ref, vals)], 0, bits, attn_ref, lanes(0, head, wide))


def fetch_weights(gain_hbm, w_hbm, gain_ref, w_ref, sems):
    return fetch([gain_hbm] + [w_hbm.at[t] for t in range(3)], [gain_ref] + [w_ref.at[t] for t in range(3)], sems)


def attention(h, parts, copies, bits, attn_ref, gain_ref, w_ref, normed_ref, qkv_ref):
    copies[0].wait()
    norm_into(h, parts, gain_ref, normed_ref)
    project(normed_ref, w_ref, copies[1:], qkv_ref)
    heads(qkv_ref, bits, attn_ref)


def attention_scratch(gain, weights, tokens):
    _, features, wide = weights.shape
    return [
        pltpu.VMEM(gain.shape, F32),
        pltpu.VMEM(weights.shape, BF16),
        pltpu.VMEM((tokens, features), BF16),
        pltpu.VMEM((tokens, 3 * wide), BF16),
    ]


def col_kernel(h_ref, a, b, c, d, gain_hbm, w_hbm, attn_ref, gain_ref, w_ref, normed_ref, qkv_ref, sems):
    copies = fetch_weights(gain_hbm, w_hbm, gain_ref, w_ref, sems)
    attention(h_ref[0], (a, b, c, d), copies, OWNED - 1, attn_ref, gain_ref, w_ref, normed_ref, qkv_ref)


def row_kernel(row, n_more, h_ref, *refs):
    parts_hbm, more_hbm, (gain_hbm, w_hbm) = refs[:4], refs[4 : 4 + n_more], refs[4 + n_more : 6 + n_more]
    rest = refs[6 + n_more + n_more :] if n_more else refs[6:]
    n_out = 2 if n_more else 1
    outs_hbm = rest[:n_out]
    x_ref, held_ref, gain_ref, w_ref, normed_ref, qkv_ref, sems, more_sems = rest[n_out:]
    ready = fetch([p.at[row] for p in parts_hbm], [x_ref.at[i] for i in range(4)], sems)
    copies = fetch_weights(gain_hbm, w_hbm, gain_ref, w_ref, sems.at[4:])
    earlier = fetch(more_hbm, [held_ref.at[0]], more_sems)
    for copy in ready:
        copy.wait()
    parts = [x_ref.at[i] for i in range(4)]
    attention(h_ref[0], parts, copies, 0, held_ref.at[n_more], gain_ref, w_ref, normed_ref, qkv_ref)
    if n_more:
        earlier[0].wait()
        halves = interleave(held_ref[0].astype(F32), held_ref[1].astype(F32))
        for i, half in enumerate(halves):
            held_ref[i] = half.astype(BF16)
    for copy in fetch([held_ref.at[i] for i in range(n_out)], outs_hbm, more_sems):
        copy.wait()


def out_dot(row_ref, col_ref, wr_ref, wc_ref, where):
    return jnp.dot(row_ref[...], wr_ref[:, where], preferred_element_type=F32) + jnp.dot(
        col_ref[...], wc_ref[:, where], preferred_element_type=F32
    )


def out_core_kernel(h_ref, row_ref, col_ref, wr_ref, wc_ref, y3_ref, y1_ref):
    h = h_ref[0]
    width = y3_ref.shape[1]
    y3_ref[...] = out_dot(row_ref, col_ref, wr_ref, wc_ref, block(h ^ 3, width)).astype(BF16)
    y1_ref[...] = out_dot(row_ref, col_ref, wr_ref, wc_ref, block(h ^ 1, width)).astype(BF16)


def out_chip_kernel(h_ref, row_ref, col_ref, wr_ref, wc_ref, r2_ref, s2_ref):
    width = s2_ref.shape[1]
    own = out_dot(row_ref, col_ref, wr_ref, wc_ref, block(h_ref[0] ^ 2, width))
    s2_ref[...] = (own + r2_ref[...].astype(F32)).astype(BF16)


def out_own_kernel(h_ref, row_ref, col_ref, wr_ref, wc_ref, r0_ref, own_ref):
    width = own_ref.shape[1]
    own = out_dot(row_ref, col_ref, wr_ref, wc_ref, block(h_ref[0], width))
    own_ref[...] = own + r0_ref[...].astype(F32)


def final_kernel(samples_ref, own0_ref, rx0_ref, own1_ref, rx1_ref, out_ref):
    cols = samples_ref.shape[1]
    step = min(64, cols)

    @pl.loop(0, cols // step)
    def _(i):
        at = pl.ds(pl.multiple_of(i * step, step), step)
        pair = deinterleave(
            own0_ref[at, :] + rx0_ref[at, :].astype(F32), own1_ref[at, :] + rx1_ref[at, :].astype(F32)
        )
        for r in range(2):
            out_ref[r, at, :] = (samples_ref[r, at, :].astype(F32) + pair[r]).astype(BF16)


def shards(samples, norm_gain, row_qkv, col_qkv, row_out, col_out):
    rows, cols, width = samples.shape
    assert rows == 2
    wide = col_qkv.shape[2]
    features = 4 * width
    tokens = cols
    h = lax.axis_index("head").astype(jnp.int32).reshape(1)
    gain = norm_gain.reshape(1, features)
    dma = pltpu.SemaphoreType.DMA

    def over_chip(x):
        return lax.ppermute(x, "head", [(i, i ^ 2) for i in range(4)])

    def over_core(x):
        return lax.ppermute(x, "head", [(i, i ^ 1) for i in range(4)])

    def exchange(x):
        return lax.all_to_all(x, "row", 0, 0, tiled=True)

    def gather(a):
        b = over_chip(a)
        return a, b, over_core(a), over_core(b)

    flops = 2 * tokens * features * 3 * wide + 4 * tokens * tokens * wide

    def cols(parts, after):
        return call(
            col_kernel,
            (h,),
            parts,
            (gain, col_qkv),
            (sds((tokens, wide)),),
            flops,
            attention_scratch(gain, col_qkv, tokens) + [dma((4,))],
            after,
        )[0]

    def row(r, parts, more, after):
        outs = tuple([sds((tokens, wide))] * (1 + len(more)))
        return pl.pallas_call(
            functools.partial(row_kernel, r, len(more)),
            out_shape=outs,
            in_specs=[SM] + [ANY] * (6 + len(more) + len(after)),
            out_specs=tuple([ANY] * len(outs)),
            scratch_shapes=[pltpu.VMEM((4, tokens, width), BF16), pltpu.VMEM((2, tokens, wide), BF16)]
            + attention_scratch(gain, row_qkv, tokens)
            + [dma((8,)), dma((2,))],
            compiler_params=params(WHOLE),
            cost_estimate=cost(flops, parts, 4),
        )(h, *parts, *more, gain, row_qkv, *after)

    piece = 4 * tokens * wide * width

    def out(row_attn, col_attn, after, after_chip):
        ops = (row_attn, col_attn, row_out, col_out)
        y3, y1 = call(out_core_kernel, (h,), ops, (), (sds((tokens, width)),) * 2, 2 * piece, (), after)
        (s2,) = call(out_chip_kernel, (h,), ops + (over_core(y3),), (), (sds((tokens, width)),), piece, (), after_chip)

        def own(after):
            more = ops + (over_core(y1),)
            return call(out_own_kernel, (h,), more, (), (sds((tokens, width), F32),), piece, (), after)[0]

        return own, s2, over_chip(s2)

    every = gather(samples)
    mine = exchange(permute(samples)).reshape(-1, 2, 2 * OWNED, width)
    (row0,) = row(0, every, (), ())
    mine, row0 = lax.optimization_barrier((mine, row0))
    start0 = mine[:, 0].reshape(tokens, width)
    chip0 = over_chip(start0)
    mine, _ = lax.optimization_barrier((mine, chip0))
    start1 = mine[:, 1].reshape(tokens, width)
    chip1 = over_chip(start1)
    rows0, rows1 = row(1, every, (row0,), (row0,))
    chip0, rows0 = lax.optimization_barrier((chip0, rows0))
    parts0 = (start0, chip0, over_core(start0), over_core(chip0))
    attn0 = cols(parts0, (rows0,))
    back0 = exchange(attn0)
    start1, chip1, _ = lax.optimization_barrier((start1, chip1, attn0))
    attn1 = cols((start1, chip1, over_core(start1), over_core(chip1)), (attn0,))
    back1 = exchange(attn1)
    own0, s0, rx0 = out(rows0, back0, (attn1,), ())
    own1, s1, rx1 = out(rows1, back1, (s0,), (rx0,))
    own0 = own0((s1,))
    own1 = own1((own0,))
    return call(final_kernel, (), (samples, own0, rx0, own1, rx1), (), (sds(samples.shape),), samples.size)[0]


def solution(mesh):
    placed = (
        P("row", None, "head"),
        P(),
        P(None, None, "head"),
        P(None, None, "head"),
        P("head", None),
        P("head", None),
    )
    return jax.shard_map(
        shards, mesh=mesh, in_specs=placed, out_specs=P("row", None, "head"), check_vma=False
    )
```

time: 181 us -> 152 us (0.84)
  waiting for transfers between devices: 82 us -> 39.2 us
  Pallas kernels: 29.6 us -> 45.8 us
  local copies, waits for them, and re-layouts: 12.7 us -> 5.78 us
  starting transfers between devices: 55.3 us -> 59.6 us
    ppermute x4 -> x5, waiting for transfers between devices: 49.7 us -> 25 us  [over_chip(): return lax.ppermute(x, 'head', [(i, i ^ 2) for i in range(4)])]
    all_to_all x4 -> x3, waiting for transfers between devices: 28.8 us -> 10.5 us  [exchange(): return lax.all_to_all(x, 'row', 0, 0, tiled=True)]
    pallas_call x13 -> x12, Pallas kernels: 29.6 us -> 45.8 us  [the longest x9 25.4 us: call(): pl.pallas_call(kernel, out_shape=tuple(outs), in_specs=[SM] * len(scalars...]
    ppermute x8 -> x10, starting transfers between devices: 8.85 us -> 19.4 us  [over_core(): return lax.ppermute(x, 'head', [(i, i ^ 1) for i in range(4)])]
    unnamed x28 -> x26, local copies, waits for them, and re-layouts: 11.5 us -> 5.71 us
    all_to_all x4 -> x3, starting transfers between devices: 42.3 us -> 36.7 us  [exchange(): return lax.all_to_all(x, 'row', 0, 0, tiled=True)]
    ppermute x4 -> x5, starting transfers between devices: 4.17 us -> 3.43 us  [over_chip(): return lax.ppermute(x, 'head', [(i, i ^ 2) for i in range(4)])]
    ppermute x8 -> x10, waiting for transfers between devices: 3.54 us -> 3.64 us  [over_core(): return lax.ppermute(x, 'head', [(i, i ^ 1) for i in range(4)])]
  transfers between devices with their start and end apart: 16 -> 18, of which waited for: 9 -> 10; matrix products, arithmetic and copies ran while one was open for 0% -> 0% of each run, Pallas kernels for 13% -> 28%
where the time goes in v2:
time: 152 us; the launch traced here: 151 us
  starting transfers between devices  59.6 us (39%)
  Pallas kernels  45.8 us (30%)
  waiting for transfers between devices  39.2 us (26%)
  local copies, waits for them, and re-layouts  5.78 us (4%)
    all_to_all x3, starting transfers between devices, exchange(): return lax.all_to_all(x, 'row', 0, 0, tiled=True)  36.7 us
    pallas_call x9, Pallas kernels, call(): pl.pallas_call(kernel, out_shape=tuple(outs), in_specs=[SM] * len(scalars...  25.4 us
    ppermute x5, waiting for transfers between devices, over_chip(): return lax.ppermute(x, 'head', [(i, i ^ 2) for i in range(4)])  25 us
    ppermute x10, starting transfers between devices, over_core(): return lax.ppermute(x, 'head', [(i, i ^ 1) for i in range(4)])  19.4 us
    pallas_call x2, Pallas kernels, row(): pl.pallas_call(functools.partial(row_kernel, r, len(more)), out_shape=out...  18.4 us
    all_to_all x3, waiting for transfers between devices, exchange(): return lax.all_to_all(x, 'row', 0, 0, tiled=True)  10.5 us
    unnamed x26, local copies, waits for them, and re-layouts  5.71 us
    ppermute x10, waiting for transfers between devices, over_core(): return lax.ppermute(x, 'head', [(i, i ^ 1) for i in range(4)])  3.64 us
  transfers between devices with their start and end apart: 18, of which 10 were waited for; matrix products, arithmetic and copies ran while one was open for 0% of the time, Pallas kernels for 28%

profile of v2, /device:TPU:1, one launch (start us, length us, event | category | flops | bytes accessed | tf_op | source)
XLA Modules:
  0.0 150.7 jit_solution(8672329576602996621)
XLA Ops:
  0.0 2.0 %collective-permute-start = (bf16[2,512,512]{2,1,0:T(8,128)(2,1)}, bf16[2,512,512]{2,1,0:T(8,128)(2,1)S(1)}, u32[]{:S(2)}, u32[]{:S(2)}) collective-permute-start(bf16[2,512,512]{2,1,0:T(8,128)(2,1)} %refs_0_.5), channel_id=1, source_target_pairs={{0,2},{1,3},{2,0},{3,1},{4,6},{5,7},{6,4},{7,5},{8,10},{9,11},{10,... | collective-permute-start | bytes 3145736 | tf_op jit(solution)/shard_map/ppermute | solution.py:288
  2.0 2.1 %shard_map.64 = bf16[1024,512]{1,0:T(8,128)(2,1)} custom-call(bf16[2,512,512]{2,1,0:T(8,128)(2,1)} %refs_0_.5), custom_call_target="tpu_custom_call" | custom-call | flops 524288 | bytes 2097152 | tf_op jit(solution)/shard_map/pallas_call | solution.py:137
  4.2 14.0 %all-to-all-start = ((bf16[64,16,512]{2,1,0:T(8,128)(2,1)}), bf16[64,16,512]{2,1,0:T(8,128)(2,1)S(1)}, u32[]{:S(2)}, u32[]{:S(2)}) async-start(bf16[64,16,512]{2,1,0:T(8,128)(2,1)} %bitcast.24), calls=%async_computation | async-start | bytes 2097152 | tf_op jit(solution)/shard_map/all_to_all | solution.py:294
  18.2 0.0 copy-done.2
  18.2 1.3 collective-permute-start.1
  19.5 6.7 %collective-permute-done.refs_1_ = bf16[2,512,512]{2,1,0:T(8,128)(2,1)S(1)} collective-permute-done((bf16[2,512,512]{2,1,0:T(8,128)(2,1)}, bf16[2,512,512]{2,1,0:T(8,128)(2,1)S(1)}, u32[]{:S(2)}, u32[]{:S(2)}) %collective-permute-start) | collective-permute-done | bytes 1048608 | tf_op jit(solution)/shard_map/ppermute | solution.py:288
  26.2 6.4 %collective-permute-start.2 = (bf16[2,512,512]{2,1,0:T(8,128)(2,1)S(1)}, bf16[2,512,512]{2,1,0:T(8,128)(2,1)}, u32[]{:S(2)}, u32[]{:S(2)}) collective-permute-start(bf16[2,512,512]{2,1,0:T(8,128)(2,1)S(1)} %collective-permute-done.refs_1_), channel_id=1, source_target_pairs={{0,1},{1,0},{2,3},{3,2},{4,5},{5,4},{6,7},{7,6},{8,9},{9,8},{10,11... | collective-permute-start | bytes 3145736 | tf_op jit(solution)/shard_map/ppermute | solution.py:291
  32.6 0.0 collective-permute-done.1.refs_2_
  32.6 2.4 %collective-permute-done.2.refs_3_ = bf16[2,512,512]{2,1,0:T(8,128)(2,1)} collective-permute-done((bf16[2,512,512]{2,1,0:T(8,128)(2,1)S(1)}, bf16[2,512,512]{2,1,0:T(8,128)(2,1)}, u32[]{:S(2)}, u32[]{:S(2)}) %collective-permute-start.2) | collective-permute-done | bytes 1048608 | tf_op jit(solution)/shard_map/ppermute | solution.py:291
  35.0 0.0 copy-done.12
  35.0 9.1 %shard_map.65.refs_4_.refs_7_ = bf16[512,256]{1,0:T(8,128)(2,1)} custom-call(s32[1]{0:T(128)} %bitcast.h_ref.refs_0_, bf16[2,512,512]{2,1,0:T(8,128)(2,1)} %refs_0_.5, bf16[2,512,512]{2,1,0:T(8,128)(2,1)} %copy-done.12, bf16[2,512,512]{2,1,0:T(8,128)(2,1)} %collective-permute-done.1.refs_2_, bf16[2,512,512]{2,1,0:T(8,128)(2,1)} %collective-permute-done.2.refs_3_, ...), custom_call_target="tpu_custom_call" | custom-call | flops 7516192768 | bytes 16777216 | tf_op jit(solution)/shard_map/pallas_call | solution.py:316
  44.1 0.1 all-to-all-done
  44.2 0.0 copy-start.11
  44.2 4.2 %collective-permute-start.4 = (bf16[512,512]{1,0:T(8,128)(2,1)S(1)}, bf16[512,512]{1,0:T(8,128)(2,1)S(1)}, u32[]{:S(2)}, u32[]{:S(2)}) collective-permute-start(bf16[512,512]{1,0:T(8,128)(2,1)S(1)} %slice_bitcast_fusion.1.refs_1_), channel_id=1, source_target_pairs={{0,1},{1,0},{2,3},{3,2},{4,5},{5,4},{6,7},{7,6},{8,9},{9,8},{10,11... | collective-permute-start | bytes 1572872 | tf_op jit(solution)/shard_map/ppermute | solution.py:291
  48.4 0.0 collective-permute-start.3
  48.4 9.3 %shard_map.66 = (bf16[512,256]{1,0:T(8,128)(2,1)}, bf16[512,256]{1,0:T(8,128)(2,1)}) custom-call(s32[1]{0:T(128)} %bitcast.h_ref.refs_0_, bf16[2,512,512]{2,1,0:T(8,128)(2,1)} %refs_0_.5, bf16[2,512,512]{2,1,0:T(8,128)(2,1)} %copy-done.12, bf16[2,512,512]{2,1,0:T(8,128)(2,1)} %collective-permute-done.1.refs_2_, ...), custom_call_target="tpu_custom_call" | custom-call | flops 7516192768 | bytes 16777216 | tf_op jit(solution)/shard_map/pallas_call | solution.py:316
  57.7 4.2 %collective-permute-done.3.refs_2_ = bf16[512,512]{1,0:T(8,128)(2,1)S(1)} collective-permute-done((bf16[512,512]{1,0:T(8,128)(2,1)S(1)}, bf16[512,512]{1,0:T(8,128)(2,1)S(1)}, u32[]{:S(2)}, u32[]{:S(2)}) %collective-permute-start.3) | collective-permute-done | bytes 524320 | tf_op jit(solution)/shard_map/ppermute | solution.py:288
  61.9 0.9 collective-permute-start.5
  62.8 0.3 collective-permute-start.6
  63.0 0.0 collective-permute-done.4.refs_3_
  63.1 1.2 collective-permute-done.5.refs_4_
  64.3 0.0 copy-done.11
  64.3 0.9 copy-done.4
  65.2 1.9 %copy-done.7 = bf16[3,2048,256]{2,1,0:T(8,128)(2,1)S(1)} copy-done((bf16[3,2048,256]{2,1,0:T(8,128)(2,1)S(1)}, bf16[3,2048,256]{2,1,0:T(8,128)(2,1)}, u32[]{:S(2)}) %copy-start.7) | copy-done | bytes 3145752
  67.1 7.9 %shard_map.67.refs_7_ = bf16[512,256]{1,0:T(8,128)(2,1)} custom-call(s32[1]{0:T(128)} %bitcast.h_ref.refs_0_, bf16[512,512]{1,0:T(8,128)(2,1)S(1)} %slice_bitcast_fusion.1.refs_1_, bf16[512,512]{1,0:T(8,128)(2,1)S(1)} %collective-permute-done.3.refs_2_, bf16[512,512]{1,0:T(8,128)(2,1)S(1)} %collective-permute-done.4.refs_3_, ...), custom_call_target="tpu_custom_call" | custom-call | flops 1879048192 | bytes 5513216 | tf_op jit(solution)/shard_map/pallas_call | solution.py:38
  75.0 1.7 %collective-permute-done.6.refs_2_ = bf16[512,512]{1,0:T(8,128)(2,1)} collective-permute-done((bf16[512,512]{1,0:T(8,128)(2,1)S(1)}, bf16[512,512]{1,0:T(8,128)(2,1)}, u32[]{:S(2)}, u32[]{:S(2)}) %collective-permute-start.6) | collective-permute-done | bytes 524320 | tf_op jit(solution)/shard_map/ppermute | solution.py:288
  76.7 0.8 collective-permute-start.7
  77.5 0.0 collective-permute-start.8
  77.5 13.2 %all-to-all-start.1 = ((bf16[64,8,256]{2,1,0:T(8,128)(2,1)}), bf16[64,8,256]{2,1,0:T(8,128)(2,1)S(1)}, u32[]{:S(2)}, u32[]{:S(2)}) async-start(bf16[64,8,256]{2,1,0:T(8,128)(2,1)} %bitcast.5), calls=%async_computation.1 | async-start | bytes 524288 | tf_op jit(solution)/shard_map/all_to_all | solution.py:294
  90.7 0.0 copy-start
  90.7 0.0 copy-start.1
  90.7 0.0 copy-start.5
  90.7 0.0 collective-permute-done.7.refs_3_
  90.7 0.0 collective-permute-done.8.refs_4_
  90.7 0.0 copy-start.8
  90.7 2.0 %copy-done.8 = bf16[3,2048,256]{2,1,0:T(8,128)(2,1)S(1)} copy-done((bf16[3,2048,256]{2,1,0:T(8,128)(2,1)S(1)}, bf16[3,2048,256]{2,1,0:T(8,128)(2,1)}, u32[]{:S(2)}) %copy-start.8) | copy-done | bytes 3145752
  92.8 9.3 %shard_map.68.refs_5_ = bf16[512,256]{1,0:T(8,128)(2,1)} custom-call(s32[1]{0:T(128)} %bitcast.h_ref.refs_0_, bf16[512,512]{1,0:T(8,128)(2,1)S(1)} %slice_bitcast_fusion.refs_1_, bf16[512,512]{1,0:T(8,128)(2,1)} %collective-permute-done.6.refs_2_, bf16[512,512]{1,0:T(8,128)(2,1)} %collective-permute-done.7.refs_3_, ...), custom_call_target="tpu_custom_call" | custom-call | flops 1879048192 | bytes 5513216 | tf_op jit(solution)/shard_map/pallas_call | solution.py:38
  102.0 0.5 all-to-all-done.1
  102.5 0.0 copy-done
  102.5 0.0 copy-done.1
  102.5 0.0 copy-start.6
  102.6 1.4 shard_map.69
  103.9 0.8 copy-done.9
  104.7 3.2 %collective-permute-start.10 = (bf16[512,512]{1,0:T(8,128)(2,1)}, bf16[512,512]{1,0:T(8,128)(2,1)}, u32[]{:S(2)}, u32[]{:S(2)}) collective-permute-start(bf16[512,512]{1,0:T(8,128)(2,1)} %get-tuple-element.28), channel_id=1, source_target_pairs={{0,1},{1,0},{2,3},{3,2},{4,5},{5,4},{6,7},{7,6},{8,9},{9,8},{10,11... | collective-permute-start | bytes 1572872 | tf_op jit(solution)/shard_map/ppermute | solution.py:291
  107.9 9.5 %all-to-all-start.2 = ((bf16[64,8,256]{2,1,0:T(8,128)(2,1)}), bf16[64,8,256]{2,1,0:T(8,128)(2,1)S(1)}, u32[]{:S(2)}, u32[]{:S(2)}) async-start(bf16[64,8,256]{2,1,0:T(8,128)(2,1)} %bitcast.8), calls=%async_computation.2 | async-start | bytes 524288 | tf_op jit(solution)/shard_map/all_to_all | solution.py:294
  117.5 0.0 collective-permute-done.10.refs_5_
  117.5 2.3 %shard_map.70.refs_5_ = bf16[512,512]{1,0:T(8,128)(2,1)} custom-call(s32[1]{0:T(128)} %bitcast.h_ref.refs_0_, bf16[512,256]{1,0:T(8,128)(2,1)S(1)} %copy-done.5, bf16[512,256]{1,0:T(8,128)(2,1)S(1)} %bitcast.13, bf16[256,2048]{1,0:T(8,128)(2,1)S(1)} %copy-done, bf16[256,2048]{1,0:T(8,128)(2,1)S(1)} %copy-done.1, bf16[512,512]{1,0:T(8,128)(2,1)} %collective-permute-done.10.refs_5_), custom_call_target="tpu_custom_call" | custom-call | flops 268435456 | bytes 3670016 | tf_op jit(solution)/shard_map/pallas_call | solution.py:38
  119.8 0.3 collective-permute-start.12
  120.1 10.0 %all-to-all-done.2 = bf16[64,8,256]{2,1,0:T(8,128)(2,1)S(1)} async-done(((bf16[64,8,256]{2,1,0:T(8,128)(2,1)}), bf16[64,8,256]{2,1,0:T(8,128)(2,1)S(1)}, u32[]{:S(2)}, u32[]{:S(2)}) %all-to-all-start.2) | async-done | bytes 262176 | tf_op jit(solution)/shard_map/all_to_all | solution.py:294
  130.1 0.7 shard_map.71
  130.8 2.2 %collective-permute-start.11 = (bf16[512,512]{1,0:T(8,128)(2,1)S(1)}, bf16[512,512]{1,0:T(8,128)(2,1)S(1)}, u32[]{:S(2)}, u32[]{:S(2)}) collective-permute-start(bf16[512,512]{1,0:T(8,128)(2,1)S(1)} %get-tuple-element.29), channel_id=1, source_target_pairs={{0,1},{1,0},{2,3},{3,2},{4,5},{5,4},{6,7},{7,6},{8,9},{9,8},{10,11... | collective-permute-start | bytes 1572872 | tf_op jit(solution)/shard_map/ppermute | solution.py:291
  133.0 0.1 collective-permute-start.9
  133.1 0.4 collective-permute-start.13
  133.5 1.5 %collective-permute-done.12.refs_6_.refs_2_ = bf16[512,512]{1,0:T(8,128)(2,1)} collective-permute-done((bf16[512,512]{1,0:T(8,128)(2,1)}, bf16[512,512]{1,0:T(8,128)(2,1)}, u32[]{:S(2)}, u32[]{:S(2)}) %collective-permute-start.12) | collective-permute-done | bytes 524320 | tf_op jit(solution)/shard_map/ppermute | solution.py:288
  135.0 0.0 collective-permute-done.11.refs_5_
  135.1 0.4 shard_map.72.refs_6_
  135.5 0.8 collective-permute-start.14
  136.3 0.0 collective-permute-done.9.refs_5_
  136.3 0.4 shard_map.73.refs_6_.refs_1_
  136.7 0.0 copy-start.3
  136.8 0.0 collective-permute-done.13.refs_5_
  136.8 0.4 shard_map.74.refs_3_
  137.2 10.9 %collective-permute-done.14.refs_4_ = bf16[512,512]{1,0:T(8,128)(2,1)S(1)} collective-permute-done((bf16[512,512]{1,0:T(8,128)(2,1)S(1)}, bf16[512,512]{1,0:T(8,128)(2,1)S(1)}, u32[]{:S(2)}, u32[]{:S(2)}) %collective-permute-start.14) | collective-permute-done | bytes 524320 | tf_op jit(solution)/shard_map/ppermute | solution.py:288
  148.2 2.5 %shard_map.75 = bf16[2,512,512]{2,1,0:T(8,128)(2,1)} custom-call(bf16[2,512,512]{2,1,0:T(8,128)(2,1)S(1)} %copy-done.3, f32[512,512]{1,0:T(8,128)S(1)} %shard_map.73.refs_6_.refs_1_, bf16[512,512]{1,0:T(8,128)(2,1)} %collective-permute-done.12.refs_6_.refs_2_, f32[512,512]{1,0:T(8,128)S(1)} %shard_map.74.refs_3_, ...), custom_call_target="tpu_custom_call" | custom-call | flops 524288 | bytes 5242880 | tf_op jit(solution)/shard_map/pallas_call | solution.py:38
  (12 shorter events, 0.1 us)
Async XLA Ops:
  0.0 18.2 %copy-start.2 = (bf16[2,512,512]{2,1,0:T(8,128)(2,1)S(1)}, bf16[2,512,512]{2,1,0:T(8,128)(2,1)}, u32[]{:S(2)}) copy-start(bf16[2,512,512]{2,1,0:T(8,128)(2,1)} %refs_0_.5) | copy-start | bytes 3145732
  0.0 26.2 %collective-permute-start = (bf16[2,512,512]{2,1,0:T(8,128)(2,1)}, bf16[2,512,512]{2,1,0:T(8,128)(2,1)S(1)}, u32[]{:S(2)}, u32[]{:S(2)}) collective-permute-start(bf16[2,512,512]{2,1,0:T(8,128)(2,1)} %refs_0_.5), channel_id=1, source_target_pairs={{0,2},{1,3},{2,0},{3,1},{4,6},{5,7},{6,4},{7,5},{8,10},{9,11},{10,... | collective-permute-start | bytes 3145736 | tf_op jit(solution)/shard_map/ppermute | solution.py:288
  4.2 40.0 %all-to-all-start = ((bf16[64,16,512]{2,1,0:T(8,128)(2,1)}), bf16[64,16,512]{2,1,0:T(8,128)(2,1)S(1)}, u32[]{:S(2)}, u32[]{:S(2)}) async-start(bf16[64,16,512]{2,1,0:T(8,128)(2,1)} %bitcast.24), calls=%async_computation | async-start | bytes 2097152 | tf_op jit(solution)/shard_map/all_to_all | solution.py:294
  18.2 14.4 %collective-permute-start.1 = (bf16[2,512,512]{2,1,0:T(8,128)(2,1)S(1)}, bf16[2,512,512]{2,1,0:T(8,128)(2,1)}, u32[]{:S(2)}, u32[]{:S(2)}) collective-permute-start(bf16[2,512,512]{2,1,0:T(8,128)(2,1)S(1)} %copy-done.2), channel_id=1, source_target_pairs={{0,1},{1,0},{2,3},{3,2},{4,5},{5,4},{6,7},{7,6},{8,9},{9,8},{10,11... | collective-permute-start | bytes 3145736 | tf_op jit(solution)/shard_map/ppermute | solution.py:291
  26.2 8.8 %copy-start.12 = (bf16[2,512,512]{2,1,0:T(8,128)(2,1)}, bf16[2,512,512]{2,1,0:T(8,128)(2,1)S(1)}, u32[]{:S(2)}) copy-start(bf16[2,512,512]{2,1,0:T(8,128)(2,1)S(1)} %collective-permute-done.refs_1_) | copy-start | bytes 3145732
  26.2 8.8 %collective-permute-start.2 = (bf16[2,512,512]{2,1,0:T(8,128)(2,1)S(1)}, bf16[2,512,512]{2,1,0:T(8,128)(2,1)}, u32[]{:S(2)}, u32[]{:S(2)}) collective-permute-start(bf16[2,512,512]{2,1,0:T(8,128)(2,1)S(1)} %collective-permute-done.refs_1_), channel_id=1, source_target_pairs={{0,1},{1,0},{2,3},{3,2},{4,5},{5,4},{6,7},{7,6},{8,9},{9,8},{10,11... | collective-permute-start | bytes 3145736 | tf_op jit(solution)/shard_map/ppermute | solution.py:291
  44.2 20.1 %copy-start.11 = (f32[2048]{0:T(1024)S(1)}, f32[2048]{0:T(1024)}, u32[]{:S(2)}) copy-start(f32[2048]{0:T(1024)} %param.7) | copy-start | bytes 24580
  44.2 18.9 %collective-permute-start.4 = (bf16[512,512]{1,0:T(8,128)(2,1)S(1)}, bf16[512,512]{1,0:T(8,128)(2,1)S(1)}, u32[]{:S(2)}, u32[]{:S(2)}) collective-permute-start(bf16[512,512]{1,0:T(8,128)(2,1)S(1)} %slice_bitcast_fusion.1.refs_1_), channel_id=1, source_target_pairs={{0,1},{1,0},{2,3},{3,2},{4,5},{5,4},{6,7},{7,6},{8,9},{9,8},{10,11... | collective-permute-start | bytes 1572872 | tf_op jit(solution)/shard_map/ppermute | solution.py:291
  48.4 13.5 %collective-permute-start.3 = (bf16[512,512]{1,0:T(8,128)(2,1)S(1)}, bf16[512,512]{1,0:T(8,128)(2,1)S(1)}, u32[]{:S(2)}, u32[]{:S(2)}) collective-permute-start(bf16[512,512]{1,0:T(8,128)(2,1)S(1)} %slice_bitcast_fusion.1.refs_1_), channel_id=1, source_target_pairs={{0,2},{1,3},{2,0},{3,1},{4,6},{5,7},{6,4},{7,5},{8,10},{9,11},{10,... | collective-permute-start | bytes 1572872 | tf_op jit(solution)/shard_map/ppermute | solution.py:288
  61.9 2.4 %collective-permute-start.5 = (bf16[512,512]{1,0:T(8,128)(2,1)S(1)}, bf16[512,512]{1,0:T(8,128)(2,1)S(1)}, u32[]{:S(2)}, u32[]{:S(2)}) collective-permute-start(bf16[512,512]{1,0:T(8,128)(2,1)S(1)} %collective-permute-done.3.refs_2_), channel_id=1, source_target_pairs={{0,1},{1,0},{2,3},{3,2},{4,5},{5,4},{6,7},{7,6},{8,9},{9,8},{10,11... | collective-permute-start | bytes 1572872 | tf_op jit(solution)/shard_map/ppermute | solution.py:291
  62.8 13.9 %collective-permute-start.6 = (bf16[512,512]{1,0:T(8,128)(2,1)S(1)}, bf16[512,512]{1,0:T(8,128)(2,1)}, u32[]{:S(2)}, u32[]{:S(2)}) collective-permute-start(bf16[512,512]{1,0:T(8,128)(2,1)S(1)} %slice_bitcast_fusion.refs_1_), channel_id=1, source_target_pairs={{0,2},{1,3},{2,0},{3,1},{4,6},{5,7},{6,4},{7,5},{8,10},{9,11},{10,... | collective-permute-start | bytes 1572872 | tf_op jit(solution)/shard_map/ppermute | solution.py:288
  64.3 1.0 copy-start.4
  65.2 1.9 %copy-start.7 = (bf16[3,2048,256]{2,1,0:T(8,128)(2,1)S(1)}, bf16[3,2048,256]{2,1,0:T(8,128)(2,1)}, u32[]{:S(2)}) copy-start(bf16[3,2048,256]{2,1,0:T(8,128)(2,1)} %refs_6_.5) | copy-start | bytes 9437188
  76.7 14.0 %collective-permute-start.7 = (bf16[512,512]{1,0:T(8,128)(2,1)S(1)}, bf16[512,512]{1,0:T(8,128)(2,1)}, u32[]{:S(2)}, u32[]{:S(2)}) collective-permute-start(bf16[512,512]{1,0:T(8,128)(2,1)S(1)} %slice_bitcast_fusion.refs_1_), channel_id=1, source_target_pairs={{0,1},{1,0},{2,3},{3,2},{4,5},{5,4},{6,7},{7,6},{8,9},{9,8},{10,11... | collective-permute-start | bytes 1572872 | tf_op jit(solution)/shard_map/ppermute | solution.py:291
  77.5 13.2 %collective-permute-start.8 = (bf16[512,512]{1,0:T(8,128)(2,1)}, bf16[512,512]{1,0:T(8,128)(2,1)}, u32[]{:S(2)}, u32[]{:S(2)}) collective-permute-start(bf16[512,512]{1,0:T(8,128)(2,1)} %collective-permute-done.6.refs_2_), channel_id=1, source_target_pairs={{0,1},{1,0},{2,3},{3,2},{4,5},{5,4},{6,7},{7,6},{8,9},{9,8},{10,11... | collective-permute-start | bytes 1572872 | tf_op jit(solution)/shard_map/ppermute | solution.py:291
  77.5 25.1 %all-to-all-start.1 = ((bf16[64,8,256]{2,1,0:T(8,128)(2,1)}), bf16[64,8,256]{2,1,0:T(8,128)(2,1)S(1)}, u32[]{:S(2)}, u32[]{:S(2)}) async-start(bf16[64,8,256]{2,1,0:T(8,128)(2,1)} %bitcast.5), calls=%async_computation.1 | async-start | bytes 524288 | tf_op jit(solution)/shard_map/all_to_all | solution.py:294
  90.7 11.9 %copy-start = (bf16[256,2048]{1,0:T(8,128)(2,1)S(1)}, bf16[256,2048]{1,0:T(8,128)(2,1)}, u32[]{:S(2)}) copy-start(bf16[256,2048]{1,0:T(8,128)(2,1)} %refs_3_.11) | copy-start | bytes 3145732
  90.7 11.9 %copy-start.1 = (bf16[256,2048]{1,0:T(8,128)(2,1)S(1)}, bf16[256,2048]{1,0:T(8,128)(2,1)}, u32[]{:S(2)}) copy-start(bf16[256,2048]{1,0:T(8,128)(2,1)} %refs_4_.11) | copy-start | bytes 3145732
  90.7 11.9 %copy-start.5 = (bf16[512,256]{1,0:T(8,128)(2,1)S(1)}, bf16[512,256]{1,0:T(8,128)(2,1)}, u32[]{:S(2)}) copy-start(bf16[512,256]{1,0:T(8,128)(2,1)} %get-tuple-element.21.refs_7_.refs_1_) | copy-start | bytes 786436
  90.7 2.0 %copy-start.8 = (bf16[3,2048,256]{2,1,0:T(8,128)(2,1)S(1)}, bf16[3,2048,256]{2,1,0:T(8,128)(2,1)}, u32[]{:S(2)}) copy-start(bf16[3,2048,256]{2,1,0:T(8,128)(2,1)} %refs_6_.5) | copy-start | bytes 9437188
  102.5 27.5 %copy-start.6 = (bf16[512,256]{1,0:T(8,128)(2,1)S(1)}, bf16[512,256]{1,0:T(8,128)(2,1)}, u32[]{:S(2)}) copy-start(bf16[512,256]{1,0:T(8,128)(2,1)} %get-tuple-element.27.refs_1_) | copy-start | bytes 786436
  103.9 0.8 copy-start.9
  104.7 12.8 %collective-permute-start.10 = (bf16[512,512]{1,0:T(8,128)(2,1)}, bf16[512,512]{1,0:T(8,128)(2,1)}, u32[]{:S(2)}, u32[]{:S(2)}) collective-permute-start(bf16[512,512]{1,0:T(8,128)(2,1)} %get-tuple-element.28), channel_id=1, source_target_pairs={{0,1},{1,0},{2,3},{3,2},{4,5},{5,4},{6,7},{7,6},{8,9},{9,8},{10,11... | collective-permute-start | bytes 1572872 | tf_op jit(solution)/shard_map/ppermute | solution.py:291
  107.9 22.1 %all-to-all-start.2 = ((bf16[64,8,256]{2,1,0:T(8,128)(2,1)}), bf16[64,8,256]{2,1,0:T(8,128)(2,1)S(1)}, u32[]{:S(2)}, u32[]{:S(2)}) async-start(bf16[64,8,256]{2,1,0:T(8,128)(2,1)} %bitcast.8), calls=%async_computation.2 | async-start | bytes 524288 | tf_op jit(solution)/shard_map/all_to_all | solution.py:294
  119.8 15.3 %collective-permute-start.12 = (bf16[512,512]{1,0:T(8,128)(2,1)}, bf16[512,512]{1,0:T(8,128)(2,1)}, u32[]{:S(2)}, u32[]{:S(2)}) collective-permute-start(bf16[512,512]{1,0:T(8,128)(2,1)} %shard_map.70.refs_5_), channel_id=1, source_target_pairs={{0,2},{1,3},{2,0},{3,1},{4,6},{5,7},{6,4},{7,5},{8,10},{9,11},{10,... | collective-permute-start | bytes 1572872 | tf_op jit(solution)/shard_map/ppermute | solution.py:288
  130.1 2.9 %copy-start.10 = (bf16[512,512]{1,0:T(8,128)(2,1)S(1)}, bf16[512,512]{1,0:T(8,128)(2,1)}, u32[]{:S(2)}) copy-start(bf16[512,512]{1,0:T(8,128)(2,1)} %copy-done.9) | copy-start | bytes 1572868
  130.8 4.3 %collective-permute-start.11 = (bf16[512,512]{1,0:T(8,128)(2,1)S(1)}, bf16[512,512]{1,0:T(8,128)(2,1)S(1)}, u32[]{:S(2)}, u32[]{:S(2)}) collective-permute-start(bf16[512,512]{1,0:T(8,128)(2,1)S(1)} %get-tuple-element.29), channel_id=1, source_target_pairs={{0,1},{1,0},{2,3},{3,2},{4,5},{5,4},{6,7},{7,6},{8,9},{9,8},{10,11... | collective-permute-start | bytes 1572872 | tf_op jit(solution)/shard_map/ppermute | solution.py:291
  133.0 3.3 %collective-permute-start.9 = (bf16[512,512]{1,0:T(8,128)(2,1)S(1)}, bf16[512,512]{1,0:T(8,128)(2,1)S(1)}, u32[]{:S(2)}, u32[]{:S(2)}) collective-permute-start(bf16[512,512]{1,0:T(8,128)(2,1)S(1)} %copy-done.10), channel_id=1, source_target_pairs={{0,1},{1,0},{2,3},{3,2},{4,5},{5,4},{6,7},{7,6},{8,9},{9,8},{10,11... | collective-permute-start | bytes 1572872 | tf_op jit(solution)/shard_map/ppermute | solution.py:291
  133.1 3.7 %collective-permute-start.13 = (bf16[512,512]{1,0:T(8,128)(2,1)S(1)}, bf16[512,512]{1,0:T(8,128)(2,1)S(1)}, u32[]{:S(2)}, u32[]{:S(2)}) collective-permute-start(bf16[512,512]{1,0:T(8,128)(2,1)S(1)} %get-tuple-element.30), channel_id=1, source_target_pairs={{0,1},{1,0},{2,3},{3,2},{4,5},{5,4},{6,7},{7,6},{8,9},{9,8},{10,11... | collective-permute-start | bytes 1572872 | tf_op jit(solution)/shard_map/ppermute | solution.py:291
  135.5 12.7 %collective-permute-start.14 = (bf16[512,512]{1,0:T(8,128)(2,1)S(1)}, bf16[512,512]{1,0:T(8,128)(2,1)S(1)}, u32[]{:S(2)}, u32[]{:S(2)}) collective-permute-start(bf16[512,512]{1,0:T(8,128)(2,1)S(1)} %shard_map.72.refs_6_), channel_id=1, source_target_pairs={{0,2},{1,3},{2,0},{3,1},{4,6},{5,7},{6,4},{7,5},{8,10},{9,11},{10,... | collective-permute-start | bytes 1572872 | tf_op jit(solution)/shard_map/ppermute | solution.py:288
  136.7 11.4 %copy-start.3 = (bf16[2,512,512]{2,1,0:T(8,128)(2,1)S(1)}, bf16[2,512,512]{2,1,0:T(8,128)(2,1)}, u32[]{:S(2)}) copy-start(bf16[2,512,512]{2,1,0:T(8,128)(2,1)} %refs_0_.5) | copy-start | bytes 3145732

commit v3 on v2

--- a/solution.py
+++ b/solution.py
@@ -114,8 +114,8 @@
         out_ref[i * tile : (i + 1) * tile, out_at] = (out / total).astype(BF16)
 
 
-def permute_kernel(samples_hbm, out_hbm, in_ref, out_ref, sems):
-    cols, width = samples_hbm.shape[1:]
+def permute_kernel(samples_hbm, out0_hbm, out1_hbm, in_ref, out_ref, sems):
+    cols = samples_hbm.shape[1]
     step = cols // 4
     spans = [pl.ds(i * step, step) for i in range(4)]
     arriving = fetch([samples_hbm.at[:, at] for at in spans], [in_ref.at[:, at] for at in spans], sems.at[0])
@@ -123,61 +123,56 @@
     for i, at in enumerate(spans):
         arriving[i].wait()
         halves = interleave(in_ref[0, at, :].astype(F32), in_ref[1, at, :].astype(F32))
-        tiles = jnp.stack([t.reshape(step // 8, 8, width) for t in halves], axis=1)
-        to = pl.ds(i * 2 * step, 2 * step)
-        out_ref[to, :] = tiles.reshape(2 * step, width).astype(BF16)
-        leaving += fetch([out_ref.at[to]], [out_hbm.at[to]], sems.at[1, i : i + 1])
+        for k, half in enumerate(halves):
+            out_ref[k, at, :] = half.astype(BF16)
+        leaving += fetch([out_ref.at[k, at] for k in range(2)], [o.at[at] for o in (out0_hbm, out1_hbm)], sems.at[1 + i])
     for copy in leaving:
         copy.wait()
 
 
 def permute(samples):
-    rows, cols, width = samples.shape
-    out = sds((rows * cols, width))
+    outs = (sds(samples.shape[1:]),) * 2
     return pl.pallas_call(
         permute_kernel,
-        out_shape=out,
+        out_shape=outs,
         in_specs=[ANY],
-        out_specs=ANY,
+        out_specs=(ANY, ANY),
         scratch_shapes=[
             pltpu.VMEM(samples.shape, BF16),
-            pltpu.VMEM(out.shape, BF16),
-            pltpu.SemaphoreType.DMA((2, 4)),
+            pltpu.VMEM(samples.shape, BF16),
+            pltpu.SemaphoreType.DMA((5, 4)),
         ],
         compiler_params=params(WHOLE),
-        cost_estimate=cost(samples.size, [samples, out]),
+        cost_estimate=cost(samples.size, [samples, *outs]),
     )(samples)
 
 
-def norm_into(h, refs, gain_ref, normed_ref):
-    tokens, width = refs[0].shape
+def norm_project(h, refs, gain_ref, w_ref, copies, qkv_ref, sum_ref=None):
+    width = refs[0].shape[1]
     features = 4 * width
-    tile = min(32, tokens)
-
-    @pl.loop(0, tokens // tile, unroll=2)
-    def _(i):
-        at = pl.ds(pl.multiple_of(i * tile, tile), tile)
-        total = sum(ref[at, :].astype(F32) for ref in refs)
-        mean = jnp.sum(total, axis=-1, keepdims=True) * (1.0 / features)
-        squares = 0.0
-        for ref in refs:
-            centred = ref[at, :].astype(F32) - mean
-            squares = squares + centred * centred
-        var = jnp.sum(squares, axis=-1, keepdims=True) * (1.0 / features)
-        scale = lax.rsqrt(var + 1e-05)
-        for ref, flip in zip(refs, (0, 2, 1, 3)):
-            where = block(h ^ flip, width)
-            rows = (ref[at, :].astype(F32) - mean) * scale * gain_ref[:, where]
-            normed_ref[at, where] = rows.astype(BF16)
-
-
-def project(normed_ref, w_ref, copies, qkv_ref):
     wide = w_ref.shape[2]
+    total = jnp.sum(sum(ref[...].astype(F32) for ref in refs[sum_ref is not None :]), axis=-1, keepdims=True)
+    if sum_ref is not None:
+        total = total + jnp.sum(sum_ref[...], axis=-1, keepdims=True)
+    mean = total * (1.0 / features)
+    squares = 0.0
+    for ref in refs:
+        centred = ref[...].astype(F32) - mean
+        squares = squares + centred * centred
+    var = jnp.sum(squares, axis=-1, keepdims=True) * (1.0 / features)
+    scale = lax.rsqrt(var + 1e-05)
+    blocks = [block(h ^ flip, width) for flip in (0, 2, 1, 3)]
+    normed = [
+        ((ref[...].astype(F32) - mean) * scale * gain_ref[:, where]).astype(BF16)
+        for ref, where in zip(refs, blocks)
+    ]
+    for copy in copies:
+        copy.wait()
     for t in range(3):
-        copies[t].wait()
-        qkv_ref[:, t * wide : (t + 1) * wide] = jnp.dot(
-            normed_ref[...], w_ref[t], preferred_element_type=F32
-        ).astype(BF16)
+        product = sum(
+            jnp.dot(x, w_ref[t, where, :], preferred_element_type=F32) for x, where in zip(normed, blocks)
+        )
+        qkv_ref[:, t * wide : (t + 1) * wide] = product.astype(BF16)
 
 
 def heads(qkv_ref, bits, attn_ref):
@@ -187,51 +182,35 @@
         attend(qkv_ref, lanes(0, head, wide), [(qkv_ref, keys)], [(qkv_ref, vals)], 0, bits, attn_ref, lanes(0, head, wide))
 
 
-def fetch_weights(gain_hbm, w_hbm, gain_ref, w_ref, sems):
-    return fetch([gain_hbm] + [w_hbm.at[t] for t in range(3)], [gain_ref] + [w_ref.at[t] for t in range(3)], sems)
-
-
-def attention(h, parts, copies, bits, attn_ref, gain_ref, w_ref, normed_ref, qkv_ref):
-    copies[0].wait()
-    norm_into(h, parts, gain_ref, normed_ref)
-    project(normed_ref, w_ref, copies[1:], qkv_ref)
-    heads(qkv_ref, bits, attn_ref)
-
-
-def attention_scratch(gain, weights, tokens):
-    _, features, wide = weights.shape
-    return [
-        pltpu.VMEM(gain.shape, F32),
-        pltpu.VMEM(weights.shape, BF16),
-        pltpu.VMEM((tokens, features), BF16),
-        pltpu.VMEM((tokens, 3 * wide), BF16),
-    ]
-
-
-def col_kernel(h_ref, a, b, c, d, gain_hbm, w_hbm, attn_ref, gain_ref, w_ref, normed_ref, qkv_ref, sems):
-    copies = fetch_weights(gain_hbm, w_hbm, gain_ref, w_ref, sems)
-    attention(h_ref[0], (a, b, c, d), copies, OWNED - 1, attn_ref, gain_ref, w_ref, normed_ref, qkv_ref)
-
-
-def row_kernel(row, n_more, h_ref, *refs):
-    parts_hbm, more_hbm, (gain_hbm, w_hbm) = refs[:4], refs[4 : 4 + n_more], refs[4 + n_more : 6 + n_more]
-    rest = refs[6 + n_more + n_more :] if n_more else refs[6:]
-    n_out = 2 if n_more else 1
-    outs_hbm = rest[:n_out]
-    x_ref, held_ref, gain_ref, w_ref, normed_ref, qkv_ref, sems, more_sems = rest[n_out:]
-    ready = fetch([p.at[row] for p in parts_hbm], [x_ref.at[i] for i in range(4)], sems)
-    copies = fetch_weights(gain_hbm, w_hbm, gain_ref, w_ref, sems.at[4:])
-    earlier = fetch(more_hbm, [held_ref.at[0]], more_sems)
-    for copy in ready:
-        copy.wait()
-    parts = [x_ref.at[i] for i in range(4)]
-    attention(h_ref[0], parts, copies, 0, held_ref.at[n_more], gain_ref, w_ref, normed_ref, qkv_ref)
-    if n_more:
-        earlier[0].wait()
-        halves = interleave(held_ref[0].astype(F32), held_ref[1].astype(F32))
-        for i, half in enumerate(halves):
-            held_ref[i] = half.astype(BF16)
-    for copy in fetch([held_ref.at[i] for i in range(n_out)], outs_hbm, more_sems):
+def sum_kernel(x_ref, sum_ref):
+    lanes = sum_ref.shape[1]
+    sum_ref[...] = sum(x_ref[:, i : i + lanes].astype(F32) for i in range(0, x_ref.shape[1], lanes))
+
+
+def col_kernel(n_sums, h_ref, a, b, c, d, gain_ref, w_ref, *refs):
+    attn_ref, qkv_ref = refs[-2:]
+    norm_project(h_ref[0], (a, b, c, d), gain_ref, w_ref, (), qkv_ref, refs[0] if n_sums else None)
+    heads(qkv_ref, OWNED - 1, attn_ref)
+
+
+def row_kernel(h_ref, *refs):
+    parts_hbm, gain_hbm, w_hbm = refs[:4], refs[4], refs[5]
+    x_ref, held_ref, gain_ref, w_ref, qkv_ref, sems = refs[-6:]
+    outs_hbm = refs[-8:-6]
+    first = fetch([gain_hbm] + [p.at[0] for p in parts_hbm], [gain_ref] + [x_ref.at[0, i] for i in range(4)], sems)
+    weights = fetch([w_hbm], [w_ref], sems.at[5:])
+    second = fetch([p.at[1] for p in parts_hbm], [x_ref.at[1, i] for i in range(4)], sems.at[6:])
+    for row, ready, copies in ((0, first, weights), (1, second, ())):
+        for copy in ready:
+            copy.wait()
+        norm_project(h_ref[0], [x_ref.at[row, i] for i in range(4)], gain_ref, w_ref, copies, qkv_ref)
+        heads(qkv_ref, 0, held_ref.at[row])
+    halves = interleave(held_ref[0].astype(F32), held_ref[1].astype(F32))
+    leaving = []
+    for i, half in enumerate(halves):
+        held_ref[2 + i] = half.astype(BF16)
+        leaving += fetch([held_ref.at[2 + i]], [outs_hbm[i]], sems.at[i:])
+    for copy in leaving:
         copy.wait()
 
 
@@ -299,31 +278,36 @@
 
     flops = 2 * tokens * features * 3 * wide + 4 * tokens * tokens * wide
 
-    def cols(parts, after):
+    def cols(parts, after, sums=()):
         return call(
-            col_kernel,
+            functools.partial(col_kernel, len(sums)),
             (h,),
-            parts,
-            (gain, col_qkv),
+            (*parts, gain, col_qkv, *sums),
+            (),
             (sds((tokens, wide)),),
             flops,
-            attention_scratch(gain, col_qkv, tokens) + [dma((4,))],
+            [pltpu.VMEM((tokens, 3 * wide), BF16)],
             after,
         )[0]
 
-    def row(r, parts, more, after):
-        outs = tuple([sds((tokens, wide))] * (1 + len(more)))
+    def both_rows(parts, after, weight):
+        outs = (sds((tokens, wide)),) * 2
         return pl.pallas_call(
-            functools.partial(row_kernel, r, len(more)),
+            row_kernel,
             out_shape=outs,
-            in_specs=[SM] + [ANY] * (6 + len(more) + len(after)),
-            out_specs=tuple([ANY] * len(outs)),
-            scratch_shapes=[pltpu.VMEM((4, tokens, width), BF16), pltpu.VMEM((2, tokens, wide), BF16)]
-            + attention_scratch(gain, row_qkv, tokens)
-            + [dma((8,)), dma((2,))],
+            in_specs=[SM] + [ANY] * (6 + len(after)),
+            out_specs=(ANY, ANY),
+            scratch_shapes=[
+                pltpu.VMEM((2, 4, tokens, width), BF16),
+                pltpu.VMEM((4, tokens, wide), BF16),
+                pltpu.VMEM(gain.shape, F32),
+                pltpu.VMEM(row_qkv.shape, BF16),
+                pltpu.VMEM((tokens, 3 * wide), BF16),
+                dma((10,)),
+            ],
             compiler_params=params(WHOLE),
-            cost_estimate=cost(flops, parts, 4),
-        )(h, *parts, *more, gain, row_qkv, *after)
+            cost_estimate=cost(2 * flops, parts, weight),
+        )(h, *parts, gain, row_qkv, *after)
 
     piece = 4 * tokens * wide * width
 
@@ -339,24 +323,23 @@
         return own, s2, over_chip(s2)
 
     every = gather(samples)
-    mine = exchange(permute(samples)).reshape(-1, 2, 2 * OWNED, width)
-    (row0,) = row(0, every, (), ())
-    mine, row0 = lax.optimization_barrier((mine, row0))
-    start0 = mine[:, 0].reshape(tokens, width)
+    mixed0, mixed1 = permute(samples)
+    start0 = exchange(mixed0)
     chip0 = over_chip(start0)
-    mine, _ = lax.optimization_barrier((mine, chip0))
-    start1 = mine[:, 1].reshape(tokens, width)
+    mixed1, start0 = lax.optimization_barrier((mixed1, start0))
+    start1 = exchange(mixed1)
+    rows0, rows1 = both_rows(every, (), 1)
+    core0, diagonal0 = over_core(start0), over_core(chip0)
+    start0, rows0 = lax.optimization_barrier((start0, rows0))
+    attn0 = cols((start0, chip0, core0, diagonal0), ())
+    start1, attn0, rows0 = lax.optimization_barrier((start1, attn0, rows0))
     chip1 = over_chip(start1)
-    rows0, rows1 = row(1, every, (row0,), (row0,))
-    chip0, rows0 = lax.optimization_barrier((chip0, rows0))
-    parts0 = (start0, chip0, over_core(start0), over_core(chip0))
-    attn0 = cols(parts0, (rows0,))
     back0 = exchange(attn0)
-    start1, chip1, _ = lax.optimization_barrier((start1, chip1, attn0))
-    attn1 = cols((start1, chip1, over_core(start1), over_core(chip1)), (attn0,))
+    (sums,) = call(sum_kernel, (), (start1,), (), (sds((tokens, HD), F32),), 4 * flops)
+    attn1 = cols((start1, chip1, over_core(start1), over_core(chip1)), (), (sums,))
     back1 = exchange(attn1)
     own0, s0, rx0 = out(rows0, back0, (attn1,), ())
-    own1, s1, rx1 = out(rows1, back1, (s0,), (rx0,))
+    own1, s1, rx1 = out(rows1, back1, (rx0,), ())
     own0 = own0((s1,))
     own1 = own1((own0,))
     return call(final_kernel, (), (samples, own0, rx0, own1, rx1), (), (sds(samples.shape),), samples.size)[0]

time: 152 us -> 141 us (0.928)
  blocking collectives: 0 us -> 20.1 us
  Pallas kernels: 45.8 us -> 29.5 us
  waiting for transfers between devices: 39.2 us -> 29.8 us
  local copies, waits for them, and re-layouts: 5.78 us -> 1.92 us
    all_to_all x0 -> x1, blocking collectives: none -> 20.1 us  [exchange(): return lax.all_to_all(x, 'row', 0, 0, tiled=True)]
    pallas_call x9 -> x10, Pallas kernels: 25.4 us -> 15.6 us  [call(): pl.pallas_call(kernel, out_shape=tuple(outs), in_specs=[SM] * len(scalars...]
    ppermute x5, waiting for transfers between devices: 25 us -> 17.8 us  [over_chip(): return lax.ppermute(x, 'head', [(i, i ^ 2) for i in range(4)])]
    pallas_call x3 -> x2, Pallas kernels: 20.5 us -> 13.9 us  [the longest x1 11.8 us: both_rows(): pl.pallas_call(row_kernel, out_shape=outs, in_specs=[SM] + [ANY] * (6 + l...]
    ppermute x10, starting transfers between devices: 19.4 us -> 14.6 us  [over_core(): return lax.ppermute(x, 'head', [(i, i ^ 1) for i in range(4)])]
    unnamed x26 -> x16, local copies, waits for them, and re-layouts: 5.71 us -> 1.92 us
    all_to_all x3, starting transfers between devices: 36.7 us -> 39.9 us  [exchange(): return lax.all_to_all(x, 'row', 0, 0, tiled=True)]
    all_to_all x3, waiting for transfers between devices: 10.5 us -> 7.78 us  [exchange(): return lax.all_to_all(x, 'row', 0, 0, tiled=True)]
  transfers between devices with their start and end apart: 18 -> 18, of which waited for: 10 -> 7; matrix products, arithmetic and copies ran while one was open for 0% -> 0% of each run, Pallas kernels for 28% -> 19%
where the time goes in v3:
time: 141 us
  starting transfers between devices  59.3 us (42%)
  waiting for transfers between devices  29.8 us (21%)
  Pallas kernels  29.5 us (21%)
  blocking collectives  20.1 us (14%)
  local copies, waits for them, and re-layouts  1.92 us (1%)
    all_to_all x3, starting transfers between devices, exchange(): return lax.all_to_all(x, 'row', 0, 0, tiled=True)  39.9 us
    all_to_all x1, blocking collectives, exchange(): return lax.all_to_all(x, 'row', 0, 0, tiled=True)  20.1 us
    ppermute x5, waiting for transfers between devices, over_chip(): return lax.ppermute(x, 'head', [(i, i ^ 2) for i in range(4)])  17.8 us
    pallas_call x10, Pallas kernels, call(): pl.pallas_call(kernel, out_shape=tuple(outs), in_specs=[SM] * len(scalars...  15.6 us
    ppermute x10, starting transfers between devices, over_core(): return lax.ppermute(x, 'head', [(i, i ^ 1) for i in range(4)])  14.6 us
    pallas_call x1, Pallas kernels, both_rows(): pl.pallas_call(row_kernel, out_shape=outs, in_specs=[SM] + [ANY] * (6 + l...  11.8 us
    all_to_all x3, waiting for transfers between devices, exchange(): return lax.all_to_all(x, 'row', 0, 0, tiled=True)  7.78 us
    ppermute x5, starting transfers between devices, over_chip(): return lax.ppermute(x, 'head', [(i, i ^ 2) for i in range(4)])  4.83 us
  transfers between devices with their start and end apart: 18, of which 7 were waited for; matrix products, arithmetic and copies ran while one was open for 0% of the time, Pallas kernels for 19%

profile of v3, /device:TPU:1, one launch (start us, length us, event | category | flops | bytes accessed | tf_op | source)
XLA Modules:
  0.0 140.8 jit_solution(7676073910905229100)
XLA Ops:
  0.0 2.0 %collective-permute-start = (bf16[2,512,512]{2,1,0:T(8,128)(2,1)}, bf16[2,512,512]{2,1,0:T(8,128)(2,1)}, u32[]{:S(2)}, u32[]{:S(2)}) collective-permute-start(bf16[2,512,512]{2,1,0:T(8,128)(2,1)} %refs_0_.3), channel_id=1, source_target_pairs={{0,2},{1,3},{2,0},{3,1},{4,6},{5,7},{6,4},{7,5},{8,10},{9,11},{10,... | collective-permute-start | bytes 3145736 | tf_op jit(solution)/shard_map/ppermute | solution.py:267
  2.0 2.2 %shard_map.64 = (bf16[512,512]{1,0:T(8,128)(2,1)}, bf16[512,512]{1,0:T(8,128)(2,1)}) custom-call(bf16[2,512,512]{2,1,0:T(8,128)(2,1)} %refs_0_.3), custom_call_target="tpu_custom_call" | custom-call | flops 524288 | bytes 2097152 | tf_op jit(solution)/shard_map/pallas_call | solution.py:135
  4.2 14.0 %all-to-all-start = ((bf16[64,8,512]{2,1,0:T(8,128)(2,1)}), bf16[64,8,512]{2,1,0:T(8,128)(2,1)S(1)}, u32[]{:S(2)}, u32[]{:S(2)}) async-start(bf16[64,8,512]{2,1,0:T(8,128)(2,1)} %bitcast.28), calls=%async_computation | async-start | bytes 1048576 | tf_op jit(solution)/shard_map/all_to_all | solution.py:273
  18.2 1.3 collective-permute-start.1
  19.6 7.0 %collective-permute-done.refs_1_ = bf16[2,512,512]{2,1,0:T(8,128)(2,1)} collective-permute-done((bf16[2,512,512]{2,1,0:T(8,128)(2,1)}, bf16[2,512,512]{2,1,0:T(8,128)(2,1)}, u32[]{:S(2)}, u32[]{:S(2)}) %collective-permute-start) | collective-permute-done | bytes 1048608 | tf_op jit(solution)/shard_map/ppermute | solution.py:267
  26.6 4.6 %collective-permute-start.2 = (bf16[2,512,512]{2,1,0:T(8,128)(2,1)}, bf16[2,512,512]{2,1,0:T(8,128)(2,1)}, u32[]{:S(2)}, u32[]{:S(2)}) collective-permute-start(bf16[2,512,512]{2,1,0:T(8,128)(2,1)} %collective-permute-done.refs_1_), channel_id=1, source_target_pairs={{0,1},{1,0},{2,3},{3,2},{4,5},{5,4},{6,7},{7,6},{8,9},{9,8},{10,11... | collective-permute-start | bytes 3145736 | tf_op jit(solution)/shard_map/ppermute | solution.py:270
  31.2 3.2 %all-to-all-done = bf16[64,8,512]{2,1,0:T(8,128)(2,1)S(1)} async-done(((bf16[64,8,512]{2,1,0:T(8,128)(2,1)}), bf16[64,8,512]{2,1,0:T(8,128)(2,1)S(1)}, u32[]{:S(2)}, u32[]{:S(2)}) %all-to-all-start) | async-done | bytes 524320 | tf_op jit(solution)/shard_map/all_to_all | solution.py:273
  34.4 0.0 collective-permute-start.3
  34.4 12.8 %all-to-all-start.1 = ((bf16[64,8,512]{2,1,0:T(8,128)(2,1)}), bf16[64,8,512]{2,1,0:T(8,128)(2,1)S(1)}, u32[]{:S(2)}, u32[]{:S(2)}) async-start(bf16[64,8,512]{2,1,0:T(8,128)(2,1)} %bitcast.27), calls=%async_computation.1 | async-start | bytes 1048576 | tf_op jit(solution)/shard_map/all_to_all | solution.py:273
  47.2 1.4 %collective-permute-start.4 = (bf16[512,512]{1,0:T(8,128)(2,1)S(1)}, bf16[512,512]{1,0:T(8,128)(2,1)S(1)}, u32[]{:S(2)}, u32[]{:S(2)}) collective-permute-start(bf16[512,512]{1,0:T(8,128)(2,1)S(1)} %bitcast.22), channel_id=1, source_target_pairs={{0,1},{1,0},{2,3},{3,2},{4,5},{5,4},{6,7},{7,6},{8,9},{9,8},{10,11... | collective-permute-start | bytes 1572872 | tf_op jit(solution)/shard_map/ppermute | solution.py:270
  48.6 0.0 collective-permute-done.3.refs_2_
  48.6 0.3 collective-permute-start.5
  48.9 0.0 collective-permute-done.1.refs_2_
  48.9 0.0 collective-permute-done.2.refs_3_
  48.9 11.8 %shard_map.65 = (bf16[512,256]{1,0:T(8,128)(2,1)}, bf16[512,256]{1,0:T(8,128)(2,1)}) custom-call(s32[1]{0:T(128)} %bitcast.h_ref.refs_0_, bf16[2,512,512]{2,1,0:T(8,128)(2,1)} %refs_0_.3, bf16[2,512,512]{2,1,0:T(8,128)(2,1)} %collective-permute-done.refs_1_, bf16[2,512,512]{2,1,0:T(8,128)(2,1)} %collective-permute-done.1.refs_2_, ...), custom_call_target="tpu_custom_call" | custom-call | flops 3758096384 | bytes 4194304 | tf_op jit(solution)/shard_map/pallas_call | solution.py:295
  60.7 0.0 collective-permute-done.4.refs_3_
  60.7 0.0 collective-permute-done.5.refs_4_
  60.7 0.0 copy-done.7
  60.7 0.0 copy-start.5
  60.7 1.9 %copy-done.5 = bf16[3,2048,256]{2,1,0:T(8,128)(2,1)S(1)} copy-done((bf16[3,2048,256]{2,1,0:T(8,128)(2,1)S(1)}, bf16[3,2048,256]{2,1,0:T(8,128)(2,1)}, u32[]{:S(2)}) %copy-start.5) | copy-done | bytes 3145752
  62.6 5.2 %shard_map.66 = bf16[512,256]{1,0:T(8,128)(2,1)} custom-call(s32[1]{0:T(128)} %bitcast.h_ref.refs_0_, bf16[512,512]{1,0:T(8,128)(2,1)S(1)} %bitcast.23, bf16[512,512]{1,0:T(8,128)(2,1)S(1)} %collective-permute-done.3.refs_2_, bf16[512,512]{1,0:T(8,128)(2,1)S(1)} %collective-permute-done.4.refs_3_, bf16[512,512]{1,0:T(8,128)(2,1)S(1)} %collective-permute-done.5.refs_4_, ...), custom_call_target="tpu_custom_call" | custom-call | flops 1879048192 | bytes 5513216 | tf_op jit(solution)/shard_map/pallas_call | solution.py:38
  67.8 0.0 all-to-all-done.1
  67.8 0.3 collective-permute-start.6
  68.1 0.5 collective-permute-start.7
  68.6 13.0 %all-to-all-start.2 = ((bf16[64,8,256]{2,1,0:T(8,128)(2,1)}), bf16[64,8,256]{2,1,0:T(8,128)(2,1)S(1)}, u32[]{:S(2)}, u32[]{:S(2)}) async-start(bf16[64,8,256]{2,1,0:T(8,128)(2,1)} %bitcast.6), calls=%async_computation.2 | async-start | bytes 524288 | tf_op jit(solution)/shard_map/all_to_all | solution.py:273
  81.7 0.0 copy-start.6
  81.7 0.0 collective-permute-done.6.refs_2_
  81.7 0.6 collective-permute-start.8
  82.3 0.1 shard_map.67.refs_7_
  82.3 0.0 copy-start
  82.4 0.0 copy-start.1
  82.4 0.0 copy-start.3
  82.4 0.0 collective-permute-done.7.refs_3_
  82.4 1.6 %collective-permute-done.8.refs_4_ = bf16[512,512]{1,0:T(8,128)(2,1)S(1)} collective-permute-done((bf16[512,512]{1,0:T(8,128)(2,1)}, bf16[512,512]{1,0:T(8,128)(2,1)S(1)}, u32[]{:S(2)}, u32[]{:S(2)}) %collective-permute-start.8) | collective-permute-done | bytes 524320 | tf_op jit(solution)/shard_map/ppermute | solution.py:270
  84.0 0.0 copy-done.6
  84.0 5.7 %shard_map.68.refs_5_ = bf16[512,256]{1,0:T(8,128)(2,1)S(1)} custom-call(s32[1]{0:T(128)} %bitcast.h_ref.refs_0_, bf16[512,512]{1,0:T(8,128)(2,1)S(1)} %bitcast.20, bf16[512,512]{1,0:T(8,128)(2,1)} %collective-permute-done.6.refs_2_, bf16[512,512]{1,0:T(8,128)(2,1)} %collective-permute-done.7.refs_3_, bf16[512,512]{1,0:T(8,128)(2,1)S(1)} %collective-permute-done.8.refs_4_, ...), custom_call_target="tpu_custom_call" | custom-call | flops 1879048192 | bytes 5775360 | tf_op jit(solution)/shard_map/pallas_call | solution.py:38
  89.7 4.6 %all-to-all-done.2 = bf16[64,8,256]{2,1,0:T(8,128)(2,1)S(1)} async-done(((bf16[64,8,256]{2,1,0:T(8,128)(2,1)}), bf16[64,8,256]{2,1,0:T(8,128)(2,1)S(1)}, u32[]{:S(2)}, u32[]{:S(2)}) %all-to-all-start.2) | async-done | bytes 262176 | tf_op jit(solution)/shard_map/all_to_all | solution.py:273
  94.3 0.0 copy-done
  94.3 0.0 copy-done.1
  94.3 0.0 copy-done.3
  94.3 0.0 copy-start.4
  94.3 0.7 shard_map.69
  95.0 2.0 %collective-permute-start.10 = (bf16[512,512]{1,0:T(8,128)(2,1)S(1)}, bf16[512,512]{1,0:T(8,128)(2,1)S(1)}, u32[]{:S(2)}, u32[]{:S(2)}) collective-permute-start(bf16[512,512]{1,0:T(8,128)(2,1)S(1)} %get-tuple-element.32), channel_id=1, source_target_pairs={{0,1},{1,0},{2,3},{3,2},{4,5},{5,4},{6,7},{7,6},{8,9},{9,8},{10,11... | collective-permute-start | bytes 1572872 | tf_op jit(solution)/shard_map/ppermute | solution.py:270
  97.0 1.5 %collective-permute-done.10.refs_5_ = bf16[512,512]{1,0:T(8,128)(2,1)S(1)} collective-permute-done((bf16[512,512]{1,0:T(8,128)(2,1)S(1)}, bf16[512,512]{1,0:T(8,128)(2,1)S(1)}, u32[]{:S(2)}, u32[]{:S(2)}) %collective-permute-start.10) | collective-permute-done | bytes 524320 | tf_op jit(solution)/shard_map/ppermute | solution.py:270
  98.5 0.4 shard_map.70
  99.0 1.0 collective-permute-start.11
  100.0 20.1 %all_to_all.46 = bf16[64,8,256]{2,1,0:T(8,128)(2,1)S(1)} all-to-all(bf16[64,8,256]{2,1,0:T(8,128)(2,1)S(1)} %bitcast.16), channel_id=1, replica_groups=mesh['row'=64,'head'=4] {'row'}, dimensions={0} | all-to-all | bytes 524288 | tf_op jit(solution)/shard_map/all_to_all | solution.py:273
  120.0 0.0 collective-permute-done.11.refs_5_.refs_2_
  120.0 0.0 copy-done.4
  120.1 0.7 shard_map.71
  120.8 3.3 %collective-permute-start.12 = (bf16[512,512]{1,0:T(8,128)(2,1)S(1)}, bf16[512,512]{1,0:T(8,128)(2,1)S(1)}, u32[]{:S(2)}, u32[]{:S(2)}) collective-permute-start(bf16[512,512]{1,0:T(8,128)(2,1)S(1)} %get-tuple-element.33), channel_id=1, source_target_pairs={{0,1},{1,0},{2,3},{3,2},{4,5},{5,4},{6,7},{7,6},{8,9},{9,8},{10,11... | collective-permute-start | bytes 1572872 | tf_op jit(solution)/shard_map/ppermute | solution.py:270
  124.1 0.1 collective-permute-start.9
  124.2 0.4 collective-permute-start.13
  124.6 1.0 collective-permute-done.12.refs_5_
  125.7 0.4 shard_map.72.refs_6_
  126.1 1.5 %collective-permute-start.14 = (bf16[512,512]{1,0:T(8,128)(2,1)S(1)}, bf16[512,512]{1,0:T(8,128)(2,1)S(1)}, u32[]{:S(2)}, u32[]{:S(2)}) collective-permute-start(bf16[512,512]{1,0:T(8,128)(2,1)S(1)} %shard_map.72.refs_6_), channel_id=1, source_target_pairs={{0,2},{1,3},{2,0},{3,1},{4,6},{5,7},{6,4},{7,5},{8,10},{9,11},{10,... | collective-permute-start | bytes 1572872 | tf_op jit(solution)/shard_map/ppermute | solution.py:267
  127.6 0.0 collective-permute-done.9.refs_5_
  127.6 0.4 shard_map.73.refs_6_.refs_1_
  128.1 0.0 copy-start.2
  128.1 0.0 collective-permute-done.13.refs_5_
  128.1 0.4 shard_map.74.refs_3_
  128.6 10.8 %collective-permute-done.14.refs_4_ = bf16[512,512]{1,0:T(8,128)(2,1)S(1)} collective-permute-done((bf16[512,512]{1,0:T(8,128)(2,1)S(1)}, bf16[512,512]{1,0:T(8,128)(2,1)S(1)}, u32[]{:S(2)}, u32[]{:S(2)}) %collective-permute-start.14) | collective-permute-done | bytes 524320 | tf_op jit(solution)/shard_map/ppermute | solution.py:267
  139.3 0.0 copy-done.2
  139.3 1.5 %shard_map.75 = bf16[2,512,512]{2,1,0:T(8,128)(2,1)} custom-call(bf16[2,512,512]{2,1,0:T(8,128)(2,1)S(1)} %copy-done.2, f32[512,512]{1,0:T(8,128)S(1)} %shard_map.73.refs_6_.refs_1_, bf16[512,512]{1,0:T(8,128)(2,1)S(1)} %collective-permute-done.11.refs_5_.refs_2_, f32[512,512]{1,0:T(8,128)S(1)} %shard_map.74.refs_3_, ...), custom_call_target="tpu_custom_call" | custom-call | flops 524288 | bytes 5242880 | tf_op jit(solution)/shard_map/pallas_call | solution.py:38
  (1 shorter events, 0.0 us)
Async XLA Ops:
  0.0 26.6 %collective-permute-start = (bf16[2,512,512]{2,1,0:T(8,128)(2,1)}, bf16[2,512,512]{2,1,0:T(8,128)(2,1)}, u32[]{:S(2)}, u32[]{:S(2)}) collective-permute-start(bf16[2,512,512]{2,1,0:T(8,128)(2,1)} %refs_0_.3), channel_id=1, source_target_pairs={{0,2},{1,3},{2,0},{3,1},{4,6},{5,7},{6,4},{7,5},{8,10},{9,11},{10,... | collective-permute-start | bytes 3145736 | tf_op jit(solution)/shard_map/ppermute | solution.py:267
  4.2 30.2 %all-to-all-start = ((bf16[64,8,512]{2,1,0:T(8,128)(2,1)}), bf16[64,8,512]{2,1,0:T(8,128)(2,1)S(1)}, u32[]{:S(2)}, u32[]{:S(2)}) async-start(bf16[64,8,512]{2,1,0:T(8,128)(2,1)} %bitcast.28), calls=%async_computation | async-start | bytes 1048576 | tf_op jit(solution)/shard_map/all_to_all | solution.py:273
  18.2 30.7 %collective-permute-start.1 = (bf16[2,512,512]{2,1,0:T(8,128)(2,1)}, bf16[2,512,512]{2,1,0:T(8,128)(2,1)}, u32[]{:S(2)}, u32[]{:S(2)}) collective-permute-start(bf16[2,512,512]{2,1,0:T(8,128)(2,1)} %refs_0_.3), channel_id=1, source_target_pairs={{0,1},{1,0},{2,3},{3,2},{4,5},{5,4},{6,7},{7,6},{8,9},{9,8},{10,11... | collective-permute-start | bytes 3145736 | tf_op jit(solution)/shard_map/ppermute | solution.py:270
  26.6 22.4 %collective-permute-start.2 = (bf16[2,512,512]{2,1,0:T(8,128)(2,1)}, bf16[2,512,512]{2,1,0:T(8,128)(2,1)}, u32[]{:S(2)}, u32[]{:S(2)}) collective-permute-start(bf16[2,512,512]{2,1,0:T(8,128)(2,1)} %collective-permute-done.refs_1_), channel_id=1, source_target_pairs={{0,1},{1,0},{2,3},{3,2},{4,5},{5,4},{6,7},{7,6},{8,9},{9,8},{10,11... | collective-permute-start | bytes 3145736 | tf_op jit(solution)/shard_map/ppermute | solution.py:270
  34.4 14.3 %collective-permute-start.3 = (bf16[512,512]{1,0:T(8,128)(2,1)S(1)}, bf16[512,512]{1,0:T(8,128)(2,1)S(1)}, u32[]{:S(2)}, u32[]{:S(2)}) collective-permute-start(bf16[512,512]{1,0:T(8,128)(2,1)S(1)} %bitcast.21), channel_id=1, source_target_pairs={{0,2},{1,3},{2,0},{3,1},{4,6},{5,7},{6,4},{7,5},{8,10},{9,11},{10,... | collective-permute-start | bytes 1572872 | tf_op jit(solution)/shard_map/ppermute | solution.py:267
  34.4 33.5 %all-to-all-start.1 = ((bf16[64,8,512]{2,1,0:T(8,128)(2,1)}), bf16[64,8,512]{2,1,0:T(8,128)(2,1)S(1)}, u32[]{:S(2)}, u32[]{:S(2)}) async-start(bf16[64,8,512]{2,1,0:T(8,128)(2,1)} %bitcast.27), calls=%async_computation.1 | async-start | bytes 1048576 | tf_op jit(solution)/shard_map/all_to_all | solution.py:273
  47.2 13.5 %collective-permute-start.4 = (bf16[512,512]{1,0:T(8,128)(2,1)S(1)}, bf16[512,512]{1,0:T(8,128)(2,1)S(1)}, u32[]{:S(2)}, u32[]{:S(2)}) collective-permute-start(bf16[512,512]{1,0:T(8,128)(2,1)S(1)} %bitcast.22), channel_id=1, source_target_pairs={{0,1},{1,0},{2,3},{3,2},{4,5},{5,4},{6,7},{7,6},{8,9},{9,8},{10,11... | collective-permute-start | bytes 1572872 | tf_op jit(solution)/shard_map/ppermute | solution.py:270
  48.6 12.1 %collective-permute-start.5 = (bf16[512,512]{1,0:T(8,128)(2,1)S(1)}, bf16[512,512]{1,0:T(8,128)(2,1)S(1)}, u32[]{:S(2)}, u32[]{:S(2)}) collective-permute-start(bf16[512,512]{1,0:T(8,128)(2,1)S(1)} %collective-permute-done.3.refs_2_), channel_id=1, source_target_pairs={{0,1},{1,0},{2,3},{3,2},{4,5},{5,4},{6,7},{7,6},{8,9},{9,8},{10,11... | collective-permute-start | bytes 1572872 | tf_op jit(solution)/shard_map/ppermute | solution.py:270
  48.9 11.8 %copy-start.7 = (f32[2048]{0:T(1024)S(1)}, f32[2048]{0:T(1024)}, u32[]{:S(2)}) copy-start(f32[2048]{0:T(1024)} %param.7) | copy-start | bytes 24580
  60.7 1.9 %copy-start.5 = (bf16[3,2048,256]{2,1,0:T(8,128)(2,1)S(1)}, bf16[3,2048,256]{2,1,0:T(8,128)(2,1)}, u32[]{:S(2)}) copy-start(bf16[3,2048,256]{2,1,0:T(8,128)(2,1)} %refs_6_.3) | copy-start | bytes 9437188
  67.8 13.8 %collective-permute-start.6 = (bf16[512,512]{1,0:T(8,128)(2,1)S(1)}, bf16[512,512]{1,0:T(8,128)(2,1)}, u32[]{:S(2)}, u32[]{:S(2)}) collective-permute-start(bf16[512,512]{1,0:T(8,128)(2,1)S(1)} %bitcast.17), channel_id=1, source_target_pairs={{0,2},{1,3},{2,0},{3,1},{4,6},{5,7},{6,4},{7,5},{8,10},{9,11},{10,... | collective-permute-start | bytes 1572872 | tf_op jit(solution)/shard_map/ppermute | solution.py:267
  68.1 14.3 %collective-permute-start.7 = (bf16[512,512]{1,0:T(8,128)(2,1)S(1)}, bf16[512,512]{1,0:T(8,128)(2,1)}, u32[]{:S(2)}, u32[]{:S(2)}) collective-permute-start(bf16[512,512]{1,0:T(8,128)(2,1)S(1)} %bitcast.18), channel_id=1, source_target_pairs={{0,1},{1,0},{2,3},{3,2},{4,5},{5,4},{6,7},{7,6},{8,9},{9,8},{10,11... | collective-permute-start | bytes 1572872 | tf_op jit(solution)/shard_map/ppermute | solution.py:270
  68.6 25.7 %all-to-all-start.2 = ((bf16[64,8,256]{2,1,0:T(8,128)(2,1)}), bf16[64,8,256]{2,1,0:T(8,128)(2,1)S(1)}, u32[]{:S(2)}, u32[]{:S(2)}) async-start(bf16[64,8,256]{2,1,0:T(8,128)(2,1)} %bitcast.6), calls=%async_computation.2 | async-start | bytes 524288 | tf_op jit(solution)/shard_map/all_to_all | solution.py:273
  81.7 2.4 %copy-start.6 = (bf16[3,2048,256]{2,1,0:T(8,128)(2,1)S(1)}, bf16[3,2048,256]{2,1,0:T(8,128)(2,1)}, u32[]{:S(2)}) copy-start(bf16[3,2048,256]{2,1,0:T(8,128)(2,1)} %refs_6_.3) | copy-start | bytes 9437188
  81.7 2.3 %collective-permute-start.8 = (bf16[512,512]{1,0:T(8,128)(2,1)}, bf16[512,512]{1,0:T(8,128)(2,1)S(1)}, u32[]{:S(2)}, u32[]{:S(2)}) collective-permute-start(bf16[512,512]{1,0:T(8,128)(2,1)} %collective-permute-done.6.refs_2_), channel_id=1, source_target_pairs={{0,1},{1,0},{2,3},{3,2},{4,5},{5,4},{6,7},{7,6},{8,9},{9,8},{10,11... | collective-permute-start | bytes 1572872 | tf_op jit(solution)/shard_map/ppermute | solution.py:270
  82.3 11.9 %copy-start = (bf16[256,2048]{1,0:T(8,128)(2,1)S(1)}, bf16[256,2048]{1,0:T(8,128)(2,1)}, u32[]{:S(2)}) copy-start(bf16[256,2048]{1,0:T(8,128)(2,1)} %refs_3_.11) | copy-start | bytes 3145732
  82.4 11.9 %copy-start.1 = (bf16[256,2048]{1,0:T(8,128)(2,1)S(1)}, bf16[256,2048]{1,0:T(8,128)(2,1)}, u32[]{:S(2)}) copy-start(bf16[256,2048]{1,0:T(8,128)(2,1)} %refs_4_.11) | copy-start | bytes 3145732
  82.4 11.9 %copy-start.3 = (bf16[512,256]{1,0:T(8,128)(2,1)S(1)}, bf16[512,256]{1,0:T(8,128)(2,1)}, u32[]{:S(2)}) copy-start(bf16[512,256]{1,0:T(8,128)(2,1)} %get-tuple-element.27.refs_1_) | copy-start | bytes 786436
  94.3 25.8 %copy-start.4 = (bf16[512,256]{1,0:T(8,128)(2,1)S(1)}, bf16[512,256]{1,0:T(8,128)(2,1)}, u32[]{:S(2)}) copy-start(bf16[512,256]{1,0:T(8,128)(2,1)} %get-tuple-element.31.refs_1_) | copy-start | bytes 786436
  95.0 3.5 %collective-permute-start.10 = (bf16[512,512]{1,0:T(8,128)(2,1)S(1)}, bf16[512,512]{1,0:T(8,128)(2,1)S(1)}, u32[]{:S(2)}, u32[]{:S(2)}) collective-permute-start(bf16[512,512]{1,0:T(8,128)(2,1)S(1)} %get-tuple-element.32), channel_id=1, source_target_pairs={{0,1},{1,0},{2,3},{3,2},{4,5},{5,4},{6,7},{7,6},{8,9},{9,8},{10,11... | collective-permute-start | bytes 1572872 | tf_op jit(solution)/shard_map/ppermute | solution.py:270
  99.0 21.1 %collective-permute-start.11 = (bf16[512,512]{1,0:T(8,128)(2,1)S(1)}, bf16[512,512]{1,0:T(8,128)(2,1)S(1)}, u32[]{:S(2)}, u32[]{:S(2)}) collective-permute-start(bf16[512,512]{1,0:T(8,128)(2,1)S(1)} %shard_map.70), channel_id=1, source_target_pairs={{0,2},{1,3},{2,0},{3,1},{4,6},{5,7},{6,4},{7,5},{8,10},{9,11},{10,... | collective-permute-start | bytes 1572872 | tf_op jit(solution)/shard_map/ppermute | solution.py:267
  120.8 4.9 %collective-permute-start.12 = (bf16[512,512]{1,0:T(8,128)(2,1)S(1)}, bf16[512,512]{1,0:T(8,128)(2,1)S(1)}, u32[]{:S(2)}, u32[]{:S(2)}) collective-permute-start(bf16[512,512]{1,0:T(8,128)(2,1)S(1)} %get-tuple-element.33), channel_id=1, source_target_pairs={{0,1},{1,0},{2,3},{3,2},{4,5},{5,4},{6,7},{7,6},{8,9},{9,8},{10,11... | collective-permute-start | bytes 1572872 | tf_op jit(solution)/shard_map/ppermute | solution.py:270
  124.1 3.5 %collective-permute-start.9 = (bf16[512,512]{1,0:T(8,128)(2,1)S(1)}, bf16[512,512]{1,0:T(8,128)(2,1)S(1)}, u32[]{:S(2)}, u32[]{:S(2)}) collective-permute-start(bf16[512,512]{1,0:T(8,128)(2,1)S(1)} %get-tuple-element.30), channel_id=1, source_target_pairs={{0,1},{1,0},{2,3},{3,2},{4,5},{5,4},{6,7},{7,6},{8,9},{9,8},{10,11... | collective-permute-start | bytes 1572872 | tf_op jit(solution)/shard_map/ppermute | solution.py:270
  124.2 3.9 %collective-permute-start.13 = (bf16[512,512]{1,0:T(8,128)(2,1)S(1)}, bf16[512,512]{1,0:T(8,128)(2,1)S(1)}, u32[]{:S(2)}, u32[]{:S(2)}) collective-permute-start(bf16[512,512]{1,0:T(8,128)(2,1)S(1)} %get-tuple-element.34), channel_id=1, source_target_pairs={{0,1},{1,0},{2,3},{3,2},{4,5},{5,4},{6,7},{7,6},{8,9},{9,8},{10,11... | collective-permute-start | bytes 1572872 | tf_op jit(solution)/shard_map/ppermute | solution.py:270
  126.1 13.2 %collective-permute-start.14 = (bf16[512,512]{1,0:T(8,128)(2,1)S(1)}, bf16[512,512]{1,0:T(8,128)(2,1)S(1)}, u32[]{:S(2)}, u32[]{:S(2)}) collective-permute-start(bf16[512,512]{1,0:T(8,128)(2,1)S(1)} %shard_map.72.refs_6_), channel_id=1, source_target_pairs={{0,2},{1,3},{2,0},{3,1},{4,6},{5,7},{6,4},{7,5},{8,10},{9,11},{10,... | collective-permute-start | bytes 1572872 | tf_op jit(solution)/shard_map/ppermute | solution.py:267
  128.1 11.2 %copy-start.2 = (bf16[2,512,512]{2,1,0:T(8,128)(2,1)S(1)}, bf16[2,512,512]{2,1,0:T(8,128)(2,1)}, u32[]{:S(2)}) copy-start(bf16[2,512,512]{2,1,0:T(8,128)(2,1)} %refs_0_.3) | copy-start | bytes 3145732

commit v4 on v3

--- a/solution.py
+++ b/solution.py
@@ -114,7 +114,7 @@
         out_ref[i * tile : (i + 1) * tile, out_at] = (out / total).astype(BF16)
 
 
-def permute_kernel(samples_hbm, out0_hbm, out1_hbm, in_ref, out_ref, sems):
+def permute_kernel(samples_hbm, out0_hbm, out1_hbm, row0_hbm, row1_hbm, in_ref, out_ref, sems):
     cols = samples_hbm.shape[1]
     step = cols // 4
     spans = [pl.ds(i * step, step) for i in range(4)]
@@ -122,6 +122,7 @@
     leaving = []
     for i, at in enumerate(spans):
         arriving[i].wait()
+        leaving += fetch([in_ref.at[r, at] for r in range(2)], [o.at[at] for o in (row0_hbm, row1_hbm)], sems.at[5 + i])
         halves = interleave(in_ref[0, at, :].astype(F32), in_ref[1, at, :].astype(F32))
         for k, half in enumerate(halves):
             out_ref[k, at, :] = half.astype(BF16)
@@ -131,16 +132,16 @@
 
 
 def permute(samples):
-    outs = (sds(samples.shape[1:]),) * 2
+    outs = (sds(samples.shape[1:]),) * 4
     return pl.pallas_call(
         permute_kernel,
         out_shape=outs,
         in_specs=[ANY],
-        out_specs=(ANY, ANY),
+        out_specs=(ANY,) * 4,
         scratch_shapes=[
             pltpu.VMEM(samples.shape, BF16),
             pltpu.VMEM(samples.shape, BF16),
-            pltpu.SemaphoreType.DMA((5, 4)),
+            pltpu.SemaphoreType.DMA((9, 4)),
         ],
         compiler_params=params(WHOLE),
         cost_estimate=cost(samples.size, [samples, *outs]),
@@ -193,24 +194,24 @@
     heads(qkv_ref, OWNED - 1, attn_ref)
 
 
-def row_kernel(h_ref, *refs):
-    parts_hbm, gain_hbm, w_hbm = refs[:4], refs[4], refs[5]
-    x_ref, held_ref, gain_ref, w_ref, qkv_ref, sems = refs[-6:]
-    outs_hbm = refs[-8:-6]
-    first = fetch([gain_hbm] + [p.at[0] for p in parts_hbm], [gain_ref] + [x_ref.at[0, i] for i in range(4)], sems)
-    weights = fetch([w_hbm], [w_ref], sems.at[5:])
-    second = fetch([p.at[1] for p in parts_hbm], [x_ref.at[1, i] for i in range(4)], sems.at[6:])
-    for row, ready, copies in ((0, first, weights), (1, second, ())):
-        for copy in ready:
-            copy.wait()
-        norm_project(h_ref[0], [x_ref.at[row, i] for i in range(4)], gain_ref, w_ref, copies, qkv_ref)
-        heads(qkv_ref, 0, held_ref.at[row])
-    halves = interleave(held_ref[0].astype(F32), held_ref[1].astype(F32))
-    leaving = []
-    for i, half in enumerate(halves):
-        held_ref[2 + i] = half.astype(BF16)
-        leaving += fetch([held_ref.at[2 + i]], [outs_hbm[i]], sems.at[i:])
-    for copy in leaving:
+def row_kernel(row, n_more, h_ref, *refs):
+    parts_hbm, more_hbm, (gain_hbm, w_hbm) = refs[:4], refs[4 : 4 + n_more], refs[4 + n_more : 6 + n_more]
+    n_out = 2 if n_more else 1
+    x_ref, held_ref, gain_ref, w_ref, qkv_ref, sems, more_sems = refs[-7:]
+    outs_hbm = refs[-7 - n_out : -7]
+    ready = fetch([gain_hbm, parts_hbm[0].at[row], *parts_hbm[1:]], [gain_ref] + [x_ref.at[i] for i in range(4)], sems)
+    copies = fetch([w_hbm], [w_ref], sems.at[5:])
+    earlier = fetch(more_hbm, [held_ref.at[0]], more_sems)
+    for copy in ready:
+        copy.wait()
+    norm_project(h_ref[0], [x_ref.at[i] for i in range(4)], gain_ref, w_ref, copies, qkv_ref)
+    heads(qkv_ref, 0, held_ref.at[n_more])
+    if n_more:
+        earlier[0].wait()
+        halves = interleave(held_ref[0].astype(F32), held_ref[1].astype(F32))
+        for i, half in enumerate(halves):
+            held_ref[i] = half.astype(BF16)
+    for copy in fetch([held_ref.at[i] for i in range(n_out)], outs_hbm, more_sems):
         copy.wait()
 
 
@@ -239,18 +240,34 @@
     own_ref[...] = own + r0_ref[...].astype(F32)
 
 
-def final_kernel(samples_ref, own0_ref, rx0_ref, own1_ref, rx1_ref, out_ref):
-    cols = samples_ref.shape[1]
-    step = min(64, cols)
-
-    @pl.loop(0, cols // step)
-    def _(i):
-        at = pl.ds(pl.multiple_of(i * step, step), step)
+def final_kernel(samples_ref, own0_ref, rx0_ref, own1_ref, rx1_ref, out_hbm, out_ref, sems):
+    pieces = sems.shape[0]
+    step = samples_ref.shape[1] // pieces
+    leaving = []
+    for i in range(pieces):
+        at = slice(i * step, (i + 1) * step)
         pair = deinterleave(
             own0_ref[at, :] + rx0_ref[at, :].astype(F32), own1_ref[at, :] + rx1_ref[at, :].astype(F32)
         )
         for r in range(2):
             out_ref[r, at, :] = (samples_ref[r, at, :].astype(F32) + pair[r]).astype(BF16)
+        leaving += fetch([out_ref.at[:, at]], [out_hbm.at[:, at]], sems.at[i:])
+    for copy in leaving:
+        copy.wait()
+
+
+def final(*ins):
+    samples = ins[0]
+    pieces = min(8, samples.shape[1] // 16)
+    return pl.pallas_call(
+        final_kernel,
+        out_shape=sds(samples.shape),
+        in_specs=[VM] * len(ins),
+        out_specs=ANY,
+        scratch_shapes=[pltpu.VMEM(samples.shape, BF16), pltpu.SemaphoreType.DMA((pieces,))],
+        compiler_params=params(ROOMY),
+        cost_estimate=cost(samples.size, [*ins, samples]),
+    )(*ins)
 
 
 def shards(samples, norm_gain, row_qkv, col_qkv, row_out, col_out):
@@ -290,24 +307,25 @@
             after,
         )[0]
 
-    def both_rows(parts, after, weight):
-        outs = (sds((tokens, wide)),) * 2
+    def row(r, parts, more, after, weight):
+        outs = tuple([sds((tokens, wide))] * (1 + len(more)))
         return pl.pallas_call(
-            row_kernel,
+            functools.partial(row_kernel, r, len(more)),
             out_shape=outs,
-            in_specs=[SM] + [ANY] * (6 + len(after)),
-            out_specs=(ANY, ANY),
+            in_specs=[SM] + [ANY] * (6 + len(more) + len(after)),
+            out_specs=tuple([ANY] * len(outs)),
             scratch_shapes=[
-                pltpu.VMEM((2, 4, tokens, width), BF16),
-                pltpu.VMEM((4, tokens, wide), BF16),
+                pltpu.VMEM((4, tokens, width), BF16),
+                pltpu.VMEM((2, tokens, wide), BF16),
                 pltpu.VMEM(gain.shape, F32),
                 pltpu.VMEM(row_qkv.shape, BF16),
                 pltpu.VMEM((tokens, 3 * wide), BF16),
-                dma((10,)),
+                dma((6,)),
+                dma((2,)),
             ],
             compiler_params=params(WHOLE),
-            cost_estimate=cost(2 * flops, parts, weight),
-        )(h, *parts, gain, row_qkv, *after)
+            cost_estimate=cost(flops, parts, weight),
+        )(h, *parts, *more, gain, row_qkv, *after)
 
     piece = 4 * tokens * wide * width
 
@@ -322,13 +340,17 @@
 
         return own, s2, over_chip(s2)
 
-    every = gather(samples)
-    mixed0, mixed1 = permute(samples)
+    mixed0, mixed1, first, second = permute(samples)
     start0 = exchange(mixed0)
+    parts = gather(first)
+    (row0,) = row(0, (samples, *parts[1:]), (), (), 1)
+    second, _ = lax.optimization_barrier((second, parts[1]))
+    parts = gather(second)
+    start0, row0 = lax.optimization_barrier((start0, row0))
     chip0 = over_chip(start0)
     mixed1, start0 = lax.optimization_barrier((mixed1, start0))
     start1 = exchange(mixed1)
-    rows0, rows1 = both_rows(every, (), 1)
+    rows0, rows1 = row(1, (samples, *parts[1:]), (row0,), (), 1)
     core0, diagonal0 = over_core(start0), over_core(chip0)
     start0, rows0 = lax.optimization_barrier((start0, rows0))
     attn0 = cols((start0, chip0, core0, diagonal0), ())
@@ -342,7 +364,7 @@
     own1, s1, rx1 = out(rows1, back1, (rx0,), ())
     own0 = own0((s1,))
     own1 = own1((own0,))
-    return call(final_kernel, (), (samples, own0, rx0, own1, rx1), (), (sds(samples.shape),), samples.size)[0]
+    return final(samples, own0, rx0, own1, rx1)
 
 
 def solution(mesh):

time: 141 us -> 141 us (level)
  waiting for transfers between devices: 29.8 us -> 26.6 us
  Pallas kernels: 29.5 us -> 32.2 us
  local copies, waits for them, and re-layouts: 1.92 us -> 3.52 us
    ppermute x5 -> x6, waiting for transfers between devices: 17.8 us -> 11.9 us  [over_chip(): return lax.ppermute(x, 'head', [(i, i ^ 2) for i in range(4)])]
    ppermute x10 -> x12, starting transfers between devices: 14.6 us -> 18.8 us  [over_core(): return lax.ppermute(x, 'head', [(i, i ^ 1) for i in range(4)])]
    all_to_all x3, starting transfers between devices: 39.9 us -> 36 us  [exchange(): return lax.all_to_all(x, 'row', 0, 0, tiled=True)]
    pallas_call x1 -> x3, Pallas kernels: 11.8 us -> 15.5 us  [the longest x2 14.3 us: row(): pl.pallas_call(functools.partial(row_kernel, r, len(more)), out_shape=out...]
    ppermute x10 -> x12, waiting for transfers between devices: 4.22 us -> 6.87 us  [over_core(): return lax.ppermute(x, 'head', [(i, i ^ 1) for i in range(4)])]
    ppermute x5 -> x6, starting transfers between devices: 4.83 us -> 3.18 us  [over_chip(): return lax.ppermute(x, 'head', [(i, i ^ 2) for i in range(4)])]
    unnamed x16 -> x26, local copies, waits for them, and re-layouts: 1.92 us -> 3.52 us
    pallas_call x10 -> x9, Pallas kernels: 15.6 us -> 14.1 us  [call(): pl.pallas_call(kernel, out_shape=tuple(outs), in_specs=[SM] * len(scalars...]
  transfers between devices with their start and end apart: 18 -> 21, of which waited for: 7 -> 11; matrix products, arithmetic and copies ran while one was open for 0% -> 0% of each run, Pallas kernels for 19% -> 19%
where the time goes in v4:
time: 141 us; the launch traced here: 140 us
  starting transfers between devices  58 us (41%)
  Pallas kernels  32.2 us (23%)
  waiting for transfers between devices  26.6 us (19%)
  blocking collectives  19.4 us (14%)
  local copies, waits for them, and re-layouts  3.52 us (2%)
    all_to_all x3, starting transfers between devices, exchange(): return lax.all_to_all(x, 'row', 0, 0, tiled=True)  36 us
    all_to_all x1, blocking collectives, exchange(): return lax.all_to_all(x, 'row', 0, 0, tiled=True)  19.4 us
    ppermute x12, starting transfers between devices, over_core(): return lax.ppermute(x, 'head', [(i, i ^ 1) for i in range(4)])  18.8 us
    pallas_call x2, Pallas kernels, row(): pl.pallas_call(functools.partial(row_kernel, r, len(more)), out_shape=out...  14.3 us
    pallas_call x9, Pallas kernels, call(): pl.pallas_call(kernel, out_shape=tuple(outs), in_specs=[SM] * len(scalars...  14.1 us
    ppermute x6, waiting for transfers between devices, over_chip(): return lax.ppermute(x, 'head', [(i, i ^ 2) for i in range(4)])  11.9 us
    all_to_all x3, waiting for transfers between devices, exchange(): return lax.all_to_all(x, 'row', 0, 0, tiled=True)  7.78 us
    ppermute x12, waiting for transfers between devices, over_core(): return lax.ppermute(x, 'head', [(i, i ^ 1) for i in range(4)])  6.87 us
  transfers between devices with their start and end apart: 21, of which 11 were waited for; matrix products, arithmetic and copies ran while one was open for 0% of the time, Pallas kernels for 19%

profile of v4, /device:TPU:1, one launch (start us, length us, event | category | flops | bytes accessed | tf_op | source)
XLA Modules:
  0.0 140.1 jit_solution(1938763015841955811)
XLA Ops:
  0.0 2.6 %shard_map.64 = (bf16[512,512]{1,0:T(8,128)(2,1)}, bf16[512,512]{1,0:T(8,128)(2,1)}, bf16[512,512]{1,0:T(8,128)(2,1)}, bf16[512,512]{1,0:T(8,128)(2,1)}) custom-call(bf16[2,512,512]{2,1,0:T(8,128)(2,1)} %samples_ref.1), custom_call_target="tpu_custom_call" | custom-call | flops 524288 | bytes 3145728 | tf_op jit(solution)/shard_map/pallas_call | solution.py:136
  2.6 2.1 %collective-permute-start = (bf16[512,512]{1,0:T(8,128)(2,1)}, bf16[512,512]{1,0:T(8,128)(2,1)S(1)}, u32[]{:S(2)}, u32[]{:S(2)}) collective-permute-start(bf16[512,512]{1,0:T(8,128)(2,1)} %get-tuple-element.27), channel_id=1, source_target_pairs={{0,2},{1,3},{2,0},{3,1},{4,6},{5,7},{6,4},{7,5},{8,10},{9,11},{10,... | collective-permute-start | bytes 1572872 | tf_op jit(solution)/shard_map/ppermute | solution.py:284
  4.7 14.0 %all-to-all-start = ((bf16[64,8,512]{2,1,0:T(8,128)(2,1)}), bf16[64,8,512]{2,1,0:T(8,128)(2,1)S(1)}, u32[]{:S(2)}, u32[]{:S(2)}) async-start(bf16[64,8,512]{2,1,0:T(8,128)(2,1)} %bitcast.28), calls=%async_computation | async-start | bytes 1048576 | tf_op jit(solution)/shard_map/all_to_all | solution.py:290
  18.7 1.3 collective-permute-start.1
  20.0 0.0 collective-permute-done.refs_1_
  20.0 0.1 collective-permute-start.2
  20.1 0.0 collective-permute-start.3
  20.1 1.6 %collective-permute-done.1.refs_2_ = bf16[512,512]{1,0:T(8,128)(2,1)S(1)} collective-permute-done((bf16[512,512]{1,0:T(8,128)(2,1)}, bf16[512,512]{1,0:T(8,128)(2,1)S(1)}, u32[]{:S(2)}, u32[]{:S(2)}) %collective-permute-start.1) | collective-permute-done | bytes 524320 | tf_op jit(solution)/shard_map/ppermute | solution.py:287
  21.8 0.5 collective-permute-done.2.refs_3_
  22.3 0.3 copy-done.11
  22.6 0.5 copy-done.12
  23.1 7.1 %shard_map.65.refs_4_ = bf16[512,256]{1,0:T(8,128)(2,1)} custom-call(s32[1]{0:T(128)} %bitcast.h_ref.refs_0_, bf16[2,512,512]{2,1,0:T(8,128)(2,1)} %samples_ref.1, bf16[512,512]{1,0:T(8,128)(2,1)} %copy-done.9, bf16[512,512]{1,0:T(8,128)(2,1)} %copy-done.11, bf16[512,512]{1,0:T(8,128)(2,1)} %copy-done.12, f32[1,2048]{1,0:T(1,128)} %bitcast.24, ...), custom_call_target="tpu_custom_call" | custom-call | flops 1879048192 | bytes 2621440 | tf_op jit(solution)/shard_map/pallas_call | solution.py:312
  30.2 3.9 %all-to-all-done = bf16[64,8,512]{2,1,0:T(8,128)(2,1)S(1)} async-done(((bf16[64,8,512]{2,1,0:T(8,128)(2,1)}), bf16[64,8,512]{2,1,0:T(8,128)(2,1)S(1)}, u32[]{:S(2)}, u32[]{:S(2)}) %all-to-all-start) | async-done | bytes 524320 | tf_op jit(solution)/shard_map/all_to_all | solution.py:290
  34.1 0.0 collective-permute-start.6
  34.1 9.1 %all-to-all-start.1 = ((bf16[64,8,512]{2,1,0:T(8,128)(2,1)}), bf16[64,8,512]{2,1,0:T(8,128)(2,1)S(1)}, u32[]{:S(2)}, u32[]{:S(2)}) async-start(bf16[64,8,512]{2,1,0:T(8,128)(2,1)} %bitcast.4), calls=%async_computation.1 | async-start | bytes 1048576 | tf_op jit(solution)/shard_map/all_to_all | solution.py:290
  43.3 0.0 copy-start.7
  43.3 2.3 %collective-permute-start.4 = (bf16[512,512]{1,0:T(8,128)(2,1)S(1)}, bf16[512,512]{1,0:T(8,128)(2,1)S(1)}, u32[]{:S(2)}, u32[]{:S(2)}) collective-permute-start(bf16[512,512]{1,0:T(8,128)(2,1)S(1)} %copy-done.8), channel_id=1, source_target_pairs={{0,1},{1,0},{2,3},{3,2},{4,5},{5,4},{6,7},{7,6},{8,9},{9,8},{10,11... | collective-permute-start | bytes 1572872 | tf_op jit(solution)/shard_map/ppermute | solution.py:287
  45.6 0.0 collective-permute-done.3.refs_1_
  45.6 0.1 collective-permute-start.5
  45.7 0.4 collective-permute-start.7
  46.1 0.2 collective-permute-done.6.refs_2_
  46.3 6.9 %collective-permute-start.8 = (bf16[512,512]{1,0:T(8,128)(2,1)S(1)}, bf16[512,512]{1,0:T(8,128)(2,1)S(1)}, u32[]{:S(2)}, u32[]{:S(2)}) collective-permute-start(bf16[512,512]{1,0:T(8,128)(2,1)S(1)} %collective-permute-done.6.refs_2_), channel_id=1, source_target_pairs={{0,1},{1,0},{2,3},{3,2},{4,5},{5,4},{6,7},{7,6},{8,9},{9,8},{10,11... | collective-permute-start | bytes 1572872 | tf_op jit(solution)/shard_map/ppermute | solution.py:287
  53.2 0.0 collective-permute-done.4.refs_2_
  53.2 0.8 copy-done.10
  54.0 0.0 collective-permute-done.5.refs_3_
  54.0 7.3 %shard_map.66 = (bf16[512,256]{1,0:T(8,128)(2,1)}, bf16[512,256]{1,0:T(8,128)(2,1)}) custom-call(s32[1]{0:T(128)} %bitcast.h_ref.refs_0_, bf16[2,512,512]{2,1,0:T(8,128)(2,1)} %samples_ref.1, bf16[512,512]{1,0:T(8,128)(2,1)} %collective-permute-done.3.refs_1_, bf16[512,512]{1,0:T(8,128)(2,1)} %copy-done.10, bf16[512,512]{1,0:T(8,128)(2,1)} %collective-permute-done.5.refs_3_, ...), custom_call_target="tpu_custom_call" | custom-call | flops 1879048192 | bytes 2621440 | tf_op jit(solution)/shard_map/pallas_call | solution.py:312
  61.3 0.0 collective-permute-done.7.refs_3_
  61.3 0.0 collective-permute-done.8.refs_4_
  61.3 0.0 copy-start.5
  61.3 1.9 %copy-done.5 = bf16[3,2048,256]{2,1,0:T(8,128)(2,1)S(1)} copy-done((bf16[3,2048,256]{2,1,0:T(8,128)(2,1)S(1)}, bf16[3,2048,256]{2,1,0:T(8,128)(2,1)}, u32[]{:S(2)}) %copy-start.5) | copy-done | bytes 3145752
  63.2 5.2 %shard_map.67 = bf16[512,256]{1,0:T(8,128)(2,1)} custom-call(s32[1]{0:T(128)} %bitcast.h_ref.refs_0_, bf16[512,512]{1,0:T(8,128)(2,1)S(1)} %bitcast.19, bf16[512,512]{1,0:T(8,128)(2,1)S(1)} %collective-permute-done.6.refs_2_, bf16[512,512]{1,0:T(8,128)(2,1)S(1)} %collective-permute-done.7.refs_3_, bf16[512,512]{1,0:T(8,128)(2,1)S(1)} %collective-permute-done.8.refs_4_, ...), custom_call_target="tpu_custom_call" | custom-call | flops 1879048192 | bytes 5513216 | tf_op jit(solution)/shard_map/pallas_call | solution.py:38
  68.4 0.0 all-to-all-done.1
  68.4 0.9 collective-permute-start.9
  69.3 0.3 collective-permute-start.10
  69.6 12.8 %all-to-all-start.2 = ((bf16[64,8,256]{2,1,0:T(8,128)(2,1)}), bf16[64,8,256]{2,1,0:T(8,128)(2,1)S(1)}, u32[]{:S(2)}, u32[]{:S(2)}) async-start(bf16[64,8,256]{2,1,0:T(8,128)(2,1)} %bitcast.6), calls=%async_computation.2 | async-start | bytes 524288 | tf_op jit(solution)/shard_map/all_to_all | solution.py:290
  82.4 0.0 copy-start.6
  82.4 0.0 collective-permute-done.9.refs_2_
  82.4 0.8 collective-permute-start.11
  83.2 0.1 shard_map.68.refs_7_
  83.3 0.0 copy-start
  83.3 0.0 copy-start.1
  83.3 1.6 %collective-permute-done.11.refs_4_ = bf16[512,512]{1,0:T(8,128)(2,1)S(1)} collective-permute-done((bf16[512,512]{1,0:T(8,128)(2,1)}, bf16[512,512]{1,0:T(8,128)(2,1)S(1)}, u32[]{:S(2)}, u32[]{:S(2)}) %collective-permute-start.11) | collective-permute-done | bytes 524320 | tf_op jit(solution)/shard_map/ppermute | solution.py:287
  85.0 5.7 %shard_map.69.refs_5_ = bf16[512,256]{1,0:T(8,128)(2,1)S(1)} custom-call(s32[1]{0:T(128)} %bitcast.h_ref.refs_0_, bf16[512,512]{1,0:T(8,128)(2,1)S(1)} %bitcast.23, bf16[512,512]{1,0:T(8,128)(2,1)} %collective-permute-done.9.refs_2_, bf16[512,512]{1,0:T(8,128)(2,1)} %collective-permute-done.10.refs_3_, bf16[512,512]{1,0:T(8,128)(2,1)S(1)} %collective-permute-done.11.refs_4_, ...), custom_call_target="tpu_custom_call" | custom-call | flops 1879048192 | bytes 5775360 | tf_op jit(solution)/shard_map/pallas_call | solution.py:38
  90.6 3.8 %all-to-all-done.2 = bf16[64,8,256]{2,1,0:T(8,128)(2,1)S(1)} async-done(((bf16[64,8,256]{2,1,0:T(8,128)(2,1)}), bf16[64,8,256]{2,1,0:T(8,128)(2,1)S(1)}, u32[]{:S(2)}, u32[]{:S(2)}) %all-to-all-start.2) | async-done | bytes 262176 | tf_op jit(solution)/shard_map/all_to_all | solution.py:290
  94.5 0.7 shard_map.70
  95.2 2.8 %collective-permute-start.13 = (bf16[512,512]{1,0:T(8,128)(2,1)S(1)}, bf16[512,512]{1,0:T(8,128)(2,1)S(1)}, u32[]{:S(2)}, u32[]{:S(2)}) collective-permute-start(bf16[512,512]{1,0:T(8,128)(2,1)S(1)} %get-tuple-element.42), channel_id=1, source_target_pairs={{0,1},{1,0},{2,3},{3,2},{4,5},{5,4},{6,7},{7,6},{8,9},{9,8},{10,11... | collective-permute-start | bytes 1572872 | tf_op jit(solution)/shard_map/ppermute | solution.py:287
  98.0 1.5 %collective-permute-done.13.refs_5_ = bf16[512,512]{1,0:T(8,128)(2,1)S(1)} collective-permute-done((bf16[512,512]{1,0:T(8,128)(2,1)S(1)}, bf16[512,512]{1,0:T(8,128)(2,1)S(1)}, u32[]{:S(2)}, u32[]{:S(2)}) %collective-permute-start.13) | collective-permute-done | bytes 524320 | tf_op jit(solution)/shard_map/ppermute | solution.py:287
  99.5 0.4 shard_map.71
  100.0 0.1 collective-permute-start.14
  100.1 19.4 %all_to_all.46 = bf16[64,8,256]{2,1,0:T(8,128)(2,1)S(1)} all-to-all(bf16[64,8,256]{2,1,0:T(8,128)(2,1)S(1)} %bitcast.16), channel_id=1, replica_groups=mesh['row'=64,'head'=4] {'row'}, dimensions={0} | all-to-all | bytes 524288 | tf_op jit(solution)/shard_map/all_to_all | solution.py:290
  119.5 0.7 shard_map.72
  120.2 3.3 %collective-permute-start.15 = (bf16[512,512]{1,0:T(8,128)(2,1)S(1)}, bf16[512,512]{1,0:T(8,128)(2,1)S(1)}, u32[]{:S(2)}, u32[]{:S(2)}) collective-permute-start(bf16[512,512]{1,0:T(8,128)(2,1)S(1)} %get-tuple-element.43), channel_id=1, source_target_pairs={{0,1},{1,0},{2,3},{3,2},{4,5},{5,4},{6,7},{7,6},{8,9},{9,8},{10,11... | collective-permute-start | bytes 1572872 | tf_op jit(solution)/shard_map/ppermute | solution.py:287
  123.6 0.1 collective-permute-start.12
  123.7 0.4 collective-permute-start.16
  124.1 1.0 collective-permute-done.15.refs_5_
  125.1 0.4 shard_map.73.refs_6_
  125.5 0.1 collective-permute-start.17
  125.6 0.2 collective-permute-done.12.refs_5_
  125.8 0.4 shard_map.74.refs_6_.own0_ref
  126.3 0.0 copy-start.2
  126.3 0.3 collective-permute-done.16.refs_5_
  126.6 0.4 shard_map.75.own1_ref
  127.0 11.7 %collective-permute-done.17.rx1_ref = bf16[512,512]{1,0:T(8,128)(2,1)S(1)} collective-permute-done((bf16[512,512]{1,0:T(8,128)(2,1)S(1)}, bf16[512,512]{1,0:T(8,128)(2,1)S(1)}, u32[]{:S(2)}, u32[]{:S(2)}) %collective-permute-start.17) | collective-permute-done | bytes 524320 | tf_op jit(solution)/shard_map/ppermute | solution.py:284
  138.8 1.2 shard_map.76
  (18 shorter events, 0.0 us)
Async XLA Ops:
  2.6 17.5 %collective-permute-start = (bf16[512,512]{1,0:T(8,128)(2,1)}, bf16[512,512]{1,0:T(8,128)(2,1)S(1)}, u32[]{:S(2)}, u32[]{:S(2)}) collective-permute-start(bf16[512,512]{1,0:T(8,128)(2,1)} %get-tuple-element.27), channel_id=1, source_target_pairs={{0,2},{1,3},{2,0},{3,1},{4,6},{5,7},{6,4},{7,5},{8,10},{9,11},{10,... | collective-permute-start | bytes 1572872 | tf_op jit(solution)/shard_map/ppermute | solution.py:284
  4.7 29.4 %all-to-all-start = ((bf16[64,8,512]{2,1,0:T(8,128)(2,1)}), bf16[64,8,512]{2,1,0:T(8,128)(2,1)S(1)}, u32[]{:S(2)}, u32[]{:S(2)}) async-start(bf16[64,8,512]{2,1,0:T(8,128)(2,1)} %bitcast.28), calls=%async_computation | async-start | bytes 1048576 | tf_op jit(solution)/shard_map/all_to_all | solution.py:290
  18.7 3.1 %collective-permute-start.1 = (bf16[512,512]{1,0:T(8,128)(2,1)}, bf16[512,512]{1,0:T(8,128)(2,1)S(1)}, u32[]{:S(2)}, u32[]{:S(2)}) collective-permute-start(bf16[512,512]{1,0:T(8,128)(2,1)} %get-tuple-element.27), channel_id=1, source_target_pairs={{0,1},{1,0},{2,3},{3,2},{4,5},{5,4},{6,7},{7,6},{8,9},{9,8},{10,11... | collective-permute-start | bytes 1572872 | tf_op jit(solution)/shard_map/ppermute | solution.py:287
  20.0 2.3 %copy-start.9 = (bf16[512,512]{1,0:T(8,128)(2,1)}, bf16[512,512]{1,0:T(8,128)(2,1)S(1)}, u32[]{:S(2)}) copy-start(bf16[512,512]{1,0:T(8,128)(2,1)S(1)} %collective-permute-done.refs_1_) | copy-start | bytes 1572868
  20.0 2.3 %collective-permute-start.2 = (bf16[512,512]{1,0:T(8,128)(2,1)S(1)}, bf16[512,512]{1,0:T(8,128)(2,1)S(1)}, u32[]{:S(2)}, u32[]{:S(2)}) collective-permute-start(bf16[512,512]{1,0:T(8,128)(2,1)S(1)} %collective-permute-done.refs_1_), channel_id=1, source_target_pairs={{0,1},{1,0},{2,3},{3,2},{4,5},{5,4},{6,7},{7,6},{8,9},{9,8},{10,11... | collective-permute-start | bytes 1572872 | tf_op jit(solution)/shard_map/ppermute | solution.py:287
  20.1 25.5 %collective-permute-start.3 = (bf16[512,512]{1,0:T(8,128)(2,1)}, bf16[512,512]{1,0:T(8,128)(2,1)}, u32[]{:S(2)}, u32[]{:S(2)}) collective-permute-start(bf16[512,512]{1,0:T(8,128)(2,1)} %get-tuple-element.32), channel_id=1, source_target_pairs={{0,2},{1,3},{2,0},{3,1},{4,6},{5,7},{6,4},{7,5},{8,10},{9,11},{10,... | collective-permute-start | bytes 1572872 | tf_op jit(solution)/shard_map/ppermute | solution.py:284
  21.8 0.8 copy-start.11
  22.3 0.8 copy-start.12
  23.1 20.2 %copy-start.8 = (bf16[512,512]{1,0:T(8,128)(2,1)S(1)}, bf16[512,512]{1,0:T(8,128)(2,1)}, u32[]{:S(2)}) copy-start(bf16[512,512]{1,0:T(8,128)(2,1)} %get-tuple-element.32) | copy-start | bytes 1572868
  34.1 12.2 %collective-permute-start.6 = (bf16[512,512]{1,0:T(8,128)(2,1)S(1)}, bf16[512,512]{1,0:T(8,128)(2,1)S(1)}, u32[]{:S(2)}, u32[]{:S(2)}) collective-permute-start(bf16[512,512]{1,0:T(8,128)(2,1)S(1)} %bitcast.17), channel_id=1, source_target_pairs={{0,2},{1,3},{2,0},{3,1},{4,6},{5,7},{6,4},{7,5},{8,10},{9,11},{10,... | collective-permute-start | bytes 1572872 | tf_op jit(solution)/shard_map/ppermute | solution.py:284
  34.1 34.3 %all-to-all-start.1 = ((bf16[64,8,512]{2,1,0:T(8,128)(2,1)}), bf16[64,8,512]{2,1,0:T(8,128)(2,1)S(1)}, u32[]{:S(2)}, u32[]{:S(2)}) async-start(bf16[64,8,512]{2,1,0:T(8,128)(2,1)} %bitcast.4), calls=%async_computation.1 | async-start | bytes 1048576 | tf_op jit(solution)/shard_map/all_to_all | solution.py:290
  43.3 18.0 %copy-start.7 = (f32[2048]{0:T(1024)S(1)}, f32[2048]{0:T(1024)}, u32[]{:S(2)}) copy-start(f32[2048]{0:T(1024)} %param.7) | copy-start | bytes 24580
  43.3 9.9 %collective-permute-start.4 = (bf16[512,512]{1,0:T(8,128)(2,1)S(1)}, bf16[512,512]{1,0:T(8,128)(2,1)S(1)}, u32[]{:S(2)}, u32[]{:S(2)}) collective-permute-start(bf16[512,512]{1,0:T(8,128)(2,1)S(1)} %copy-done.8), channel_id=1, source_target_pairs={{0,1},{1,0},{2,3},{3,2},{4,5},{5,4},{6,7},{7,6},{8,9},{9,8},{10,11... | collective-permute-start | bytes 1572872 | tf_op jit(solution)/shard_map/ppermute | solution.py:287
  45.6 8.4 %collective-permute-start.5 = (bf16[512,512]{1,0:T(8,128)(2,1)}, bf16[512,512]{1,0:T(8,128)(2,1)}, u32[]{:S(2)}, u32[]{:S(2)}) collective-permute-start(bf16[512,512]{1,0:T(8,128)(2,1)} %collective-permute-done.3.refs_1_), channel_id=1, source_target_pairs={{0,1},{1,0},{2,3},{3,2},{4,5},{5,4},{6,7},{7,6},{8,9},{9,8},{10,11... | collective-permute-start | bytes 1572872 | tf_op jit(solution)/shard_map/ppermute | solution.py:287
  45.7 15.6 %collective-permute-start.7 = (bf16[512,512]{1,0:T(8,128)(2,1)S(1)}, bf16[512,512]{1,0:T(8,128)(2,1)S(1)}, u32[]{:S(2)}, u32[]{:S(2)}) collective-permute-start(bf16[512,512]{1,0:T(8,128)(2,1)S(1)} %bitcast.18), channel_id=1, source_target_pairs={{0,1},{1,0},{2,3},{3,2},{4,5},{5,4},{6,7},{7,6},{8,9},{9,8},{10,11... | collective-permute-start | bytes 1572872 | tf_op jit(solution)/shard_map/ppermute | solution.py:287
  46.3 15.0 %collective-permute-start.8 = (bf16[512,512]{1,0:T(8,128)(2,1)S(1)}, bf16[512,512]{1,0:T(8,128)(2,1)S(1)}, u32[]{:S(2)}, u32[]{:S(2)}) collective-permute-start(bf16[512,512]{1,0:T(8,128)(2,1)S(1)} %collective-permute-done.6.refs_2_), channel_id=1, source_target_pairs={{0,1},{1,0},{2,3},{3,2},{4,5},{5,4},{6,7},{7,6},{8,9},{9,8},{10,11... | collective-permute-start | bytes 1572872 | tf_op jit(solution)/shard_map/ppermute | solution.py:287
  53.2 0.8 copy-start.10
  61.3 1.9 %copy-start.5 = (bf16[3,2048,256]{2,1,0:T(8,128)(2,1)S(1)}, bf16[3,2048,256]{2,1,0:T(8,128)(2,1)}, u32[]{:S(2)}) copy-start(bf16[3,2048,256]{2,1,0:T(8,128)(2,1)} %refs_6_.5) | copy-start | bytes 9437188
  68.4 14.0 %collective-permute-start.9 = (bf16[512,512]{1,0:T(8,128)(2,1)S(1)}, bf16[512,512]{1,0:T(8,128)(2,1)}, u32[]{:S(2)}, u32[]{:S(2)}) collective-permute-start(bf16[512,512]{1,0:T(8,128)(2,1)S(1)} %bitcast.20), channel_id=1, source_target_pairs={{0,2},{1,3},{2,0},{3,1},{4,6},{5,7},{6,4},{7,5},{8,10},{9,11},{10,... | collective-permute-start | bytes 1572872 | tf_op jit(solution)/shard_map/ppermute | solution.py:284
  69.3 14.0 %collective-permute-start.10 = (bf16[512,512]{1,0:T(8,128)(2,1)S(1)}, bf16[512,512]{1,0:T(8,128)(2,1)}, u32[]{:S(2)}, u32[]{:S(2)}) collective-permute-start(bf16[512,512]{1,0:T(8,128)(2,1)S(1)} %bitcast.21), channel_id=1, source_target_pairs={{0,1},{1,0},{2,3},{3,2},{4,5},{5,4},{6,7},{7,6},{8,9},{9,8},{10,11... | collective-permute-start | bytes 1572872 | tf_op jit(solution)/shard_map/ppermute | solution.py:287
  69.6 24.9 %all-to-all-start.2 = ((bf16[64,8,256]{2,1,0:T(8,128)(2,1)}), bf16[64,8,256]{2,1,0:T(8,128)(2,1)S(1)}, u32[]{:S(2)}, u32[]{:S(2)}) async-start(bf16[64,8,256]{2,1,0:T(8,128)(2,1)} %bitcast.6), calls=%async_computation.2 | async-start | bytes 524288 | tf_op jit(solution)/shard_map/all_to_all | solution.py:290
  82.4 2.6 %copy-start.6 = (bf16[3,2048,256]{2,1,0:T(8,128)(2,1)S(1)}, bf16[3,2048,256]{2,1,0:T(8,128)(2,1)}, u32[]{:S(2)}) copy-start(bf16[3,2048,256]{2,1,0:T(8,128)(2,1)} %refs_6_.5) | copy-start | bytes 9437188
  82.4 2.6 %collective-permute-start.11 = (bf16[512,512]{1,0:T(8,128)(2,1)}, bf16[512,512]{1,0:T(8,128)(2,1)S(1)}, u32[]{:S(2)}, u32[]{:S(2)}) collective-permute-start(bf16[512,512]{1,0:T(8,128)(2,1)} %collective-permute-done.9.refs_2_), channel_id=1, source_target_pairs={{0,1},{1,0},{2,3},{3,2},{4,5},{5,4},{6,7},{7,6},{8,9},{9,8},{10,11... | collective-permute-start | bytes 1572872 | tf_op jit(solution)/shard_map/ppermute | solution.py:287
  83.3 11.2 %copy-start = (bf16[256,2048]{1,0:T(8,128)(2,1)S(1)}, bf16[256,2048]{1,0:T(8,128)(2,1)}, u32[]{:S(2)}) copy-start(bf16[256,2048]{1,0:T(8,128)(2,1)} %refs_3_.11) | copy-start | bytes 3145732
  83.3 11.2 %copy-start.1 = (bf16[256,2048]{1,0:T(8,128)(2,1)S(1)}, bf16[256,2048]{1,0:T(8,128)(2,1)}, u32[]{:S(2)}) copy-start(bf16[256,2048]{1,0:T(8,128)(2,1)} %refs_4_.11) | copy-start | bytes 3145732
  83.3 11.2 %copy-start.3 = (bf16[512,256]{1,0:T(8,128)(2,1)S(1)}, bf16[512,256]{1,0:T(8,128)(2,1)}, u32[]{:S(2)}) copy-start(bf16[512,256]{1,0:T(8,128)(2,1)} %get-tuple-element.37.refs_1_) | copy-start | bytes 786436
  94.5 25.0 %copy-start.4 = (bf16[512,256]{1,0:T(8,128)(2,1)S(1)}, bf16[512,256]{1,0:T(8,128)(2,1)}, u32[]{:S(2)}) copy-start(bf16[512,256]{1,0:T(8,128)(2,1)} %get-tuple-element.41.refs_1_) | copy-start | bytes 786436
  95.2 4.3 %collective-permute-start.13 = (bf16[512,512]{1,0:T(8,128)(2,1)S(1)}, bf16[512,512]{1,0:T(8,128)(2,1)S(1)}, u32[]{:S(2)}, u32[]{:S(2)}) collective-permute-start(bf16[512,512]{1,0:T(8,128)(2,1)S(1)} %get-tuple-element.42), channel_id=1, source_target_pairs={{0,1},{1,0},{2,3},{3,2},{4,5},{5,4},{6,7},{7,6},{8,9},{9,8},{10,11... | collective-permute-start | bytes 1572872 | tf_op jit(solution)/shard_map/ppermute | solution.py:287
  100.0 19.5 %collective-permute-start.14 = (bf16[512,512]{1,0:T(8,128)(2,1)S(1)}, bf16[512,512]{1,0:T(8,128)(2,1)S(1)}, u32[]{:S(2)}, u32[]{:S(2)}) collective-permute-start(bf16[512,512]{1,0:T(8,128)(2,1)S(1)} %shard_map.71), channel_id=1, source_target_pairs={{0,2},{1,3},{2,0},{3,1},{4,6},{5,7},{6,4},{7,5},{8,10},{9,11},{10,... | collective-permute-start | bytes 1572872 | tf_op jit(solution)/shard_map/ppermute | solution.py:284
  120.2 4.9 %collective-permute-start.15 = (bf16[512,512]{1,0:T(8,128)(2,1)S(1)}, bf16[512,512]{1,0:T(8,128)(2,1)S(1)}, u32[]{:S(2)}, u32[]{:S(2)}) collective-permute-start(bf16[512,512]{1,0:T(8,128)(2,1)S(1)} %get-tuple-element.43), channel_id=1, source_target_pairs={{0,1},{1,0},{2,3},{3,2},{4,5},{5,4},{6,7},{7,6},{8,9},{9,8},{10,11... | collective-permute-start | bytes 1572872 | tf_op jit(solution)/shard_map/ppermute | solution.py:287
  123.6 2.3 %collective-permute-start.12 = (bf16[512,512]{1,0:T(8,128)(2,1)S(1)}, bf16[512,512]{1,0:T(8,128)(2,1)S(1)}, u32[]{:S(2)}, u32[]{:S(2)}) collective-permute-start(bf16[512,512]{1,0:T(8,128)(2,1)S(1)} %get-tuple-element.40), channel_id=1, source_target_pairs={{0,1},{1,0},{2,3},{3,2},{4,5},{5,4},{6,7},{7,6},{8,9},{9,8},{10,11... | collective-permute-start | bytes 1572872 | tf_op jit(solution)/shard_map/ppermute | solution.py:287
  123.7 2.9 %collective-permute-start.16 = (bf16[512,512]{1,0:T(8,128)(2,1)S(1)}, bf16[512,512]{1,0:T(8,128)(2,1)S(1)}, u32[]{:S(2)}, u32[]{:S(2)}) collective-permute-start(bf16[512,512]{1,0:T(8,128)(2,1)S(1)} %get-tuple-element.44), channel_id=1, source_target_pairs={{0,1},{1,0},{2,3},{3,2},{4,5},{5,4},{6,7},{7,6},{8,9},{9,8},{10,11... | collective-permute-start | bytes 1572872 | tf_op jit(solution)/shard_map/ppermute | solution.py:287
  125.5 13.2 %collective-permute-start.17 = (bf16[512,512]{1,0:T(8,128)(2,1)S(1)}, bf16[512,512]{1,0:T(8,128)(2,1)S(1)}, u32[]{:S(2)}, u32[]{:S(2)}) collective-permute-start(bf16[512,512]{1,0:T(8,128)(2,1)S(1)} %shard_map.73.refs_6_), channel_id=1, source_target_pairs={{0,2},{1,3},{2,0},{3,1},{4,6},{5,7},{6,4},{7,5},{8,10},{9,11},{10,... | collective-permute-start | bytes 1572872 | tf_op jit(solution)/shard_map/ppermute | solution.py:284
  126.3 12.5 %copy-start.2 = (bf16[2,512,512]{2,1,0:T(8,128)(2,1)S(1)}, bf16[2,512,512]{2,1,0:T(8,128)(2,1)}, u32[]{:S(2)}) copy-start(bf16[2,512,512]{2,1,0:T(8,128)(2,1)} %samples_ref.1) | copy-start | bytes 3145732

commit v5 on v4

--- a/solution.py
+++ b/solution.py
@@ -221,11 +221,9 @@
     )
 
 
-def out_core_kernel(h_ref, row_ref, col_ref, wr_ref, wc_ref, y3_ref, y1_ref):
-    h = h_ref[0]
-    width = y3_ref.shape[1]
-    y3_ref[...] = out_dot(row_ref, col_ref, wr_ref, wc_ref, block(h ^ 3, width)).astype(BF16)
-    y1_ref[...] = out_dot(row_ref, col_ref, wr_ref, wc_ref, block(h ^ 1, width)).astype(BF16)
+def out_core_kernel(flip, h_ref, row_ref, col_ref, wr_ref, wc_ref, y_ref):
+    where = block(h_ref[0] ^ flip, y_ref.shape[1])
+    y_ref[...] = out_dot(row_ref, col_ref, wr_ref, wc_ref, where).astype(BF16)
 
 
 def out_chip_kernel(h_ref, row_ref, col_ref, wr_ref, wc_ref, r2_ref, s2_ref):
@@ -331,7 +329,8 @@
 
     def out(row_attn, col_attn, after, after_chip):
         ops = (row_attn, col_attn, row_out, col_out)
-        y3, y1 = call(out_core_kernel, (h,), ops, (), (sds((tokens, width)),) * 2, 2 * piece, (), after)
+        (y3,) = call(functools.partial(out_core_kernel, 3), (h,), ops, (), (sds((tokens, width)),), piece, (), after)
+        (y1,) = call(functools.partial(out_core_kernel, 1), (h,), ops, (), (sds((tokens, width)),), piece, (), (y3,))
         (s2,) = call(out_chip_kernel, (h,), ops + (over_core(y3),), (), (sds((tokens, width)),), piece, (), after_chip)
 
         def own(after):

time: 141 us -> 140 us (level)
    pallas_call x9 -> x11, Pallas kernels: 14.1 us -> 14.4 us  [call(): pl.pallas_call(kernel, out_shape=tuple(outs), in_specs=[SM] * len(scalars...]
    unnamed x26 -> x28, local copies, waits for them, and re-layouts: 3.52 us -> 3.55 us
  transfers between devices with their start and end apart: 21 -> 21, of which waited for: 11 -> 10; matrix products, arithmetic and copies ran while one was open for 0% -> 0% of each run, Pallas kernels for 19% -> 20%
where the time goes in v5:
time: 140 us
  starting transfers between devices  58.1 us (42%)
  Pallas kernels  32.5 us (23%)
  waiting for transfers between devices  25.6 us (18%)
  blocking collectives  19.4 us (14%)
  local copies, waits for them, and re-layouts  3.55 us (3%)
    all_to_all x3, starting transfers between devices, exchange(): return lax.all_to_all(x, 'row', 0, 0, tiled=True)  35.9 us
    all_to_all x1, blocking collectives, exchange(): return lax.all_to_all(x, 'row', 0, 0, tiled=True)  19.4 us
    ppermute x12, starting transfers between devices, over_core(): return lax.ppermute(x, 'head', [(i, i ^ 1) for i in range(4)])  19 us
    pallas_call x11, Pallas kernels, call(): pl.pallas_call(kernel, out_shape=tuple(outs), in_specs=[SM] * len(scalars...  14.4 us
    pallas_call x2, Pallas kernels, row(): pl.pallas_call(functools.partial(row_kernel, r, len(more)), out_shape=out...  14.3 us
    ppermute x6, waiting for transfers between devices, over_chip(): return lax.ppermute(x, 'head', [(i, i ^ 2) for i in range(4)])  11.9 us
    all_to_all x3, waiting for transfers between devices, exchange(): return lax.all_to_all(x, 'row', 0, 0, tiled=True)  7.77 us
    ppermute x12, waiting for transfers between devices, over_core(): return lax.ppermute(x, 'head', [(i, i ^ 1) for i in range(4)])  5.96 us
  transfers between devices with their start and end apart: 21, of which 10 were waited for; matrix products, arithmetic and copies ran while one was open for 0% of the time, Pallas kernels for 20%

profile of v5, /device:TPU:1, one launch (start us, length us, event | category | flops | bytes accessed | tf_op | source)
XLA Modules:
  0.0 139.6 jit_solution(2684323898181319877)
XLA Ops:
  0.0 2.6 %shard_map.64 = (bf16[512,512]{1,0:T(8,128)(2,1)}, bf16[512,512]{1,0:T(8,128)(2,1)}, bf16[512,512]{1,0:T(8,128)(2,1)}, bf16[512,512]{1,0:T(8,128)(2,1)}) custom-call(bf16[2,512,512]{2,1,0:T(8,128)(2,1)} %samples_ref.1), custom_call_target="tpu_custom_call" | custom-call | flops 524288 | bytes 3145728 | tf_op jit(solution)/shard_map/pallas_call | solution.py:136
  2.6 2.1 %collective-permute-start = (bf16[512,512]{1,0:T(8,128)(2,1)}, bf16[512,512]{1,0:T(8,128)(2,1)S(1)}, u32[]{:S(2)}, u32[]{:S(2)}) collective-permute-start(bf16[512,512]{1,0:T(8,128)(2,1)} %get-tuple-element.23), channel_id=1, source_target_pairs={{0,2},{1,3},{2,0},{3,1},{4,6},{5,7},{6,4},{7,5},{8,10},{9,11},{10,... | collective-permute-start | bytes 1572872 | tf_op jit(solution)/shard_map/ppermute | solution.py:282
  4.7 14.0 %all-to-all-start = ((bf16[64,8,512]{2,1,0:T(8,128)(2,1)}), bf16[64,8,512]{2,1,0:T(8,128)(2,1)S(1)}, u32[]{:S(2)}, u32[]{:S(2)}) async-start(bf16[64,8,512]{2,1,0:T(8,128)(2,1)} %bitcast.30), calls=%async_computation | async-start | bytes 1048576 | tf_op jit(solution)/shard_map/all_to_all | solution.py:288
  18.7 1.3 collective-permute-start.1
  20.0 0.0 collective-permute-done.refs_1_
  20.0 0.1 collective-permute-start.2
  20.1 0.0 collective-permute-start.3
  20.1 1.6 %collective-permute-done.1.refs_2_ = bf16[512,512]{1,0:T(8,128)(2,1)S(1)} collective-permute-done((bf16[512,512]{1,0:T(8,128)(2,1)}, bf16[512,512]{1,0:T(8,128)(2,1)S(1)}, u32[]{:S(2)}, u32[]{:S(2)}) %collective-permute-start.1) | collective-permute-done | bytes 524320 | tf_op jit(solution)/shard_map/ppermute | solution.py:285
  21.8 0.5 collective-permute-done.2.refs_3_
  22.3 0.3 copy-done.12
  22.6 0.5 copy-done.13
  23.1 7.1 %shard_map.65.refs_4_ = bf16[512,256]{1,0:T(8,128)(2,1)} custom-call(s32[1]{0:T(128)} %bitcast.h_ref.refs_0_, bf16[2,512,512]{2,1,0:T(8,128)(2,1)} %samples_ref.1, bf16[512,512]{1,0:T(8,128)(2,1)} %copy-done.10, bf16[512,512]{1,0:T(8,128)(2,1)} %copy-done.12, bf16[512,512]{1,0:T(8,128)(2,1)} %copy-done.13, f32[1,2048]{1,0:T(1,128)} %bitcast.26, ...), custom_call_target="tpu_custom_call" | custom-call | flops 1879048192 | bytes 2621440 | tf_op jit(solution)/shard_map/pallas_call | solution.py:310
  30.2 3.9 %all-to-all-done = bf16[64,8,512]{2,1,0:T(8,128)(2,1)S(1)} async-done(((bf16[64,8,512]{2,1,0:T(8,128)(2,1)}), bf16[64,8,512]{2,1,0:T(8,128)(2,1)S(1)}, u32[]{:S(2)}, u32[]{:S(2)}) %all-to-all-start) | async-done | bytes 524320 | tf_op jit(solution)/shard_map/all_to_all | solution.py:288
  34.1 0.0 collective-permute-start.6
  34.1 9.2 %all-to-all-start.1 = ((bf16[64,8,512]{2,1,0:T(8,128)(2,1)}), bf16[64,8,512]{2,1,0:T(8,128)(2,1)S(1)}, u32[]{:S(2)}, u32[]{:S(2)}) async-start(bf16[64,8,512]{2,1,0:T(8,128)(2,1)} %bitcast.4), calls=%async_computation.1 | async-start | bytes 1048576 | tf_op jit(solution)/shard_map/all_to_all | solution.py:288
  43.3 0.0 copy-start.7
  43.3 2.3 %collective-permute-start.4 = (bf16[512,512]{1,0:T(8,128)(2,1)S(1)}, bf16[512,512]{1,0:T(8,128)(2,1)S(1)}, u32[]{:S(2)}, u32[]{:S(2)}) collective-permute-start(bf16[512,512]{1,0:T(8,128)(2,1)S(1)} %copy-done.8), channel_id=1, source_target_pairs={{0,1},{1,0},{2,3},{3,2},{4,5},{5,4},{6,7},{7,6},{8,9},{9,8},{10,11... | collective-permute-start | bytes 1572872 | tf_op jit(solution)/shard_map/ppermute | solution.py:285
  45.6 0.0 collective-permute-done.3.refs_1_
  45.6 0.1 collective-permute-start.5
  45.7 0.4 collective-permute-start.7
  46.1 0.2 collective-permute-done.6.refs_2_
  46.3 6.9 %collective-permute-start.8 = (bf16[512,512]{1,0:T(8,128)(2,1)S(1)}, bf16[512,512]{1,0:T(8,128)(2,1)S(1)}, u32[]{:S(2)}, u32[]{:S(2)}) collective-permute-start(bf16[512,512]{1,0:T(8,128)(2,1)S(1)} %collective-permute-done.6.refs_2_), channel_id=1, source_target_pairs={{0,1},{1,0},{2,3},{3,2},{4,5},{5,4},{6,7},{7,6},{8,9},{9,8},{10,11... | collective-permute-start | bytes 1572872 | tf_op jit(solution)/shard_map/ppermute | solution.py:285
  53.2 0.0 collective-permute-done.4.refs_2_
  53.2 0.8 copy-done.11
  54.0 7.3 %shard_map.66 = (bf16[512,256]{1,0:T(8,128)(2,1)}, bf16[512,256]{1,0:T(8,128)(2,1)}) custom-call(s32[1]{0:T(128)} %bitcast.h_ref.refs_0_, bf16[2,512,512]{2,1,0:T(8,128)(2,1)} %samples_ref.1, bf16[512,512]{1,0:T(8,128)(2,1)} %copy-done.9, bf16[512,512]{1,0:T(8,128)(2,1)} %copy-done.11, bf16[512,512]{1,0:T(8,128)(2,1)} %collective-permute-done.5.refs_3_, ...), custom_call_target="tpu_custom_call" | custom-call | flops 1879048192 | bytes 2621440 | tf_op jit(solution)/shard_map/pallas_call | solution.py:310
  61.3 0.0 collective-permute-done.7.refs_3_
  61.3 0.0 copy-start.5
  61.3 1.9 %copy-done.5 = bf16[3,2048,256]{2,1,0:T(8,128)(2,1)S(1)} copy-done((bf16[3,2048,256]{2,1,0:T(8,128)(2,1)S(1)}, bf16[3,2048,256]{2,1,0:T(8,128)(2,1)}, u32[]{:S(2)}) %copy-start.5) | copy-done | bytes 3145752
  63.2 5.2 %shard_map.67 = bf16[512,256]{1,0:T(8,128)(2,1)} custom-call(s32[1]{0:T(128)} %bitcast.h_ref.refs_0_, bf16[512,512]{1,0:T(8,128)(2,1)S(1)} %bitcast.21, bf16[512,512]{1,0:T(8,128)(2,1)S(1)} %collective-permute-done.6.refs_2_, bf16[512,512]{1,0:T(8,128)(2,1)S(1)} %collective-permute-done.7.refs_3_, bf16[512,512]{1,0:T(8,128)(2,1)S(1)} %collective-permute-done.8.refs_4_, ...), custom_call_target="tpu_custom_call" | custom-call | flops 1879048192 | bytes 5513216 | tf_op jit(solution)/shard_map/pallas_call | solution.py:38
  68.4 0.9 collective-permute-start.9
  69.3 0.3 collective-permute-start.10
  69.6 12.8 %all-to-all-start.2 = ((bf16[64,8,256]{2,1,0:T(8,128)(2,1)}), bf16[64,8,256]{2,1,0:T(8,128)(2,1)S(1)}, u32[]{:S(2)}, u32[]{:S(2)}) async-start(bf16[64,8,256]{2,1,0:T(8,128)(2,1)} %bitcast.6), calls=%async_computation.2 | async-start | bytes 524288 | tf_op jit(solution)/shard_map/all_to_all | solution.py:288
  82.4 0.0 copy-start.6
  82.4 0.0 collective-permute-done.9.refs_2_
  82.4 0.8 collective-permute-start.11
  83.2 0.1 shard_map.68.refs_7_
  83.3 0.0 copy-start
  83.3 0.0 copy-start.1
  83.3 1.6 %collective-permute-done.11.refs_4_ = bf16[512,512]{1,0:T(8,128)(2,1)S(1)} collective-permute-done((bf16[512,512]{1,0:T(8,128)(2,1)}, bf16[512,512]{1,0:T(8,128)(2,1)S(1)}, u32[]{:S(2)}, u32[]{:S(2)}) %collective-permute-start.11) | collective-permute-done | bytes 524320 | tf_op jit(solution)/shard_map/ppermute | solution.py:285
  85.0 5.7 %shard_map.69.refs_5_ = bf16[512,256]{1,0:T(8,128)(2,1)S(1)} custom-call(s32[1]{0:T(128)} %bitcast.h_ref.refs_0_, bf16[512,512]{1,0:T(8,128)(2,1)S(1)} %bitcast.25, bf16[512,512]{1,0:T(8,128)(2,1)} %collective-permute-done.9.refs_2_, bf16[512,512]{1,0:T(8,128)(2,1)} %collective-permute-done.10.refs_3_, bf16[512,512]{1,0:T(8,128)(2,1)S(1)} %collective-permute-done.11.refs_4_, ...), custom_call_target="tpu_custom_call" | custom-call | flops 1879048192 | bytes 5775360 | tf_op jit(solution)/shard_map/pallas_call | solution.py:38
  90.6 3.8 %all-to-all-done.2 = bf16[64,8,256]{2,1,0:T(8,128)(2,1)S(1)} async-done(((bf16[64,8,256]{2,1,0:T(8,128)(2,1)}), bf16[64,8,256]{2,1,0:T(8,128)(2,1)S(1)}, u32[]{:S(2)}, u32[]{:S(2)}) %all-to-all-start.2) | async-done | bytes 262176 | tf_op jit(solution)/shard_map/all_to_all | solution.py:288
  94.5 0.4 shard_map.70.refs_5_
  94.9 2.7 %collective-permute-start.13 = (bf16[512,512]{1,0:T(8,128)(2,1)S(1)}, bf16[512,512]{1,0:T(8,128)(2,1)S(1)}, u32[]{:S(2)}, u32[]{:S(2)}) collective-permute-start(bf16[512,512]{1,0:T(8,128)(2,1)S(1)} %shard_map.70.refs_5_), channel_id=1, source_target_pairs={{0,1},{1,0},{2,3},{3,2},{4,5},{5,4},{6,7},{7,6},{8,9},{9,8},{10,11... | collective-permute-start | bytes 1572872 | tf_op jit(solution)/shard_map/ppermute | solution.py:285
  97.7 1.5 %collective-permute-done.13.refs_5_ = bf16[512,512]{1,0:T(8,128)(2,1)S(1)} collective-permute-done((bf16[512,512]{1,0:T(8,128)(2,1)S(1)}, bf16[512,512]{1,0:T(8,128)(2,1)S(1)}, u32[]{:S(2)}, u32[]{:S(2)}) %collective-permute-start.13) | collective-permute-done | bytes 524320 | tf_op jit(solution)/shard_map/ppermute | solution.py:285
  99.2 0.4 shard_map.72
  99.7 0.1 collective-permute-start.14
  99.8 19.4 %all_to_all.46 = bf16[64,8,256]{2,1,0:T(8,128)(2,1)S(1)} all-to-all(bf16[64,8,256]{2,1,0:T(8,128)(2,1)S(1)} %bitcast.18), channel_id=1, replica_groups=mesh['row'=64,'head'=4] {'row'}, dimensions={0} | all-to-all | bytes 524288 | tf_op jit(solution)/shard_map/all_to_all | solution.py:288
  119.2 0.0 collective-permute-done.14.refs_5_.rx0_ref
  119.2 0.4 shard_map.73.refs_5_
  119.6 3.3 %collective-permute-start.15 = (bf16[512,512]{1,0:T(8,128)(2,1)S(1)}, bf16[512,512]{1,0:T(8,128)(2,1)S(1)}, u32[]{:S(2)}, u32[]{:S(2)}) collective-permute-start(bf16[512,512]{1,0:T(8,128)(2,1)S(1)} %shard_map.73.refs_5_), channel_id=1, source_target_pairs={{0,1},{1,0},{2,3},{3,2},{4,5},{5,4},{6,7},{7,6},{8,9},{9,8},{10,11... | collective-permute-start | bytes 1572872 | tf_op jit(solution)/shard_map/ppermute | solution.py:285
  123.0 0.4 shard_map.71
  123.4 0.1 collective-permute-start.12
  123.5 0.4 shard_map.76
  124.0 0.6 collective-permute-start.16
  124.6 0.0 collective-permute-done.15.refs_5_
  124.6 0.4 shard_map.74.refs_6_
  125.0 0.1 collective-permute-start.17
  125.1 0.3 collective-permute-done.12.refs_5_
  125.4 0.4 shard_map.75.refs_6_.own0_ref
  125.9 0.0 copy-start.2
  125.9 0.3 collective-permute-done.16.refs_5_
  126.2 0.4 shard_map.77.own1_ref
  126.6 11.6 %collective-permute-done.17.rx1_ref = bf16[512,512]{1,0:T(8,128)(2,1)S(1)} collective-permute-done((bf16[512,512]{1,0:T(8,128)(2,1)S(1)}, bf16[512,512]{1,0:T(8,128)(2,1)S(1)}, u32[]{:S(2)}, u32[]{:S(2)}) %collective-permute-start.17) | collective-permute-done | bytes 524320 | tf_op jit(solution)/shard_map/ppermute | solution.py:282
  138.3 1.2 shard_map.78
  (22 shorter events, 0.0 us)
Async XLA Ops:
  2.6 17.5 %collective-permute-start = (bf16[512,512]{1,0:T(8,128)(2,1)}, bf16[512,512]{1,0:T(8,128)(2,1)S(1)}, u32[]{:S(2)}, u32[]{:S(2)}) collective-permute-start(bf16[512,512]{1,0:T(8,128)(2,1)} %get-tuple-element.23), channel_id=1, source_target_pairs={{0,2},{1,3},{2,0},{3,1},{4,6},{5,7},{6,4},{7,5},{8,10},{9,11},{10,... | collective-permute-start | bytes 1572872 | tf_op jit(solution)/shard_map/ppermute | solution.py:282
  4.7 29.4 %all-to-all-start = ((bf16[64,8,512]{2,1,0:T(8,128)(2,1)}), bf16[64,8,512]{2,1,0:T(8,128)(2,1)S(1)}, u32[]{:S(2)}, u32[]{:S(2)}) async-start(bf16[64,8,512]{2,1,0:T(8,128)(2,1)} %bitcast.30), calls=%async_computation | async-start | bytes 1048576 | tf_op jit(solution)/shard_map/all_to_all | solution.py:288
  18.7 3.1 %collective-permute-start.1 = (bf16[512,512]{1,0:T(8,128)(2,1)}, bf16[512,512]{1,0:T(8,128)(2,1)S(1)}, u32[]{:S(2)}, u32[]{:S(2)}) collective-permute-start(bf16[512,512]{1,0:T(8,128)(2,1)} %get-tuple-element.23), channel_id=1, source_target_pairs={{0,1},{1,0},{2,3},{3,2},{4,5},{5,4},{6,7},{7,6},{8,9},{9,8},{10,11... | collective-permute-start | bytes 1572872 | tf_op jit(solution)/shard_map/ppermute | solution.py:285
  20.0 2.3 %copy-start.10 = (bf16[512,512]{1,0:T(8,128)(2,1)}, bf16[512,512]{1,0:T(8,128)(2,1)S(1)}, u32[]{:S(2)}) copy-start(bf16[512,512]{1,0:T(8,128)(2,1)S(1)} %collective-permute-done.refs_1_) | copy-start | bytes 1572868
  20.0 2.3 %collective-permute-start.2 = (bf16[512,512]{1,0:T(8,128)(2,1)S(1)}, bf16[512,512]{1,0:T(8,128)(2,1)S(1)}, u32[]{:S(2)}, u32[]{:S(2)}) collective-permute-start(bf16[512,512]{1,0:T(8,128)(2,1)S(1)} %collective-permute-done.refs_1_), channel_id=1, source_target_pairs={{0,1},{1,0},{2,3},{3,2},{4,5},{5,4},{6,7},{7,6},{8,9},{9,8},{10,11... | collective-permute-start | bytes 1572872 | tf_op jit(solution)/shard_map/ppermute | solution.py:285
  20.1 25.5 %collective-permute-start.3 = (bf16[512,512]{1,0:T(8,128)(2,1)}, bf16[512,512]{1,0:T(8,128)(2,1)S(1)}, u32[]{:S(2)}, u32[]{:S(2)}) collective-permute-start(bf16[512,512]{1,0:T(8,128)(2,1)} %get-tuple-element.28), channel_id=1, source_target_pairs={{0,2},{1,3},{2,0},{3,1},{4,6},{5,7},{6,4},{7,5},{8,10},{9,11},{10,... | collective-permute-start | bytes 1572872 | tf_op jit(solution)/shard_map/ppermute | solution.py:282
  21.8 0.8 copy-start.12
  22.3 0.8 copy-start.13
  23.1 20.2 %copy-start.8 = (bf16[512,512]{1,0:T(8,128)(2,1)S(1)}, bf16[512,512]{1,0:T(8,128)(2,1)}, u32[]{:S(2)}) copy-start(bf16[512,512]{1,0:T(8,128)(2,1)} %get-tuple-element.28) | copy-start | bytes 1572868
  34.1 12.2 %collective-permute-start.6 = (bf16[512,512]{1,0:T(8,128)(2,1)S(1)}, bf16[512,512]{1,0:T(8,128)(2,1)S(1)}, u32[]{:S(2)}, u32[]{:S(2)}) collective-permute-start(bf16[512,512]{1,0:T(8,128)(2,1)S(1)} %bitcast.19), channel_id=1, source_target_pairs={{0,2},{1,3},{2,0},{3,1},{4,6},{5,7},{6,4},{7,5},{8,10},{9,11},{10,... | collective-permute-start | bytes 1572872 | tf_op jit(solution)/shard_map/ppermute | solution.py:282
  34.1 34.3 %all-to-all-start.1 = ((bf16[64,8,512]{2,1,0:T(8,128)(2,1)}), bf16[64,8,512]{2,1,0:T(8,128)(2,1)S(1)}, u32[]{:S(2)}, u32[]{:S(2)}) async-start(bf16[64,8,512]{2,1,0:T(8,128)(2,1)} %bitcast.4), calls=%async_computation.1 | async-start | bytes 1048576 | tf_op jit(solution)/shard_map/all_to_all | solution.py:288
  43.3 18.0 %copy-start.7 = (f32[2048]{0:T(1024)S(1)}, f32[2048]{0:T(1024)}, u32[]{:S(2)}) copy-start(f32[2048]{0:T(1024)} %param.7) | copy-start | bytes 24580
  43.3 9.9 %collective-permute-start.4 = (bf16[512,512]{1,0:T(8,128)(2,1)S(1)}, bf16[512,512]{1,0:T(8,128)(2,1)S(1)}, u32[]{:S(2)}, u32[]{:S(2)}) collective-permute-start(bf16[512,512]{1,0:T(8,128)(2,1)S(1)} %copy-done.8), channel_id=1, source_target_pairs={{0,1},{1,0},{2,3},{3,2},{4,5},{5,4},{6,7},{7,6},{8,9},{9,8},{10,11... | collective-permute-start | bytes 1572872 | tf_op jit(solution)/shard_map/ppermute | solution.py:285
  45.6 8.4 %copy-start.9 = (bf16[512,512]{1,0:T(8,128)(2,1)}, bf16[512,512]{1,0:T(8,128)(2,1)S(1)}, u32[]{:S(2)}) copy-start(bf16[512,512]{1,0:T(8,128)(2,1)S(1)} %collective-permute-done.3.refs_1_) | copy-start | bytes 1572868
  45.6 8.4 %collective-permute-start.5 = (bf16[512,512]{1,0:T(8,128)(2,1)S(1)}, bf16[512,512]{1,0:T(8,128)(2,1)}, u32[]{:S(2)}, u32[]{:S(2)}) collective-permute-start(bf16[512,512]{1,0:T(8,128)(2,1)S(1)} %collective-permute-done.3.refs_1_), channel_id=1, source_target_pairs={{0,1},{1,0},{2,3},{3,2},{4,5},{5,4},{6,7},{7,6},{8,9},{9,8},{10,11... | collective-permute-start | bytes 1572872 | tf_op jit(solution)/shard_map/ppermute | solution.py:285
  45.7 15.6 %collective-permute-start.7 = (bf16[512,512]{1,0:T(8,128)(2,1)S(1)}, bf16[512,512]{1,0:T(8,128)(2,1)S(1)}, u32[]{:S(2)}, u32[]{:S(2)}) collective-permute-start(bf16[512,512]{1,0:T(8,128)(2,1)S(1)} %bitcast.20), channel_id=1, source_target_pairs={{0,1},{1,0},{2,3},{3,2},{4,5},{5,4},{6,7},{7,6},{8,9},{9,8},{10,11... | collective-permute-start | bytes 1572872 | tf_op jit(solution)/shard_map/ppermute | solution.py:285
  46.3 15.0 %collective-permute-start.8 = (bf16[512,512]{1,0:T(8,128)(2,1)S(1)}, bf16[512,512]{1,0:T(8,128)(2,1)S(1)}, u32[]{:S(2)}, u32[]{:S(2)}) collective-permute-start(bf16[512,512]{1,0:T(8,128)(2,1)S(1)} %collective-permute-done.6.refs_2_), channel_id=1, source_target_pairs={{0,1},{1,0},{2,3},{3,2},{4,5},{5,4},{6,7},{7,6},{8,9},{9,8},{10,11... | collective-permute-start | bytes 1572872 | tf_op jit(solution)/shard_map/ppermute | solution.py:285
  53.2 0.8 copy-start.11
  61.3 1.9 %copy-start.5 = (bf16[3,2048,256]{2,1,0:T(8,128)(2,1)S(1)}, bf16[3,2048,256]{2,1,0:T(8,128)(2,1)}, u32[]{:S(2)}) copy-start(bf16[3,2048,256]{2,1,0:T(8,128)(2,1)} %refs_6_.5) | copy-start | bytes 9437188
  68.4 14.0 %collective-permute-start.9 = (bf16[512,512]{1,0:T(8,128)(2,1)S(1)}, bf16[512,512]{1,0:T(8,128)(2,1)}, u32[]{:S(2)}, u32[]{:S(2)}) collective-permute-start(bf16[512,512]{1,0:T(8,128)(2,1)S(1)} %bitcast.22), channel_id=1, source_target_pairs={{0,2},{1,3},{2,0},{3,1},{4,6},{5,7},{6,4},{7,5},{8,10},{9,11},{10,... | collective-permute-start | bytes 1572872 | tf_op jit(solution)/shard_map/ppermute | solution.py:282
  69.3 14.0 %collective-permute-start.10 = (bf16[512,512]{1,0:T(8,128)(2,1)S(1)}, bf16[512,512]{1,0:T(8,128)(2,1)}, u32[]{:S(2)}, u32[]{:S(2)}) collective-permute-start(bf16[512,512]{1,0:T(8,128)(2,1)S(1)} %bitcast.23), channel_id=1, source_target_pairs={{0,1},{1,0},{2,3},{3,2},{4,5},{5,4},{6,7},{7,6},{8,9},{9,8},{10,11... | collective-permute-start | bytes 1572872 | tf_op jit(solution)/shard_map/ppermute | solution.py:285
  69.6 24.9 %all-to-all-start.2 = ((bf16[64,8,256]{2,1,0:T(8,128)(2,1)}), bf16[64,8,256]{2,1,0:T(8,128)(2,1)S(1)}, u32[]{:S(2)}, u32[]{:S(2)}) async-start(bf16[64,8,256]{2,1,0:T(8,128)(2,1)} %bitcast.6), calls=%async_computation.2 | async-start | bytes 524288 | tf_op jit(solution)/shard_map/all_to_all | solution.py:288
  82.4 2.6 %copy-start.6 = (bf16[3,2048,256]{2,1,0:T(8,128)(2,1)S(1)}, bf16[3,2048,256]{2,1,0:T(8,128)(2,1)}, u32[]{:S(2)}) copy-start(bf16[3,2048,256]{2,1,0:T(8,128)(2,1)} %refs_6_.5) | copy-start | bytes 9437188
  82.4 2.6 %collective-permute-start.11 = (bf16[512,512]{1,0:T(8,128)(2,1)}, bf16[512,512]{1,0:T(8,128)(2,1)S(1)}, u32[]{:S(2)}, u32[]{:S(2)}) collective-permute-start(bf16[512,512]{1,0:T(8,128)(2,1)} %collective-permute-done.9.refs_2_), channel_id=1, source_target_pairs={{0,1},{1,0},{2,3},{3,2},{4,5},{5,4},{6,7},{7,6},{8,9},{9,8},{10,11... | collective-permute-start | bytes 1572872 | tf_op jit(solution)/shard_map/ppermute | solution.py:285
  83.3 11.2 %copy-start = (bf16[256,2048]{1,0:T(8,128)(2,1)S(1)}, bf16[256,2048]{1,0:T(8,128)(2,1)}, u32[]{:S(2)}) copy-start(bf16[256,2048]{1,0:T(8,128)(2,1)} %refs_3_.15) | copy-start | bytes 3145732
  83.3 11.2 %copy-start.1 = (bf16[256,2048]{1,0:T(8,128)(2,1)S(1)}, bf16[256,2048]{1,0:T(8,128)(2,1)}, u32[]{:S(2)}) copy-start(bf16[256,2048]{1,0:T(8,128)(2,1)} %refs_4_.15) | copy-start | bytes 3145732
  83.3 11.2 %copy-start.3 = (bf16[512,256]{1,0:T(8,128)(2,1)S(1)}, bf16[512,256]{1,0:T(8,128)(2,1)}, u32[]{:S(2)}) copy-start(bf16[512,256]{1,0:T(8,128)(2,1)} %get-tuple-element.33.refs_1_) | copy-start | bytes 786436
  94.5 24.7 %copy-start.4 = (bf16[512,256]{1,0:T(8,128)(2,1)S(1)}, bf16[512,256]{1,0:T(8,128)(2,1)}, u32[]{:S(2)}) copy-start(bf16[512,256]{1,0:T(8,128)(2,1)} %get-tuple-element.36.refs_1_) | copy-start | bytes 786436
  94.9 4.3 %collective-permute-start.13 = (bf16[512,512]{1,0:T(8,128)(2,1)S(1)}, bf16[512,512]{1,0:T(8,128)(2,1)S(1)}, u32[]{:S(2)}, u32[]{:S(2)}) collective-permute-start(bf16[512,512]{1,0:T(8,128)(2,1)S(1)} %shard_map.70.refs_5_), channel_id=1, source_target_pairs={{0,1},{1,0},{2,3},{3,2},{4,5},{5,4},{6,7},{7,6},{8,9},{9,8},{10,11... | collective-permute-start | bytes 1572872 | tf_op jit(solution)/shard_map/ppermute | solution.py:285
  99.7 19.5 %collective-permute-start.14 = (bf16[512,512]{1,0:T(8,128)(2,1)S(1)}, bf16[512,512]{1,0:T(8,128)(2,1)S(1)}, u32[]{:S(2)}, u32[]{:S(2)}) collective-permute-start(bf16[512,512]{1,0:T(8,128)(2,1)S(1)} %shard_map.72), channel_id=1, source_target_pairs={{0,2},{1,3},{2,0},{3,1},{4,6},{5,7},{6,4},{7,5},{8,10},{9,11},{10,... | collective-permute-start | bytes 1572872 | tf_op jit(solution)/shard_map/ppermute | solution.py:282
  119.6 4.9 %collective-permute-start.15 = (bf16[512,512]{1,0:T(8,128)(2,1)S(1)}, bf16[512,512]{1,0:T(8,128)(2,1)S(1)}, u32[]{:S(2)}, u32[]{:S(2)}) collective-permute-start(bf16[512,512]{1,0:T(8,128)(2,1)S(1)} %shard_map.73.refs_5_), channel_id=1, source_target_pairs={{0,1},{1,0},{2,3},{3,2},{4,5},{5,4},{6,7},{7,6},{8,9},{9,8},{10,11... | collective-permute-start | bytes 1572872 | tf_op jit(solution)/shard_map/ppermute | solution.py:285
  123.4 2.0 %collective-permute-start.12 = (bf16[512,512]{1,0:T(8,128)(2,1)S(1)}, bf16[512,512]{1,0:T(8,128)(2,1)S(1)}, u32[]{:S(2)}, u32[]{:S(2)}) collective-permute-start(bf16[512,512]{1,0:T(8,128)(2,1)S(1)} %shard_map.71), channel_id=1, source_target_pairs={{0,1},{1,0},{2,3},{3,2},{4,5},{5,4},{6,7},{7,6},{8,9},{9,8},{10,11... | collective-permute-start | bytes 1572872 | tf_op jit(solution)/shard_map/ppermute | solution.py:285
  124.0 2.2 %collective-permute-start.16 = (bf16[512,512]{1,0:T(8,128)(2,1)S(1)}, bf16[512,512]{1,0:T(8,128)(2,1)S(1)}, u32[]{:S(2)}, u32[]{:S(2)}) collective-permute-start(bf16[512,512]{1,0:T(8,128)(2,1)S(1)} %shard_map.76), channel_id=1, source_target_pairs={{0,1},{1,0},{2,3},{3,2},{4,5},{5,4},{6,7},{7,6},{8,9},{9,8},{10,11... | collective-permute-start | bytes 1572872 | tf_op jit(solution)/shard_map/ppermute | solution.py:285
  125.0 13.3 %collective-permute-start.17 = (bf16[512,512]{1,0:T(8,128)(2,1)S(1)}, bf16[512,512]{1,0:T(8,128)(2,1)S(1)}, u32[]{:S(2)}, u32[]{:S(2)}) collective-permute-start(bf16[512,512]{1,0:T(8,128)(2,1)S(1)} %shard_map.74.refs_6_), channel_id=1, source_target_pairs={{0,2},{1,3},{2,0},{3,1},{4,6},{5,7},{6,4},{7,5},{8,10},{9,11},{10,... | collective-permute-start | bytes 1572872 | tf_op jit(solution)/shard_map/ppermute | solution.py:282
  125.9 12.4 %copy-start.2 = (bf16[2,512,512]{2,1,0:T(8,128)(2,1)S(1)}, bf16[2,512,512]{2,1,0:T(8,128)(2,1)}, u32[]{:S(2)}) copy-start(bf16[2,512,512]{2,1,0:T(8,128)(2,1)} %samples_ref.1) | copy-start | bytes 3145732
